TPU v7x, 32 devices: a whole 2x2x4 slice. The times are simulated.
32 devices in a mesh: groups: 2 (over y), replica: 4 (over x, core), tensor: 4 (over z).
Axes of the slice: x: 2, y: 2, z: 4, core: 2. Of those that a mesh axis runs over, the one named last changes fastest.
Arguments:
- attn_out: bfloat16 [6144, 8192], P(('groups', 'replica'), 'tensor'), parts along dimension 0, may hold values from -6 to 6
- out_weight: bfloat16 [8192, 8192], P('tensor'), may hold values from -0.09375 to 0.09375
- store_factors: bfloat16 [64, 2, 64, 8192], P(('groups', 'replica'), None, None, 'tensor'), parts along dimension 0, may hold values from -1 to 1
- resident_factors: bfloat16 [64, 2, 64, 8192], P(('groups', 'replica'), None, None, 'tensor'), parts along dimension 0, may hold values from -1 to 1
- resident_ids: int32 [8, 8], P(('groups', 'replica')), parts along dimension 0, may hold values from 0 to 31, as said below
- evict_slots: int32 [8, 4], P(('groups', 'replica')), parts along dimension 0, may hold values from 0 to 7, as said below
- incoming: int32 [8, 4], P('groups'), parts along dimension 0, may hold values from 0 to 31, as said below
- store_place: int32 [64], P('groups'), parts along dimension 0, may hold values from 0 to 31, as said below
- req_adapter: int32 [6144], P(('groups', 'replica')), parts along dimension 0, may hold values from 0 to 31, as said below
Outputs:
- projected: bfloat16 [6144, 8192], P(('groups', 'replica'), 'tensor'), parts along dimension 0
There are 2 independent parts, one for each index of `groups`. A program takes and returns all parts, laid end to end along the dimension named above; an argument that names none is the same for every part. Nothing has to cross between parts.
Inputs may be any that keep to these rules, and one draw needn't show every extreme that they name: `store_place`: a permutation; the owner of adapter a is replica store_place[a] // 8. `resident_ids`: each row holds distinct adapters, none of them among that replica's incoming ones. `evict_slots`: each row holds distinct slots. `incoming`: each row holds distinct adapters: exactly 2 of them from each of 2 distinct owners. `req_adapter`: each request's adapter is held by exactly one of its replica's slots after refilling; every slot serves some request.
All inputs are finite; a program needn't handle non-finite values.
Results may differ from a plain program's by a relative error of at most 0.013.
Values may be sent and summed in bfloat16 or wider, within the bound.
No kernel may reach another device: no remote copies, remote signals or barrier semaphores. Data moves between devices by JAX's collectives and lax.ppermute only.
A program may use at most 192 MiB of HBM per device.

v0:
```python
import jax
import jax.numpy as jnp
from jax import lax
from jax.sharding import PartitionSpec as P


def local(
    attn_out,
    out_weight,
    store_factors,
    resident_factors,
    resident_ids,
    evict_slots,
    incoming,
    store_place,
    req_adapter,
):
    own_index = lax.axis_index("replica")
    slot_count = resident_factors.shape[0]
    rank_width = resident_factors.shape[2]
    adapter_count = store_place.shape[0]
    matches = incoming[:, :, None] == jnp.arange(adapter_count, dtype=jnp.int32)[None, None, :]
    in_place = jnp.sum(jnp.where(matches, store_place[None, None, :], 0), axis=2)
    my_place = lax.dynamic_index_in_dim(in_place, own_index, 0, keepdims=False)
    everything = lax.all_gather(store_factors, "replica", axis=0, tiled=True)
    fetched = jnp.take(everything, my_place, axis=0)
    my_evict = evict_slots[0]
    arriving_ids = lax.dynamic_index_in_dim(incoming, own_index, 0, keepdims=False)
    buffers = resident_factors.at[my_evict].set(fetched)
    slot_ids = resident_ids[0].at[my_evict].set(arriving_ids)
    uses_slot = req_adapter[:, None] == slot_ids[None, :]
    shrink_rows = buffers[:, 0].reshape(slot_count * rank_width, -1)
    expand_rows = buffers[:, 1].reshape(slot_count * rank_width, -1)
    shrunk = lax.dot_general(
        attn_out, shrink_rows, (((1,), (1,)), ((), ())), preferred_element_type=jnp.float32
    )
    summed = lax.psum(shrunk.astype(jnp.bfloat16), "tensor").astype(jnp.float32)
    spread_uses = jnp.repeat(uses_slot, rank_width, axis=1)
    masked = jnp.where(spread_uses, summed, jnp.zeros_like(summed)).astype(jnp.bfloat16)
    head_terms = jnp.dot(attn_out, out_weight, preferred_element_type=jnp.float32)
    head_total = lax.psum_scatter(
        head_terms.astype(jnp.bfloat16), "tensor", scatter_dimension=1, tiled=True
    ).astype(jnp.float32)
    adapted = jnp.dot(masked, expand_rows, preferred_element_type=jnp.float32)
    return (head_total + adapted).astype(jnp.bfloat16)


def solution(mesh):
    return jax.shard_map(
        local,
        mesh=mesh,
        in_specs=(
            P(("groups", "replica"), "tensor"),
            P("tensor", None),
            P(("groups", "replica"), None, None, "tensor"),
            P(("groups", "replica"), None, None, "tensor"),
            P(("groups", "replica"), None),
            P(("groups", "replica"), None),
            P("groups", None),
            P("groups"),
            P(("groups", "replica")),
        ),
        out_specs=P(("groups", "replica"), "tensor"),
        check_vma=False,
    )
```

profile of v0, /device:TPU:0, one launch (start us, length us, event | category | flops | bytes accessed | tf_op | source)
XLA Modules:
  0.0 414.0 jit_solution(11949719654962215558)
XLA Ops:
  6.5 0.0 copy-start
  6.5 0.0 all-gather.2.cloned.1.call-start
  6.5 4.9 %copy.15 = bf16[8,2,64,2048]{3,2,1,0:T(8,128)(2,1)} copy(bf16[8,2,64,2048]{3,2,1,0:T(8,128)(2,1)} %param.12) | data formatting | bytes 8388608
  11.4 0.0 copy-start.4
  11.4 0.0 copy-start.5
  11.4 0.0 copy-start.6
  11.4 0.0 all-gather.2.cloned.1.call-update
  11.4 0.0 all-reduce.2.cloned.1.call-start
  11.5 0.6 copy-done.4
  12.1 0.0 copy-done.5
  12.1 0.2 select_reduce_fusion
  12.3 0.0 copy-done.6
  12.4 107.8 %all-gather.2.cloned.1.call-done = bf16[32,2,64,2048]{3,2,1,0:T(8,128)(2,1)} async-done(((bf16[8,2,64,2048]{3,2,1,0:T(8,128)(2,1)}), bf16[32,2,64,2048]{3,2,1,0:T(8,128)(2,1)}) %all-gather.2.cloned.1.call-update) | async-done | bytes 16777232 | tf_op jit(solution)/shard_map/all_gather | solution.py:25
  120.2 7.8 %gather_fusion = bf16[4,2,64,2048]{3,2,1,0:T(8,128)(2,1)} fusion(bf16[32,2,64,2048]{3,2,1,0:T(8,128)(2,1)} %all-gather.2.cloned.1.call-done, s32[1024]{0:T(1024)S(1)} %pad_clamp_fusion), kind=kCustom, calls=%fused_computation | custom fusion | bytes 4194320 | tf_op jit(solution)/shard_map/jit(_take)/gather | solution.py:26
  128.0 3.2 broadcast_select_fusion
  131.1 5.8 %scatter_fusion.1 = bf16[8,2,64,2048]{3,2,1,0:T(8,128)(2,1)} fusion(bf16[8,2,64,2048]{3,2,1,0:T(8,128)(2,1)} %copy.15, s32[4]{0:T(128)S(1)} %get-tuple-element.7, bf16[4,2,64,2048]{3,2,1,0:T(8,128)(2,1)} %broadcast_select_fusion), kind=kCustom, calls=%fused_computation.2 | custom fusion | bytes 6291472 | tf_op jit(solution)/shard_map/scatter | solution.py:29
  136.9 4.1 fusion.3
  141.0 0.0 copy-done
  141.0 2.7 fusion
  143.7 0.0 all-reduce.2.cloned.1.call-update
  143.7 0.0 reduce-scatter.2.cloned.1.call-start
  143.8 31.7 %convolution_convert_fusion = bf16[768,8192]{1,0:T(8,128)(2,1)} fusion(bf16[768,2048]{1,0:T(8,128)(2,1)S(1)} %copy-done, bf16[2048,8192]{1,0:T(8,128)(2,1)} %param.10), kind=kOutput, calls=%fused_computation.3 | convolution fusion | flops 25776095232 | bytes 49283072 | tf_op jit(solution)/shard_map/dot_general | solution.py:40
  175.5 0.0 copy-start.2
  175.5 0.0 copy-start.3
  175.5 0.0 reduce-scatter.2.cloned.1.call-update
  175.5 0.6 copy-done.2
  176.1 0.6 scatter_fusion
  176.7 0.0 copy-done.3
  176.7 0.1 broadcast_compare_fusion
  176.8 10.7 %all-reduce.2.cloned.1.call-done = bf16[768,512]{0,1:T(8,128)(2,1)} async-done(((bf16[768,512]{0,1:T(8,128)(2,1)}), bf16[768,512]{0,1:T(8,128)(2,1)}) %all-reduce.2.cloned.1.call-update) | async-done | bytes 786448 | tf_op jit(solution)/shard_map/psum | solution.py:37
  187.5 2.2 select_convert_fusion
  189.7 211.4 %reduce-scatter.2.cloned.1.call-done = bf16[768,2048]{1,0:T(8,128)(2,1)} async-done(((bf16[768,8192]{1,0:T(8,128)(2,1)}), bf16[768,2048]{1,0:T(8,128)(2,1)}) %reduce-scatter.2.cloned.1.call-update) | async-done | bytes 3145744 | tf_op jit(solution)/shard_map/reduce_scatter | solution.py:41
  401.0 0.0 copy-start.1
  401.0 6.4 %add_convert_fusion = bf16[768,2048]{1,0:T(8,128)(2,1)} fusion(bf16[768,2048]{1,0:T(8,128)(2,1)} %reduce-scatter.2.cloned.1.call-done, bf16[768,512]{0,1:T(8,128)(2,1)} %select_convert_fusion, bf16[512,2048]{1,0:T(8,128)(2,1)} %bitcast.28), kind=kOutput, calls=%fused_computation.4 | convolution fusion | flops 1615331328 | bytes 9175040 | tf_op jit(solution)/shard_map/dot_general | solution.py:44
  407.5 0.0 copy-done.1
  (4 shorter events, 0.0 us)
Async XLA Ops:
  6.5 134.4 %copy-start = (bf16[768,2048]{1,0:T(8,128)(2,1)S(1)}, bf16[768,2048]{1,0:T(8,128)(2,1)}, u32[]{:S(2)}) copy-start(bf16[768,2048]{1,0:T(8,128)(2,1)} %param.9) | copy-start | bytes 9437188
  6.5 113.7 %all-gather.2.cloned.1.call-start = ((), (), s32[]{:S(2)}) async-start(), calls=%async_computation.2 | async-start | bytes 20971520 | tf_op jit(solution)/shard_map/all_gather | solution.py:25
  11.4 0.7 copy-start.4
  11.4 0.7 copy-start.5
  11.4 0.9 copy-start.6
  11.4 176.1 %all-reduce.2.cloned.1.call-start = ((), (), s32[]{:S(2)}) async-start(), calls=%async_computation.3 | async-start | bytes 1572864 | tf_op jit(solution)/shard_map/psum | solution.py:37
  143.7 257.3 %reduce-scatter.2.cloned.1.call-start = ((), (), s32[]{:S(2)}) async-start(), calls=%async_computation.1 | async-start | bytes 15728640 | tf_op jit(solution)/shard_map/reduce_scatter | solution.py:41
  175.5 0.7 copy-start.2
  175.5 1.2 copy-start.3
  401.0 6.4 %copy-start.1 = (bf16[768,2048]{1,0:T(8,128)(2,1)S(1)}, bf16[768,2048]{1,0:T(8,128)(2,1)}, u32[]{:S(2)}) copy-start(bf16[768,2048]{1,0:T(8,128)(2,1)} %param.9) | copy-start | bytes 9437188
Sparse Core Ops, SparseCore 0:
  11.5 108.6 all-gather.1
  143.8 43.5 all-reduce.1
  189.8 211.1 reduce-scatter.1
where the time goes:
time: 414 us
  waiting for transfers between devices  330 us (80%)
  matrix products  40.8 us (10%)
  local copies, waits for them, and re-layouts  24.3 us (6%)
  between operations  13.2 us (3%)
  other arithmetic  5.66 us (1%)
    reduce_scatter x1, waiting for transfers between devices, local(): lax.psum_scatter(head_terms.astype(jnp.bfloat16), 'tensor', scatter_dimen...  211 us
    all_gather x1, waiting for transfers between devices, local(): everything = lax.all_gather(store_factors, 'replica', axis=0, tiled=True)  108 us
    dot_general x1, matrix products, local(): jnp.dot(attn_out, out_weight, preferred_element_type=jnp.float32)  31.7 us
    psum x1, waiting for transfers between devices, local(): summed = lax.psum(shrunk.astype(jnp.bfloat16), 'tensor').astype(jnp.float32)  10.7 us
  transfers between devices with their start and end apart: 3, of which 3 were waited for; matrix products, arithmetic and copies ran while one was open for 8% of the time, Pallas kernels for 0%

commit v1 on v0

v1 whole, which is shorter than its diff:
```python
import functools

import jax
import jax.numpy as jnp
from jax import lax
from jax.experimental import pallas as pl
from jax.experimental.pallas import tpu as pltpu
from jax.sharding import PartitionSpec as P

SHARES = (1, 1)
CAP = 2
VMEM = 28 * 1024 * 1024
SCALE = 4.0


def cost(flops, elements):
    return pl.CostEstimate(
        flops=int(SCALE * flops), bytes_accessed=int(SCALE * 2 * elements), transcendentals=0
    )


def params():
    return pltpu.CompilerParams(vmem_limit_bytes=VMEM)


ORDER = pl.BlockSpec(memory_space=pl.ANY)


def term_kernel(sums, block_ref, a_ref, w_ref, *rest):
    came, out_ref = rest[:sums], rest[-1]
    total = jnp.dot(a_ref[...], w_ref[...], preferred_element_type=jnp.float32)
    for ref in came:
        total = total + ref[...].astype(jnp.float32)
    out_ref[...] = total.astype(out_ref.dtype)


def tile_of(width):
    return min(512, width // sum(SHARES))


def spans(width):
    tile = tile_of(width)
    found, start = [], 0
    for share in SHARES:
        tiles = share * (width // sum(SHARES)) // tile
        found.append((start, tiles))
        start += tiles
    return found


def term(attn, weight, first_tile, tile, tiles, came, after):
    rows, depth = attn.shape
    piece = pl.BlockSpec((rows, tile), lambda j, b: (0, j))
    return pl.pallas_call(
        functools.partial(term_kernel, len(came)),
        grid_spec=pltpu.PrefetchScalarGridSpec(
            num_scalar_prefetch=1,
            grid=(tiles,),
            in_specs=[
                pl.BlockSpec(memory_space=pltpu.VMEM),
                pl.BlockSpec((depth, tile), lambda j, b: (0, b[0] + j)),
            ]
            + [piece] * len(came)
            + [ORDER] * len(after),
            out_specs=piece,
        ),
        out_shape=jax.ShapeDtypeStruct((rows, tiles * tile), jnp.bfloat16),
        compiler_params=params(),
        cost_estimate=cost(2 * rows * depth * tiles * tile, depth * tiles * tile),
    )(first_tile.reshape(1).astype(jnp.int32), attn, weight, *came, *after)


def exchange(size, hop):
    if size & (size - 1) == 0:
        return [(d, d ^ hop) for d in range(size)], lambda d: d ^ hop
    return [(d, (d + hop) % size) for d in range(size)], lambda d: lax.rem(d + hop, size)


def hop_from(size, here, source):
    if size & (size - 1) == 0:
        return here ^ source
    return lax.rem(here - source + size, size)


def pick_kernel(count, row_ref, *refs):
    for n in range(count):
        refs[count + 1 + n][...] = refs[n][...]


def pick(store, rows, after):
    count = rows.shape[0] // CAP
    shape = (1,) + store.shape[1:]

    def from_spec(n):
        return pl.BlockSpec(shape, lambda c, row: (row[n * CAP + c], 0, 0, 0))

    return pl.pallas_call(
        functools.partial(pick_kernel, count),
        grid_spec=pltpu.PrefetchScalarGridSpec(
            num_scalar_prefetch=1,
            grid=(CAP,),
            in_specs=[from_spec(n) for n in range(count)] + [ORDER],
            out_specs=[pl.BlockSpec(shape, lambda c, row: (c, 0, 0, 0))] * count,
        ),
        out_shape=[jax.ShapeDtypeStruct((CAP,) + store.shape[1:], store.dtype)] * count,
        compiler_params=params(),
        cost_estimate=cost(0, 2 * rows.shape[0] * store[0].size),
    )(rows, *[store] * count, after)


def slots_kernel(count, kind_ref, index_ref, id_ref, a_ref, wanted_ref, *rest):
    from_refs = rest[:count]
    mine_ref, expand_ref, factors = rest[-3:]
    s = pl.program_id(0)
    rank = expand_ref.shape[1]
    here = pl.ds(pl.multiple_of(s * rank, rank), rank)

    for n, ref in enumerate(from_refs):

        @pl.when(kind_ref[s] == n)
        def _():
            factors[here, :] = ref[0, 0]
            expand_ref[0] = ref[0, 1]

    @pl.when(s == pl.num_programs(0) - 1)
    def _():
        shrunk = lax.dot_general(
            a_ref[...], factors[...], (((1,), (1,)), ((), ())), preferred_element_type=jnp.float32
        )
        total = jnp.zeros(mine_ref.shape, jnp.float32)
        for n in range(factors.shape[0] // rank):
            total += jnp.where(wanted_ref[...] == id_ref[n], shrunk[:, n * rank : (n + 1) * rank], 0.0)
        mine_ref[...] = total.astype(mine_ref.dtype)


def hold_slots(attn, wanted, ids, kind, index, sources, after):
    rows, depth = attn.shape
    slots = ids.shape[0]
    rank, width = sources[0].shape[2:]

    def from_spec(n):
        return pl.BlockSpec(
            (1, 2, rank, width), lambda s, kind, index, ids: (index[n * slots + s], 0, 0, 0)
        )

    return pl.pallas_call(
        functools.partial(slots_kernel, len(sources)),
        grid_spec=pltpu.PrefetchScalarGridSpec(
            num_scalar_prefetch=3,
            grid=(slots,),
            in_specs=[
                pl.BlockSpec(memory_space=pltpu.VMEM),
                pl.BlockSpec((rows, 1), lambda s, *_: (0, 0)),
            ]
            + [from_spec(n) for n in range(len(sources))]
            + [ORDER],
            out_specs=[
                pl.BlockSpec((rows, rank), lambda s, *_: (0, 0)),
                pl.BlockSpec((1, rank, width), lambda s, *_: (s, 0, 0)),
            ],
            scratch_shapes=[pltpu.VMEM((slots * rank, width), jnp.bfloat16)],
        ),
        out_shape=[
            jax.ShapeDtypeStruct((rows, rank), jnp.bfloat16),
            jax.ShapeDtypeStruct((slots, rank, width), jnp.bfloat16),
        ],
        compiler_params=params(),
        cost_estimate=cost(2 * rows * depth * slots * rank, 3 * slots * rank * width),
    )(kind, index, ids, attn, wanted, *sources, after)


def join_kernel(mine_ref, theirs_ref, after_ref, out_ref):
    out_ref[...] = (
        mine_ref[...].astype(jnp.float32) + theirs_ref[...].astype(jnp.float32)
    ).astype(out_ref.dtype)


def join(mine, theirs, after):
    whole = pl.BlockSpec(mine.shape, lambda: (0, 0))
    return pl.pallas_call(
        join_kernel,
        in_specs=[whole, whole, ORDER],
        out_specs=whole,
        out_shape=jax.ShapeDtypeStruct(mine.shape, mine.dtype),
        compiler_params=params(),
        cost_estimate=cost(0, 3 * mine.size),
    )(mine, theirs, after)


def own_kernel(block_ref, id_ref, a_ref, w_ref, chosen_ref, wanted_ref, expand_ref, after_ref, out_ref, masked):
    @pl.when(pl.program_id(0) == 0)
    def _():
        chosen = chosen_ref[...]
        rank = chosen.shape[1]
        for n in range(masked.shape[1] // rank):
            masked[:, n * rank : (n + 1) * rank] = jnp.where(
                wanted_ref[...] == id_ref[n], chosen, jnp.zeros_like(chosen)
            )

    out_ref[...] = jnp.dot(
        a_ref[...], w_ref[...], preferred_element_type=jnp.float32
    ) + jnp.dot(masked[...], expand_ref[...], preferred_element_type=jnp.float32)


def own_term(attn, weight, block, chosen, wanted, ids, expand, after):
    rows, depth = attn.shape
    ranks, width = expand.shape
    tile = tile_of(width)
    tiles = width // tile
    return pl.pallas_call(
        own_kernel,
        grid_spec=pltpu.PrefetchScalarGridSpec(
            num_scalar_prefetch=2,
            grid=(tiles,),
            in_specs=[
                pl.BlockSpec(memory_space=pltpu.VMEM),
                pl.BlockSpec((depth, tile), lambda j, b, ids: (0, b[0] * tiles + j)),
                pl.BlockSpec(chosen.shape, lambda j, *_: (0, 0)),
                pl.BlockSpec((rows, 1), lambda j, *_: (0, 0)),
                pl.BlockSpec((ranks, tile), lambda j, *_: (0, j)),
                ORDER,
            ],
            out_specs=pl.BlockSpec((rows, tile), lambda j, *_: (0, j)),
            scratch_shapes=[pltpu.VMEM((rows, ranks), jnp.bfloat16)],
        ),
        out_shape=jax.ShapeDtypeStruct((rows, width), jnp.float32),
        compiler_params=params(),
        cost_estimate=cost(2 * rows * width * (depth + ranks), (depth + ranks) * width + 2 * rows * width),
    )(block.reshape(1).astype(jnp.int32), ids, attn, weight, chosen, wanted, expand, after)


def finish_kernel(own_ref, right_ref, left_ref, *rest):
    out_ref = rest[-1]
    out_ref[...] = (
        own_ref[...] + (right_ref[...].astype(jnp.float32) + left_ref[...].astype(jnp.float32))
    ).astype(out_ref.dtype)


def finish(own, right, left, first_tile, so_far):
    rows, width = own.shape
    tile = tile_of(width)
    here = pl.BlockSpec((rows, tile), lambda j: (0, first_tile + j))
    came = pl.BlockSpec((rows, tile), lambda j: (0, j))
    extra = [] if so_far is None else [so_far]
    return pl.pallas_call(
        finish_kernel,
        grid=(right.shape[1] // tile,),
        in_specs=[here, came, came] + [pl.BlockSpec(memory_space=pl.ANY)] * len(extra),
        out_specs=here,
        out_shape=jax.ShapeDtypeStruct((rows, width), jnp.bfloat16),
        input_output_aliases={3: 0} if extra else {},
        compiler_params=params(),
        cost_estimate=cost(0, 5 * rows * right.shape[1]),
    )(own, right, left, *extra)


def make_local(replicas, tensor):
    def local(
        attn_out,
        out_weight,
        store_factors,
        resident_factors,
        resident_ids,
        evict_slots,
        incoming,
        store_place,
        req_adapter,
    ):
        z = lax.axis_index("tensor")
        own = lax.axis_index("replica")
        width = out_weight.shape[1] // tensor
        tile = tile_of(width)
        pieces = spans(width)
        slots = resident_factors.shape[0]
        store_rows = store_factors.shape[0]
        evict = evict_slots[0]
        to_right = [(d, d + 1) for d in range(tensor - 1)]
        to_left = [(d + 1, d) for d in range(tensor - 1)]

        def product(block, piece, came, after):
            start, tiles = pieces[piece]
            first = jnp.clip(block, 0, tensor - 1) * (width // tile) + start
            return term(attn_out, out_weight, first, tile, tiles, came, [] if after is attn_out else [after])

        def step_of(step, came_right, came_left, after, between):
            right_pairs = to_right[: step + 1]
            left_pairs = to_left[tensor - 2 - step :]
            right_block = tensor - 1 - step + z
            left_block = z + step + 1 - tensor
            rights, lefts = [], []
            for piece in range(len(pieces)):
                right_in = [] if came_right is None else [came_right[piece]]
                left_in = [] if came_left is None else [came_left[piece]]
                if 2 * step < tensor - 1:
                    block = jnp.where(2 * z < tensor, right_block, left_block)
                    same = right_in and right_in[0] is left_in[0]
                    out = product(block, piece, right_in + ([] if same else left_in), after)
                    after = out
                    if 2 * step + 3 < tensor:
                        moved = lax.ppermute(out, "tensor", right_pairs + left_pairs)
                        rights.append(moved)
                        lefts.append(moved)
                    else:
                        rights.append(lax.ppermute(out, "tensor", right_pairs))
                        lefts.append(lax.ppermute(out, "tensor", left_pairs))
                else:
                    out = product(right_block, piece, right_in, after)
                    rights.append(lax.ppermute(out, "tensor", right_pairs))
                    after = out
                    out = product(left_block, piece, left_in, after)
                    lefts.append(lax.ppermute(out, "tensor", left_pairs))
                    after = out
                if piece < len(pieces) - 1 or step == 0:
                    after = between(after)
            return rights, lefts, after

        matches = incoming[:, :, None] == jnp.arange(store_place.shape[0], dtype=jnp.int32)
        place = jnp.sum(jnp.where(matches, store_place, 0), axis=2)
        owners = place // store_rows
        spots = jnp.arange(place.shape[1], dtype=jnp.int32)
        earlier = jnp.sum(
            (owners[:, :, None] == owners[:, None, :]) & (spots[None, :] < spots[:, None]), axis=2
        ).astype(jnp.int32)
        asked = (owners == own)[:, :, None] & (
            earlier[:, :, None] == jnp.arange(CAP, dtype=jnp.int32)
        )
        rows_for = jnp.sum(jnp.where(asked, (place % store_rows)[:, :, None], 0), axis=1)
        hops = [exchange(replicas, hop) for hop in range(1, replicas)]
        send_rows = [
            lax.dynamic_index_in_dim(rows_for, to(own), 0, keepdims=False) for _, to in hops
        ]

        my_place = lax.dynamic_index_in_dim(place, own, 0, keepdims=False)
        my_earlier = lax.dynamic_index_in_dim(earlier, own, 0, keepdims=False)
        my_ids = lax.dynamic_index_in_dim(incoming, own, 0, keepdims=False)
        my_hop = hop_from(replicas, own, my_place // store_rows)
        my_index = jnp.where(my_hop == 0, my_place % store_rows, my_earlier)
        replaced = evict[None, :] == jnp.arange(slots, dtype=jnp.int32)[:, None]
        is_new = jnp.any(replaced, axis=1)

        def per_slot(new, old):
            chosen = jnp.sum(jnp.where(replaced, new[None, :], 0), axis=1)
            return jnp.where(is_new, chosen, old).astype(jnp.int32)

        kind = per_slot(1 + my_hop, jnp.zeros((slots,), jnp.int32))
        place_in = per_slot(my_index, jnp.arange(slots, dtype=jnp.int32))
        ids = per_slot(my_ids, resident_ids[0])
        index = jnp.concatenate(
            [jnp.where(kind == n, place_in, 0) for n in range(1 + replicas)]
        ).astype(jnp.int32)
        wanted = req_adapter[:, None]
        sources = [resident_factors, store_factors]
        state = {"mine": None, "bit": 1, "theirs": None}

        def fetch(after):
            if not send_rows:
                return after
            picked = pick(store_factors, jnp.concatenate(send_rows).astype(jnp.int32), after)
            for piece, (pairs, _) in reversed(list(zip(picked, hops))):
                sources.insert(2, lax.ppermute(piece, "replica", pairs))
            return picked[0]

        def send_mine():
            if state["bit"] < tensor:
                pairs, _ = exchange(tensor, state["bit"])
                state["theirs"] = lax.ppermute(state["mine"], "tensor", pairs)

        def shrink(after):
            state["mine"], state["expand"] = hold_slots(
                attn_out, wanted, ids, kind, index, sources, after
            )
            if tensor & (tensor - 1) == 0:
                send_mine()
            else:
                state["mine"] = lax.psum(state["mine"], "tensor")
            return state["mine"]

        def add_theirs(after):
            if state["theirs"] is None:
                return after
            state["mine"] = join(state["mine"], state["theirs"], after)
            state["bit"] *= 2
            state["theirs"] = None
            send_mine()
            return state["mine"]

        def after_pieces(step):
            if step == 0:
                calls = [None] * (len(pieces) - 1) + [fetch]
            elif step == 1:
                calls = [shrink] + [None] * len(pieces)
            else:
                calls = [None] * len(pieces)
            todo = iter(calls)

            def between(after):
                call = next(todo)
                return after if call is None else call(after)

            return between

        rights, lefts, last = None, None, attn_out
        for step in range(tensor - 1):
            if step > 1:
                last = add_theirs(last)
            rights, lefts, last = step_of(step, rights, lefts, last, after_pieces(step))
        if tensor < 3:
            last = shrink(fetch(last) if tensor == 1 else last)
        while state["theirs"] is not None:
            last = add_theirs(last)
        total = own_term(
            attn_out,
            out_weight,
            z,
            state["mine"],
            wanted,
            ids,
            state["expand"].reshape(-1, width),
            last,
        )
        if tensor == 1:
            return total.astype(jnp.bfloat16)
        out = None
        for piece, (start, _) in enumerate(pieces):
            out = finish(total, rights[piece], lefts[piece], start, out)
        return out

    return local


def solution(mesh):
    return jax.shard_map(
        make_local(mesh.shape["replica"], mesh.shape["tensor"]),
        mesh=mesh,
        in_specs=(
            P(("groups", "replica"), "tensor"),
            P("tensor", None),
            P(("groups", "replica"), None, None, "tensor"),
            P(("groups", "replica"), None, None, "tensor"),
            P(("groups", "replica"), None),
            P(("groups", "replica"), None),
            P("groups", None),
            P("groups"),
            P(("groups", "replica")),
        ),
        out_specs=P(("groups", "replica"), "tensor"),
        check_vma=False,
    )
```

time: 414 us -> 226 us (0.55)
  waiting for transfers between devices: 330 us -> 112 us
  Pallas kernels: 0 us -> 68.3 us
  matrix products: 40.8 us -> 0 us
  starting transfers between devices: 0.09 us -> 32.6 us
  local copies, waits for them, and re-layouts: 24.3 us -> 9.03 us
  between operations: 13.2 us -> 0.3 us
    reduce_scatter x1 -> x0, waiting for transfers between devices: 211 us -> none  [local(): lax.psum_scatter(head_terms.astype(jnp.bfloat16), 'tensor', scatter_dimen...]
    ppermute x0 -> x15, waiting for transfers between devices: none -> 112 us  [the longest x4 44.3 us: step_of(): rights.append(lax.ppermute(out, 'tensor', right_pairs))]
    all_gather x1 -> x0, waiting for transfers between devices: 108 us -> none  [local(): everything = lax.all_gather(store_factors, 'replica', axis=0, tiled=True)]
    pallas_call x0 -> x15, Pallas kernels: none -> 68.3 us  [the longest x8 43.6 us: term(): pl.pallas_call(functools.partial(term_kernel, len(came)), grid_spec=pltpu...]
    dot_general x3 -> x0, matrix products: 40.8 us -> none  [the longest x1 31.7 us: local(): jnp.dot(attn_out, out_weight, preferred_element_type=jnp.float32)]
    ppermute x0 -> x15, starting transfers between devices: none -> 32.6 us  [the longest x4 15 us: step_of(): rights.append(lax.ppermute(out, 'tensor', right_pairs))]
    psum x1 -> x0, waiting for transfers between devices: 10.7 us -> none  [local(): summed = lax.psum(shrunk.astype(jnp.bfloat16), 'tensor').astype(jnp.float32)]
    gather x1 -> x0, local copies, waits for them, and re-layouts: 7.77 us -> none  [local(): fetched = jnp.take(everything, my_place, axis=0)]
  transfers between devices with their start and end apart: 3 -> 15, of which waited for: 3 -> 8; matrix products, arithmetic and copies ran while one was open for 8% -> 2% of each run, Pallas kernels for 0% -> 27%
where the time goes in v1:
time: 226 us
  waiting for transfers between devices  112 us (50%)
  Pallas kernels  68.3 us (30%)
  starting transfers between devices  32.6 us (14%)
  local copies, waits for them, and re-layouts  9.03 us (4%)
  other arithmetic  3.47 us (2%)
    ppermute x4, waiting for transfers between devices, step_of(): rights.append(lax.ppermute(out, 'tensor', right_pairs))  44.3 us
    pallas_call x8, Pallas kernels, term(): pl.pallas_call(functools.partial(term_kernel, len(came)), grid_spec=pltpu...  43.6 us
    ppermute x2, waiting for transfers between devices, send_mine(): state['theirs'] = lax.ppermute(state['mine'], 'tensor', pairs)  27.3 us
    ppermute x4, starting transfers between devices, step_of(): rights.append(lax.ppermute(out, 'tensor', right_pairs))  15 us
    ppermute x2, waiting for transfers between devices, step_of(): moved = lax.ppermute(out, 'tensor', right_pairs + left_pairs)  14.9 us
    ppermute x3, waiting for transfers between devices, fetch(): sources.insert(2, lax.ppermute(piece, 'replica', pairs))  13.8 us
    pallas_call x1, Pallas kernels, own_term(): pl.pallas_call(own_kernel, grid_spec=pltpu.PrefetchScalarGridSpec(num_sca...  12.7 us
    ppermute x4, waiting for transfers between devices, step_of(): lefts.append(lax.ppermute(out, 'tensor', left_pairs))  11.6 us
  transfers between devices with their start and end apart: 15, of which 8 were waited for; matrix products, arithmetic and copies ran while one was open for 2% of the time, Pallas kernels for 27%

profile of v1, /device:TPU:0, one launch (start us, length us, event | category | flops | bytes accessed | tf_op | source)
XLA Modules:
  0.0 225.5 jit_solution(13948948673206364260)
XLA Ops:
  0.0 1.9 copy-done.3
  1.9 6.1 %shard_map.91.rest_0_ = bf16[768,1024]{1,0:T(8,128)(2,1)} custom-call(s32[1]{0:T(128)} %bitcast.7.block_ref, bf16[768,2048]{1,0:T(8,128)(2,1)S(1)} %copy-done.3, bf16[2048,8192]{1,0:T(8,128)(2,1)} %w_ref.17), custom_call_target="tpu_custom_call" | custom-call | flops 12884901888 | bytes 16777216 | tf_op jit(solution)/shard_map/pallas_call | solution.py:54
  8.0 6.1 %collective-permute-start.3 = (bf16[768,1024]{1,0:T(8,128)(2,1)}, bf16[768,1024]{1,0:T(8,128)(2,1)}, u32[]{:S(2)}, u32[]{:S(2)}) collective-permute-start(bf16[768,1024]{1,0:T(8,128)(2,1)} %shard_map.91.rest_0_), channel_id=1, source_target_pairs={{0,1},{3,2},{4,5},{7,6},{8,9},{11,10},{12,13},{15,14},{16,17},{19,... | collective-permute-start | bytes 4718600 | tf_op jit(solution)/shard_map/ppermute | solution.py:300
  14.1 1.9 copy-done.4
  15.9 5.3 %shard_map.92.refs_3_ = bf16[768,1024]{1,0:T(8,128)(2,1)S(1)} custom-call(s32[1]{0:T(128)} %bitcast.6.block_ref, bf16[768,2048]{1,0:T(8,128)(2,1)S(1)} %copy-done.4, bf16[2048,8192]{1,0:T(8,128)(2,1)} %w_ref.17, bf16[768,1024]{1,0:T(8,128)(2,1)} %shard_map.91.rest_0_), custom_call_target="tpu_custom_call" | custom-call | flops 12884901888 | bytes 16777216 | tf_op jit(solution)/shard_map/pallas_call | solution.py:54
  21.3 1.4 collective-permute-start.5
  22.7 0.0 copy-done.7
  22.7 0.0 copy-done.8
  22.7 0.2 select_reduce_fusion
  22.9 0.2 convert_reduce_fusion
  23.2 0.1 select_reduce_fusion.1
  23.3 0.2 fusion.3
  23.6 0.1 pad_add_fusion.row_ref
  23.6 2.2 copy-done
  25.8 2.3 %shard_map.93 = (bf16[2,2,64,2048]{3,2,1,0:T(8,128)(2,1)}, bf16[2,2,64,2048]{3,2,1,0:T(8,128)(2,1)}, bf16[2,2,64,2048]{3,2,1,0:T(8,128)(2,1)}) custom-call(s32[6]{0:T(128)S(1)} %pad_add_fusion.row_ref, bf16[8,2,64,2048]{3,2,1,0:T(8,128)(2,1)S(1)} %copy-done, bf16[8,2,64,2048]{3,2,1,0:T(8,128)(2,1)S(1)} %copy-done, bf16[8,2,64,2048]{3,2,1,0:T(8,128)(2,1)S(1)} %copy-done, ...), custom_call_target="tpu_custom_call" | custom-call | bytes 25165824 | tf_op jit(solution)/shard_map/pallas_call | solution.py:97
  28.2 1.5 collective-permute-start.1
  29.7 0.0 collective-permute-start.2
  29.7 0.6 collective-permute-start
  30.3 0.0 copy-done.6
  30.3 0.2 broadcast_in_dim.86.wanted_ref
  30.5 0.7 fusion.1
  31.3 0.7 select_reduce_fusion.2
  32.0 0.7 compare_select_fusion
  32.7 0.6 compare_select_fusion.1
  33.3 0.8 concatenate.6.index_ref
  34.0 13.9 %collective-permute-done.3.rest_0_ = bf16[768,1024]{1,0:T(8,128)(2,1)} collective-permute-done((bf16[768,1024]{1,0:T(8,128)(2,1)}, bf16[768,1024]{1,0:T(8,128)(2,1)}, u32[]{:S(2)}, u32[]{:S(2)}) %collective-permute-start.3) | collective-permute-done | bytes 1572896 | tf_op jit(solution)/shard_map/ppermute | solution.py:300
  48.0 1.9 copy-done.5
  49.9 5.6 %shard_map.94.rest_5_ = bf16[768,1024]{1,0:T(8,128)(2,1)S(1)} custom-call(s32[1]{0:T(128)} %bitcast.8.block_ref, bf16[768,2048]{1,0:T(8,128)(2,1)S(1)} %copy-done.5, bf16[2048,8192]{1,0:T(8,128)(2,1)} %w_ref.17, bf16[768,1024]{1,0:T(8,128)(2,1)} %collective-permute-done.3.rest_0_, bf16[2,2,64,2048]{3,2,1,0:T(8,128)(2,1)} %get-tuple-element.10.rest_1_), custom_call_target="tpu_custom_call" | custom-call | flops 12884901888 | bytes 16777216 | tf_op jit(solution)/shard_map/pallas_call | solution.py:54
  55.5 4.5 %collective-permute-start.10 = (bf16[768,1024]{1,0:T(8,128)(2,1)S(1)}, bf16[768,1024]{1,0:T(8,128)(2,1)S(1)}, u32[]{:S(2)}, u32[]{:S(2)}) collective-permute-start(bf16[768,1024]{1,0:T(8,128)(2,1)S(1)} %shard_map.94.rest_5_), channel_id=1, source_target_pairs={{0,1},{1,2},{4,5},{5,6},{8,9},{9,10},{12,13},{13,14},{16,17},{17,1... | collective-permute-start | bytes 4718600 | tf_op jit(solution)/shard_map/ppermute | solution.py:304
  60.0 0.0 collective-permute-done.1.rest_3_
  60.0 0.8 collective-permute-start.9
  60.8 13.8 %collective-permute-done.2.rest_4_ = bf16[2,2,64,2048]{3,2,1,0:T(8,128)(2,1)} collective-permute-done((bf16[2,2,64,2048]{3,2,1,0:T(8,128)(2,1)}, bf16[2,2,64,2048]{3,2,1,0:T(8,128)(2,1)}, u32[]{:S(2)}, u32[]{:S(2)}) %collective-permute-start.2) | collective-permute-done | bytes 1048608 | tf_op jit(solution)/shard_map/ppermute | solution.py:360
  74.6 0.0 collective-permute-done.rest_2_
  74.6 0.0 copy-done.1
  74.6 5.9 %shard_map.95 = (bf16[768,64]{1,0:T(8,128)(2,1)S(1)}, bf16[8,64,2048]{2,1,0:T(8,128)(2,1)S(1)}) custom-call(s32[8]{0:T(128)S(1)} %get-tuple-element.25.kind_ref, s32[40]{0:T(128)S(1)} %concatenate.6.index_ref, s32[8]{0:T(128)S(1)} %get-tuple-element.32.id_ref, bf16[768,2048]{1,0:T(8,128)(2,1)S(1)} %copy-done.5, s32[768,1]{1,0:T(8,128)S(1)} %broadcast_in_dim.86.wanted_ref, ...), custom_call_target="tpu_custom_call" | custom-call | flops 6442450944 | bytes 25165824 | tf_op jit(solution)/shard_map/pallas_call | solution.py:146
  80.5 0.1 collective-permute-start.4
  80.6 1.0 collective-permute-done.5.rest_0_
  81.6 5.3 %shard_map.96.after_ref = bf16[768,1024]{1,0:T(8,128)(2,1)S(1)} custom-call(s32[1]{0:T(128)} %bitcast.9.block_ref, bf16[768,2048]{1,0:T(8,128)(2,1)S(1)} %copy-done.5, bf16[2048,8192]{1,0:T(8,128)(2,1)} %w_ref.17, bf16[768,1024]{1,0:T(8,128)(2,1)S(1)} %collective-permute-done.5.rest_0_, bf16[768,64]{1,0:T(8,128)(2,1)S(1)} %get-tuple-element.13.rest_1_.mine_ref), custom_call_target="tpu_custom_call" | custom-call | flops 12884901888 | bytes 16777216 | tf_op jit(solution)/shard_map/pallas_call | solution.py:54
  86.9 4.5 %collective-permute-start.8 = (bf16[768,1024]{1,0:T(8,128)(2,1)S(1)}, bf16[768,1024]{1,0:T(8,128)(2,1)S(1)}, u32[]{:S(2)}, u32[]{:S(2)}) collective-permute-start(bf16[768,1024]{1,0:T(8,128)(2,1)S(1)} %shard_map.96.after_ref), channel_id=1, source_target_pairs={{0,1},{1,2},{4,5},{5,6},{8,9},{9,10},{12,13},{13,14},{16,17},{17,1... | collective-permute-start | bytes 4718600 | tf_op jit(solution)/shard_map/ppermute | solution.py:304
  91.4 0.8 collective-permute-start.7
  92.1 27.3 %collective-permute-done.4.theirs_ref = bf16[768,64]{1,0:T(8,128)(2,1)S(1)} collective-permute-done((bf16[768,64]{1,0:T(8,128)(2,1)S(1)}, bf16[768,64]{1,0:T(8,128)(2,1)S(1)}, u32[]{:S(2)}, u32[]{:S(2)}) %collective-permute-start.4) | collective-permute-done | bytes 98336 | tf_op jit(solution)/shard_map/ppermute | solution.py:366
  119.5 0.1 shard_map.97.rest_1_.mine_ref
  119.6 3.6 %collective-permute-start.6 = (bf16[768,64]{1,0:T(8,128)(2,1)S(1)}, bf16[768,64]{1,0:T(8,128)(2,1)S(1)}, u32[]{:S(2)}, u32[]{:S(2)}) collective-permute-start(bf16[768,64]{1,0:T(8,128)(2,1)S(1)} %shard_map.97.rest_1_.mine_ref), channel_id=1, source_target_pairs={{0,2},{1,3},{2,0},{3,1},{4,6},{5,7},{6,4},{7,5},{8,10},{9,11},{10,... | collective-permute-start | bytes 294920 | tf_op jit(solution)/shard_map/ppermute | solution.py:366
  123.1 0.0 collective-permute-done.10.rest_0_
  123.1 5.3 %shard_map.98.rest_1_ = bf16[768,1024]{1,0:T(8,128)(2,1)S(1)} custom-call(s32[1]{0:T(128)} %bitcast.13.block_ref, bf16[768,2048]{1,0:T(8,128)(2,1)S(1)} %copy-done.5, bf16[2048,8192]{1,0:T(8,128)(2,1)} %w_ref.17, bf16[768,1024]{1,0:T(8,128)(2,1)S(1)} %collective-permute-done.10.rest_0_, bf16[768,64]{1,0:T(8,128)(2,1)S(1)} %shard_map.97.rest_1_.mine_ref), custom_call_target="tpu_custom_call" | custom-call | flops 12884901888 | bytes 16777216 | tf_op jit(solution)/shard_map/pallas_call | solution.py:54
  128.4 1.5 collective-permute-start.13
  130.0 0.0 collective-permute-done.9.rest_0_
  130.0 5.3 %shard_map.99.rest_1_ = bf16[768,1024]{1,0:T(8,128)(2,1)S(1)} custom-call(s32[1]{0:T(128)} %bitcast.12.block_ref, bf16[768,2048]{1,0:T(8,128)(2,1)S(1)} %copy-done.5, bf16[2048,8192]{1,0:T(8,128)(2,1)} %w_ref.17, bf16[768,1024]{1,0:T(8,128)(2,1)S(1)} %collective-permute-done.9.rest_0_, bf16[768,1024]{1,0:T(8,128)(2,1)S(1)} %shard_map.98.rest_1_), custom_call_target="tpu_custom_call" | custom-call | flops 12884901888 | bytes 16777216 | tf_op jit(solution)/shard_map/pallas_call | solution.py:54
  135.3 1.5 collective-permute-start.14
  136.8 16.4 %collective-permute-done.8.rest_0_ = bf16[768,1024]{1,0:T(8,128)(2,1)S(1)} collective-permute-done((bf16[768,1024]{1,0:T(8,128)(2,1)S(1)}, bf16[768,1024]{1,0:T(8,128)(2,1)S(1)}, u32[]{:S(2)}, u32[]{:S(2)}) %collective-permute-start.8) | collective-permute-done | bytes 1572896 | tf_op jit(solution)/shard_map/ppermute | solution.py:304
  153.2 5.3 %shard_map.100.rest_1_ = bf16[768,1024]{1,0:T(8,128)(2,1)S(1)} custom-call(s32[1]{0:T(128)} %bitcast.11.block_ref, bf16[768,2048]{1,0:T(8,128)(2,1)S(1)} %copy-done.5, bf16[2048,8192]{1,0:T(8,128)(2,1)} %w_ref.17, bf16[768,1024]{1,0:T(8,128)(2,1)S(1)} %collective-permute-done.8.rest_0_, bf16[768,1024]{1,0:T(8,128)(2,1)S(1)} %shard_map.99.rest_1_), custom_call_target="tpu_custom_call" | custom-call | flops 12884901888 | bytes 16777216 | tf_op jit(solution)/shard_map/pallas_call | solution.py:54
  158.5 4.5 %collective-permute-start.11 = (bf16[768,1024]{1,0:T(8,128)(2,1)S(1)}, bf16[768,1024]{1,0:T(8,128)(2,1)S(1)}, u32[]{:S(2)}, u32[]{:S(2)}) collective-permute-start(bf16[768,1024]{1,0:T(8,128)(2,1)S(1)} %shard_map.100.rest_1_), channel_id=1, source_target_pairs={{0,1},{1,2},{2,3},{4,5},{5,6},{6,7},{8,9},{9,10},{10,11},{12,13},{... | collective-permute-start | bytes 4718600 | tf_op jit(solution)/shard_map/ppermute | solution.py:308
  163.0 0.0 collective-permute-done.7.rest_0_
  163.0 5.3 %shard_map.101.after_ref = bf16[768,1024]{1,0:T(8,128)(2,1)S(1)} custom-call(s32[1]{0:T(128)} %bitcast.10.block_ref, bf16[768,2048]{1,0:T(8,128)(2,1)S(1)} %copy-done.5, bf16[2048,8192]{1,0:T(8,128)(2,1)} %w_ref.17, bf16[768,1024]{1,0:T(8,128)(2,1)S(1)} %collective-permute-done.7.rest_0_, bf16[768,1024]{1,0:T(8,128)(2,1)S(1)} %shard_map.100.rest_1_), custom_call_target="tpu_custom_call" | custom-call | flops 12884901888 | bytes 16777216 | tf_op jit(solution)/shard_map/pallas_call | solution.py:54
  168.3 1.3 collective-permute-start.12
  169.6 0.0 collective-permute-done.6.theirs_ref
  169.7 0.1 shard_map.102.chosen_ref.after_ref
  169.7 12.7 %shard_map.103.own_ref = f32[768,2048]{1,0:T(8,128)S(1)} custom-call(s32[1]{0:T(128)} %bitcast.block_ref, s32[8]{0:T(128)S(1)} %get-tuple-element.32.id_ref, bf16[768,2048]{1,0:T(8,128)(2,1)S(1)} %copy-done.5, bf16[2048,8192]{1,0:T(8,128)(2,1)} %w_ref.17, bf16[768,64]{1,0:T(8,128)(2,1)S(1)} %shard_map.102.chosen_ref.after_ref, ...), custom_call_target="tpu_custom_call" | custom-call | flops 32212254720 | bytes 67108864 | tf_op jit(solution)/shard_map/pallas_call | solution.py:210
  182.4 8.7 %collective-permute-done.13.right_ref = bf16[768,1024]{1,0:T(8,128)(2,1)S(1)} collective-permute-done((bf16[768,1024]{1,0:T(8,128)(2,1)S(1)}, bf16[768,1024]{1,0:T(8,128)(2,1)S(1)}, u32[]{:S(2)}, u32[]{:S(2)}) %collective-permute-start.13) | collective-permute-done | bytes 1572896 | tf_op jit(solution)/shard_map/ppermute | solution.py:308
  191.2 0.0 collective-permute-done.14.left_ref
  191.2 1.8 shard_map.104.rest_0_
  193.0 11.6 %collective-permute-done.12.left_ref = bf16[768,1024]{1,0:T(8,128)(2,1)S(1)} collective-permute-done((bf16[768,1024]{1,0:T(8,128)(2,1)S(1)}, bf16[768,1024]{1,0:T(8,128)(2,1)S(1)}, u32[]{:S(2)}, u32[]{:S(2)}) %collective-permute-start.12) | collective-permute-done | bytes 1572896 | tf_op jit(solution)/shard_map/ppermute | solution.py:311
  204.6 19.1 %collective-permute-done.11.right_ref = bf16[768,1024]{1,0:T(8,128)(2,1)S(1)} collective-permute-done((bf16[768,1024]{1,0:T(8,128)(2,1)S(1)}, bf16[768,1024]{1,0:T(8,128)(2,1)S(1)}, u32[]{:S(2)}, u32[]{:S(2)}) %collective-permute-start.11) | collective-permute-done | bytes 1572896 | tf_op jit(solution)/shard_map/ppermute | solution.py:308
  223.7 1.8 shard_map.105
  (15 shorter events, 0.1 us)
Async XLA Ops:
  0.0 1.9 copy-start.3
  8.0 40.0 %collective-permute-start.3 = (bf16[768,1024]{1,0:T(8,128)(2,1)}, bf16[768,1024]{1,0:T(8,128)(2,1)}, u32[]{:S(2)}, u32[]{:S(2)}) collective-permute-start(bf16[768,1024]{1,0:T(8,128)(2,1)} %shard_map.91.rest_0_), channel_id=1, source_target_pairs={{0,1},{3,2},{4,5},{7,6},{8,9},{11,10},{12,13},{15,14},{16,17},{19,... | collective-permute-start | bytes 4718600 | tf_op jit(solution)/shard_map/ppermute | solution.py:300
  14.1 1.9 copy-start.4
  15.9 6.7 %copy-start.7 = (s32[4,4]{1,0:T(4,128)S(1)}, s32[4,4]{1,0:T(4,128)}, u32[]{:S(2)}) copy-start(s32[4,4]{1,0:T(4,128)} %param.15) | copy-start | bytes 196
  15.9 6.7 %copy-start.8 = (s32[32]{0:T(128)S(1)}, s32[32]{0:T(128)}, u32[]{:S(2)}) copy-start(s32[32]{0:T(128)} %param.16) | copy-start | bytes 388
  21.3 60.3 %collective-permute-start.5 = (bf16[768,1024]{1,0:T(8,128)(2,1)S(1)}, bf16[768,1024]{1,0:T(8,128)(2,1)S(1)}, u32[]{:S(2)}, u32[]{:S(2)}) collective-permute-start(bf16[768,1024]{1,0:T(8,128)(2,1)S(1)} %shard_map.92.refs_3_), channel_id=1, source_target_pairs={{0,1},{3,2},{4,5},{7,6},{8,9},{11,10},{12,13},{15,14},{16,17},{19,... | collective-permute-start | bytes 4718600 | tf_op jit(solution)/shard_map/ppermute | solution.py:300
  23.6 2.2 copy-start
  25.8 4.5 %copy-start.6 = (s32[768]{0:T(1024)S(1)}, s32[768]{0:T(1024)}, u32[]{:S(2)}) copy-start(s32[768]{0:T(1024)} %param.17) | copy-start | bytes 9220
  28.2 31.9 %collective-permute-start.1 = (bf16[2,2,64,2048]{3,2,1,0:T(8,128)(2,1)}, bf16[2,2,64,2048]{3,2,1,0:T(8,128)(2,1)}, u32[]{:S(2)}, u32[]{:S(2)}) collective-permute-start(bf16[2,2,64,2048]{3,2,1,0:T(8,128)(2,1)} %get-tuple-element.11), channel_id=1, source_target_pairs={{0,8},{4,12},{8,0},{12,4},{1,9},{5,13},{9,1},{13,5},{2,10},{6,14},... | collective-permute-start | bytes 3145736 | tf_op jit(solution)/shard_map/ppermute | solution.py:360
  29.7 44.9 %collective-permute-start.2 = (bf16[2,2,64,2048]{3,2,1,0:T(8,128)(2,1)}, bf16[2,2,64,2048]{3,2,1,0:T(8,128)(2,1)}, u32[]{:S(2)}, u32[]{:S(2)}) collective-permute-start(bf16[2,2,64,2048]{3,2,1,0:T(8,128)(2,1)} %get-tuple-element.12), channel_id=1, source_target_pairs={{0,12},{4,8},{8,4},{12,0},{1,13},{5,9},{9,5},{13,1},{2,14},{6,10},... | collective-permute-start | bytes 3145736 | tf_op jit(solution)/shard_map/ppermute | solution.py:360
  29.7 44.9 %collective-permute-start = (bf16[2,2,64,2048]{3,2,1,0:T(8,128)(2,1)}, bf16[2,2,64,2048]{3,2,1,0:T(8,128)(2,1)}, u32[]{:S(2)}, u32[]{:S(2)}) collective-permute-start(bf16[2,2,64,2048]{3,2,1,0:T(8,128)(2,1)} %get-tuple-element.10.rest_1_), channel_id=1, source_target_pairs={{0,4},{4,0},{8,12},{12,8},{1,5},{5,1},{9,13},{13,9},{2,6},{6,2},{1... | collective-permute-start | bytes 3145736 | tf_op jit(solution)/shard_map/ppermute | solution.py:360
  48.0 1.9 copy-start.5
  49.9 24.7 %copy-start.1 = (bf16[8,2,64,2048]{3,2,1,0:T(8,128)(2,1)S(1)}, bf16[8,2,64,2048]{3,2,1,0:T(8,128)(2,1)}, u32[]{:S(2)}) copy-start(bf16[8,2,64,2048]{3,2,1,0:T(8,128)(2,1)} %rest_1_.1) | copy-start | bytes 12582916
  49.9 24.7 %copy-start.2 = (bf16[8,2,64,2048]{3,2,1,0:T(8,128)(2,1)S(1)}, bf16[8,2,64,2048]{3,2,1,0:T(8,128)(2,1)}, u32[]{:S(2)}) copy-start(bf16[8,2,64,2048]{3,2,1,0:T(8,128)(2,1)} %rest_0_.1) | copy-start | bytes 12582916
  55.5 67.6 %collective-permute-start.10 = (bf16[768,1024]{1,0:T(8,128)(2,1)S(1)}, bf16[768,1024]{1,0:T(8,128)(2,1)S(1)}, u32[]{:S(2)}, u32[]{:S(2)}) collective-permute-start(bf16[768,1024]{1,0:T(8,128)(2,1)S(1)} %shard_map.94.rest_5_), channel_id=1, source_target_pairs={{0,1},{1,2},{4,5},{5,6},{8,9},{9,10},{12,13},{13,14},{16,17},{17,1... | collective-permute-start | bytes 4718600 | tf_op jit(solution)/shard_map/ppermute | solution.py:304
  60.0 70.0 %collective-permute-start.9 = (bf16[768,1024]{1,0:T(8,128)(2,1)S(1)}, bf16[768,1024]{1,0:T(8,128)(2,1)S(1)}, u32[]{:S(2)}, u32[]{:S(2)}) collective-permute-start(bf16[768,1024]{1,0:T(8,128)(2,1)S(1)} %shard_map.94.rest_5_), channel_id=1, source_target_pairs={{2,1},{3,2},{6,5},{7,6},{10,9},{11,10},{14,13},{15,14},{18,17},{19... | collective-permute-start | bytes 4718600 | tf_op jit(solution)/shard_map/ppermute | solution.py:305
  80.5 39.0 %collective-permute-start.4 = (bf16[768,64]{1,0:T(8,128)(2,1)S(1)}, bf16[768,64]{1,0:T(8,128)(2,1)S(1)}, u32[]{:S(2)}, u32[]{:S(2)}) collective-permute-start(bf16[768,64]{1,0:T(8,128)(2,1)S(1)} %get-tuple-element.13.rest_1_.mine_ref), channel_id=1, source_target_pairs={{0,1},{1,0},{2,3},{3,2},{4,5},{5,4},{6,7},{7,6},{8,9},{9,8},{10,11... | collective-permute-start | bytes 294920 | tf_op jit(solution)/shard_map/ppermute | solution.py:366
  86.9 66.3 %collective-permute-start.8 = (bf16[768,1024]{1,0:T(8,128)(2,1)S(1)}, bf16[768,1024]{1,0:T(8,128)(2,1)S(1)}, u32[]{:S(2)}, u32[]{:S(2)}) collective-permute-start(bf16[768,1024]{1,0:T(8,128)(2,1)S(1)} %shard_map.96.after_ref), channel_id=1, source_target_pairs={{0,1},{1,2},{4,5},{5,6},{8,9},{9,10},{12,13},{13,14},{16,17},{17,1... | collective-permute-start | bytes 4718600 | tf_op jit(solution)/shard_map/ppermute | solution.py:304
  91.4 71.6 %collective-permute-start.7 = (bf16[768,1024]{1,0:T(8,128)(2,1)S(1)}, bf16[768,1024]{1,0:T(8,128)(2,1)S(1)}, u32[]{:S(2)}, u32[]{:S(2)}) collective-permute-start(bf16[768,1024]{1,0:T(8,128)(2,1)S(1)} %shard_map.96.after_ref), channel_id=1, source_target_pairs={{2,1},{3,2},{6,5},{7,6},{10,9},{11,10},{14,13},{15,14},{18,17},{19... | collective-permute-start | bytes 4718600 | tf_op jit(solution)/shard_map/ppermute | solution.py:305
  119.6 50.1 %collective-permute-start.6 = (bf16[768,64]{1,0:T(8,128)(2,1)S(1)}, bf16[768,64]{1,0:T(8,128)(2,1)S(1)}, u32[]{:S(2)}, u32[]{:S(2)}) collective-permute-start(bf16[768,64]{1,0:T(8,128)(2,1)S(1)} %shard_map.97.rest_1_.mine_ref), channel_id=1, source_target_pairs={{0,2},{1,3},{2,0},{3,1},{4,6},{5,7},{6,4},{7,5},{8,10},{9,11},{10,... | collective-permute-start | bytes 294920 | tf_op jit(solution)/shard_map/ppermute | solution.py:366
  128.4 62.7 %collective-permute-start.13 = (bf16[768,1024]{1,0:T(8,128)(2,1)S(1)}, bf16[768,1024]{1,0:T(8,128)(2,1)S(1)}, u32[]{:S(2)}, u32[]{:S(2)}) collective-permute-start(bf16[768,1024]{1,0:T(8,128)(2,1)S(1)} %shard_map.98.rest_1_), channel_id=1, source_target_pairs={{0,1},{1,2},{2,3},{4,5},{5,6},{6,7},{8,9},{9,10},{10,11},{12,13},{... | collective-permute-start | bytes 4718600 | tf_op jit(solution)/shard_map/ppermute | solution.py:308
  135.3 55.8 %collective-permute-start.14 = (bf16[768,1024]{1,0:T(8,128)(2,1)S(1)}, bf16[768,1024]{1,0:T(8,128)(2,1)S(1)}, u32[]{:S(2)}, u32[]{:S(2)}) collective-permute-start(bf16[768,1024]{1,0:T(8,128)(2,1)S(1)} %shard_map.99.rest_1_), channel_id=1, source_target_pairs={{1,0},{2,1},{3,2},{5,4},{6,5},{7,6},{9,8},{10,9},{11,10},{13,12},{... | collective-permute-start | bytes 4718600 | tf_op jit(solution)/shard_map/ppermute | solution.py:311
  158.5 65.2 %collective-permute-start.11 = (bf16[768,1024]{1,0:T(8,128)(2,1)S(1)}, bf16[768,1024]{1,0:T(8,128)(2,1)S(1)}, u32[]{:S(2)}, u32[]{:S(2)}) collective-permute-start(bf16[768,1024]{1,0:T(8,128)(2,1)S(1)} %shard_map.100.rest_1_), channel_id=1, source_target_pairs={{0,1},{1,2},{2,3},{4,5},{5,6},{6,7},{8,9},{9,10},{10,11},{12,13},{... | collective-permute-start | bytes 4718600 | tf_op jit(solution)/shard_map/ppermute | solution.py:308
  168.3 36.3 %collective-permute-start.12 = (bf16[768,1024]{1,0:T(8,128)(2,1)S(1)}, bf16[768,1024]{1,0:T(8,128)(2,1)S(1)}, u32[]{:S(2)}, u32[]{:S(2)}) collective-permute-start(bf16[768,1024]{1,0:T(8,128)(2,1)S(1)} %shard_map.101.after_ref), channel_id=1, source_target_pairs={{1,0},{2,1},{3,2},{5,4},{6,5},{7,6},{9,8},{10,9},{11,10},{13,12},{... | collective-permute-start | bytes 4718600 | tf_op jit(solution)/shard_map/ppermute | solution.py:311

commit v2 on v1

--- a/solution.py
+++ b/solution.py
@@ -7,10 +7,11 @@
 from jax.experimental.pallas import tpu as pltpu
 from jax.sharding import PartitionSpec as P
 
-SHARES = (1, 1)
 CAP = 2
+FIRST = 1
 VMEM = 28 * 1024 * 1024
-SCALE = 4.0
+FIRST_VMEM = 60 * 1024 * 1024
+SCALE = 3.0
 
 
 def cost(flops, elements):
@@ -19,40 +20,45 @@
     )
 
 
-def params():
-    return pltpu.CompilerParams(vmem_limit_bytes=VMEM)
+def params(vmem=VMEM):
+    return pltpu.CompilerParams(vmem_limit_bytes=vmem)
 
 
 ORDER = pl.BlockSpec(memory_space=pl.ANY)
 
 
-def term_kernel(sums, block_ref, a_ref, w_ref, *rest):
-    came, out_ref = rest[:sums], rest[-1]
+def term_kernel(ranges, place_ref, a_ref, w_ref, *rest):
+    out_ref = rest[-1]
+    j = pl.program_id(0)
     total = jnp.dot(a_ref[...], w_ref[...], preferred_element_type=jnp.float32)
-    for ref in came:
-        total = total + ref[...].astype(jnp.float32)
+    for n, (low, count) in enumerate(ranges):
+        counts = (place_ref[1 + n] > 0) & (j >= low) & (j < low + count)
+        total += jnp.where(counts, rest[n][...].astype(jnp.float32), 0.0)
     out_ref[...] = total.astype(out_ref.dtype)
 
 
 def tile_of(width):
-    return min(512, width // sum(SHARES))
-
-
-def spans(width):
-    tile = tile_of(width)
-    found, start = [], 0
-    for share in SHARES:
-        tiles = share * (width // sum(SHARES)) // tile
-        found.append((start, tiles))
-        start += tiles
-    return found
+    return max(128, width // 8)
+
+
+def spans(width, first):
+    tiles = width // tile_of(width)
+    half = tiles // 2
+    shares = [half, tiles - half] if half else [tiles]
+    if first and half > 2:
+        shares = [FIRST, half - FIRST, tiles - half]
+    return [(sum(shares[:n]), share) for n, share in enumerate(shares)]
 
 
 def term(attn, weight, first_tile, tile, tiles, came, after):
     rows, depth = attn.shape
-    piece = pl.BlockSpec((rows, tile), lambda j, b: (0, j))
-    return pl.pallas_call(
-        functools.partial(term_kernel, len(came)),
+    ranges = [(low, ref.shape[1] // tile) for ref, _, low in came]
+
+    def part_spec(low, count):
+        return pl.BlockSpec((rows, tile), lambda j, b: (0, jnp.clip(j - low, 0, count - 1)))
+
+    return pl.pallas_call(
+        functools.partial(term_kernel, ranges),
         grid_spec=pltpu.PrefetchScalarGridSpec(
             num_scalar_prefetch=1,
             grid=(tiles,),
@@ -60,14 +66,70 @@
                 pl.BlockSpec(memory_space=pltpu.VMEM),
                 pl.BlockSpec((depth, tile), lambda j, b: (0, b[0] + j)),
             ]
-            + [piece] * len(came)
-            + [ORDER] * len(after),
-            out_specs=piece,
+            + [part_spec(*span) for span in ranges]
+            + [ORDER],
+            out_specs=pl.BlockSpec((rows, tile), lambda j, b: (0, j)),
         ),
         out_shape=jax.ShapeDtypeStruct((rows, tiles * tile), jnp.bfloat16),
         compiler_params=params(),
         cost_estimate=cost(2 * rows * depth * tiles * tile, depth * tiles * tile),
-    )(first_tile.reshape(1).astype(jnp.int32), attn, weight, *came, *after)
+    )(
+        jnp.stack([first_tile, *[flag for _, flag, _ in came]]).astype(jnp.int32),
+        attn,
+        weight,
+        *[ref for ref, _, _ in came],
+        after,
+    )
+
+
+def first_kernel(tile, tiles, place_ref, a_hbm, w_hbm, out_ref, a, w, sems):
+    parts, _, step = a.shape
+    column = pl.multiple_of(place_ref[0] * tile, tile)
+    copies = []
+    for k in range(parts):
+        copies.append(
+            (
+                pltpu.make_async_copy(a_hbm.at[:, pl.ds(k * step, step)], a.at[k], sems.at[0, k]),
+                pltpu.make_async_copy(
+                    w_hbm.at[pl.ds(k * step, step), pl.ds(column, tiles * tile)],
+                    w.at[k],
+                    sems.at[1, k],
+                ),
+            )
+        )
+    for of_a, of_w in copies:
+        of_w.start()
+        of_a.start()
+    total = None
+    for k, (of_a, of_w) in enumerate(copies):
+        of_w.wait()
+        of_a.wait()
+        share = jnp.dot(a[k], w[k], preferred_element_type=jnp.float32)
+        total = share if total is None else total + share
+    out_ref[...] = total.astype(out_ref.dtype)
+
+
+def first_term(attn, weight, first_tile, tile, tiles):
+    rows, depth = attn.shape
+    step = min(depth, 512)
+    parts = depth // step
+    return pl.pallas_call(
+        functools.partial(first_kernel, tile, tiles),
+        in_specs=[
+            pl.BlockSpec(memory_space=pltpu.SMEM),
+            pl.BlockSpec(memory_space=pltpu.HBM),
+            pl.BlockSpec(memory_space=pltpu.HBM),
+        ],
+        out_specs=pl.BlockSpec(memory_space=pltpu.VMEM),
+        out_shape=jax.ShapeDtypeStruct((rows, tiles * tile), jnp.bfloat16),
+        scratch_shapes=[
+            pltpu.VMEM((parts, rows, step), attn.dtype),
+            pltpu.VMEM((parts, step, tiles * tile), weight.dtype),
+            pltpu.SemaphoreType.DMA((2, parts)),
+        ],
+        compiler_params=params(FIRST_VMEM),
+        cost_estimate=cost(2 * rows * depth * tiles * tile, depth * tiles * tile),
+    )(first_tile.reshape(1).astype(jnp.int32), attn, weight)
 
 
 def exchange(size, hop):
@@ -169,22 +231,23 @@
     )(kind, index, ids, attn, wanted, *sources, after)
 
 
-def join_kernel(mine_ref, theirs_ref, after_ref, out_ref):
+def join_kernel(keep_ref, mine_ref, theirs_ref, after_ref, out_ref):
     out_ref[...] = (
-        mine_ref[...].astype(jnp.float32) + theirs_ref[...].astype(jnp.float32)
+        jnp.where(keep_ref[0] > 0, mine_ref[...].astype(jnp.float32), 0.0)
+        + theirs_ref[...].astype(jnp.float32)
     ).astype(out_ref.dtype)
 
 
-def join(mine, theirs, after):
+def join(keep, mine, theirs, after):
     whole = pl.BlockSpec(mine.shape, lambda: (0, 0))
     return pl.pallas_call(
         join_kernel,
-        in_specs=[whole, whole, ORDER],
+        in_specs=[pl.BlockSpec(memory_space=pltpu.SMEM), whole, whole, ORDER],
         out_specs=whole,
         out_shape=jax.ShapeDtypeStruct(mine.shape, mine.dtype),
         compiler_params=params(),
         cost_estimate=cost(0, 3 * mine.size),
-    )(mine, theirs, after)
+    )(jnp.reshape(keep, (1,)).astype(jnp.int32), mine, theirs, after)
 
 
 def own_kernel(block_ref, id_ref, a_ref, w_ref, chosen_ref, wanted_ref, expand_ref, after_ref, out_ref, masked):
@@ -205,8 +268,8 @@
 def own_term(attn, weight, block, chosen, wanted, ids, expand, after):
     rows, depth = attn.shape
     ranks, width = expand.shape
-    tile = tile_of(width)
-    tiles = width // tile
+    tile = width // 4
+    tiles = 4
     return pl.pallas_call(
         own_kernel,
         grid_spec=pltpu.PrefetchScalarGridSpec(
@@ -229,29 +292,30 @@
     )(block.reshape(1).astype(jnp.int32), ids, attn, weight, chosen, wanted, expand, after)
 
 
-def finish_kernel(own_ref, right_ref, left_ref, *rest):
+def finish_kernel(sums, own_ref, *rest):
     out_ref = rest[-1]
-    out_ref[...] = (
-        own_ref[...] + (right_ref[...].astype(jnp.float32) + left_ref[...].astype(jnp.float32))
-    ).astype(out_ref.dtype)
-
-
-def finish(own, right, left, first_tile, so_far):
+    total = own_ref[...]
+    for ref in rest[:sums]:
+        total += ref[...].astype(jnp.float32)
+    out_ref[...] = total.astype(out_ref.dtype)
+
+
+def finish(own, sums, first_column, so_far):
     rows, width = own.shape
-    tile = tile_of(width)
-    here = pl.BlockSpec((rows, tile), lambda j: (0, first_tile + j))
+    tile = tile_of(width) * 2
+    here = pl.BlockSpec((rows, tile), lambda j: (0, first_column // tile + j))
     came = pl.BlockSpec((rows, tile), lambda j: (0, j))
     extra = [] if so_far is None else [so_far]
     return pl.pallas_call(
-        finish_kernel,
-        grid=(right.shape[1] // tile,),
-        in_specs=[here, came, came] + [pl.BlockSpec(memory_space=pl.ANY)] * len(extra),
+        functools.partial(finish_kernel, len(sums)),
+        grid=(sums[0].shape[1] // tile,),
+        in_specs=[here] + [came] * len(sums) + [pl.BlockSpec(memory_space=pl.ANY)] * len(extra),
         out_specs=here,
         out_shape=jax.ShapeDtypeStruct((rows, width), jnp.bfloat16),
-        input_output_aliases={3: 0} if extra else {},
+        input_output_aliases={1 + len(sums): 0} if extra else {},
         compiler_params=params(),
-        cost_estimate=cost(0, 5 * rows * right.shape[1]),
-    )(own, right, left, *extra)
+        cost_estimate=cost(0, 5 * rows * sums[0].shape[1]),
+    )(own, *sums, *extra)
 
 
 def make_local(replicas, tensor):
@@ -270,49 +334,58 @@
         own = lax.axis_index("replica")
         width = out_weight.shape[1] // tensor
         tile = tile_of(width)
-        pieces = spans(width)
         slots = resident_factors.shape[0]
         store_rows = store_factors.shape[0]
         evict = evict_slots[0]
-        to_right = [(d, d + 1) for d in range(tensor - 1)]
-        to_left = [(d + 1, d) for d in range(tensor - 1)]
-
-        def product(block, piece, came, after):
-            start, tiles = pieces[piece]
+        even, odd = z % 2 == 0, z % 2 == 1
+        not_first, not_last = z > 0, z < tensor - 1
+
+        def edges(step, first):
+            pairs = []
+            for d in range(first, tensor - 1, 2):
+                pairs += [(d, d + 1)] * (d <= step)
+                pairs += [(d + 1, d)] * (d + 1 >= tensor - 1 - step)
+            return pairs
+
+        def swap(pairs):
+            return pairs + [(b, a) for a, b in pairs if (b, a) not in pairs]
+
+        def product(block, span, came_a, flag_a, came_b, flag_b, after):
+            start, tiles = span
             first = jnp.clip(block, 0, tensor - 1) * (width // tile) + start
-            return term(attn_out, out_weight, first, tile, tiles, came, [] if after is attn_out else [after])
-
-        def step_of(step, came_right, came_left, after, between):
-            right_pairs = to_right[: step + 1]
-            left_pairs = to_left[tensor - 2 - step :]
+            if after is None:
+                return first_term(attn_out, out_weight, first, tile, tiles)
+            came = []
+            for sums, flag in ((came_a, flag_a), (came_b, flag_b)):
+                for (low, count), ref in sums:
+                    if low < start + tiles and start < low + count:
+                        came.append((ref, flag, low - start))
+            return term(attn_out, out_weight, first, tile, tiles, came, after)
+
+        def step_of(step, came_x, came_y, after, between):
             right_block = tensor - 1 - step + z
             left_block = z + step + 1 - tensor
-            rights, lefts = [], []
-            for piece in range(len(pieces)):
-                right_in = [] if came_right is None else [came_right[piece]]
-                left_in = [] if came_left is None else [came_left[piece]]
+            pairs_x, pairs_y = edges(step, 0), edges(step, 1)
+            xs, ys = [], []
+            for span in spans(width, step == 0):
                 if 2 * step < tensor - 1:
-                    block = jnp.where(2 * z < tensor, right_block, left_block)
-                    same = right_in and right_in[0] is left_in[0]
-                    out = product(block, piece, right_in + ([] if same else left_in), after)
-                    after = out
-                    if 2 * step + 3 < tensor:
-                        moved = lax.ppermute(out, "tensor", right_pairs + left_pairs)
-                        rights.append(moved)
-                        lefts.append(moved)
-                    else:
-                        rights.append(lax.ppermute(out, "tensor", right_pairs))
-                        lefts.append(lax.ppermute(out, "tensor", left_pairs))
+                    goes_right = 2 * z < tensor
+                    block = jnp.where(goes_right, right_block, left_block)
+                    flag_x = jnp.where(goes_right, odd, even & not_last)
+                    flag_y = jnp.where(goes_right, even & not_first, odd & not_last)
+                    for_x = for_y = product(block, span, came_x, flag_x, came_y, flag_y, after)
                 else:
-                    out = product(right_block, piece, right_in, after)
-                    rights.append(lax.ppermute(out, "tensor", right_pairs))
-                    after = out
-                    out = product(left_block, piece, left_in, after)
-                    lefts.append(lax.ppermute(out, "tensor", left_pairs))
-                    after = out
-                if piece < len(pieces) - 1 or step == 0:
-                    after = between(after)
-            return rights, lefts, after
+                    flag = jnp.where(even, not_first, not_last)
+                    block = jnp.where(even, right_block, left_block)
+                    for_x = product(block, span, [], flag, came_y, flag, after)
+                    block = jnp.where(even, left_block, right_block)
+                    for_y = product(block, span, came_x, flag, [], flag, for_x)
+                pairs = pairs_x if step or xs else swap(pairs_x)
+                xs.append((span, lax.ppermute(for_x, "tensor", pairs)))
+                if pairs_y:
+                    ys.append((span, lax.ppermute(for_y, "tensor", pairs_y)))
+                after = between(step, len(xs) - 1, for_y)
+            return xs, ys, after
 
         matches = incoming[:, :, None] == jnp.arange(store_place.shape[0], dtype=jnp.int32)
         place = jnp.sum(jnp.where(matches, store_place, 0), axis=2)
@@ -350,7 +423,13 @@
         ).astype(jnp.int32)
         wanted = req_adapter[:, None]
         sources = [resident_factors, store_factors]
-        state = {"mine": None, "bit": 1, "theirs": None}
+        if tensor == 4:
+            inner = (z == 1) | (z == 2)
+            rounds = [(edges(0, 0), True), ([(1, 2), (2, 1)], True), ([(1, 0), (2, 3)], inner)]
+        else:
+            bits = [1 << n for n in range(tensor.bit_length() - 1)]
+            rounds = [(exchange(tensor, bit)[0], True) for bit in bits]
+        state = {"mine": None, "theirs": None, "keep": None}
 
         def fetch(after):
             if not send_rows:
@@ -361,8 +440,9 @@
             return picked[0]
 
         def send_mine():
-            if state["bit"] < tensor:
-                pairs, _ = exchange(tensor, state["bit"])
+            state["theirs"] = None
+            if rounds:
+                pairs, state["keep"] = rounds.pop(0)
                 state["theirs"] = lax.ppermute(state["mine"], "tensor", pairs)
 
         def shrink(after):
@@ -378,34 +458,22 @@
         def add_theirs(after):
             if state["theirs"] is None:
                 return after
-            state["mine"] = join(state["mine"], state["theirs"], after)
-            state["bit"] *= 2
-            state["theirs"] = None
+            state["mine"] = join(jnp.asarray(state["keep"]), state["mine"], state["theirs"], after)
             send_mine()
             return state["mine"]
 
-        def after_pieces(step):
-            if step == 0:
-                calls = [None] * (len(pieces) - 1) + [fetch]
-            elif step == 1:
-                calls = [shrink] + [None] * len(pieces)
-            else:
-                calls = [None] * len(pieces)
-            todo = iter(calls)
-
-            def between(after):
-                call = next(todo)
-                return after if call is None else call(after)
-
-            return between
-
-        rights, lefts, last = None, None, attn_out
+        def between(step, piece, after):
+            if step == 0 and piece == len(spans(width, True)) - 1:
+                return fetch(after)
+            if step == 1 and piece == 0:
+                return shrink(after)
+            return add_theirs(after)
+
+        came_x, came_y, last = [], [], None
         for step in range(tensor - 1):
-            if step > 1:
-                last = add_theirs(last)
-            rights, lefts, last = step_of(step, rights, lefts, last, after_pieces(step))
+            came_x, came_y, last = step_of(step, came_x, came_y, last, between)
         if tensor < 3:
-            last = shrink(fetch(last) if tensor == 1 else last)
+            last = shrink(last)
         while state["theirs"] is not None:
             last = add_theirs(last)
         total = own_term(
@@ -418,11 +486,10 @@
             state["expand"].reshape(-1, width),
             last,
         )
-        if tensor == 1:
-            return total.astype(jnp.bfloat16)
         out = None
-        for piece, (start, _) in enumerate(pieces):
-            out = finish(total, rights[piece], lefts[piece], start, out)
+        for span in spans(width, False):
+            sums = [ref for at, ref in came_x + came_y if at == span]
+            out = finish(total, sums, span[0] * tile, out)
         return out
 
     return local

time: 226 us -> 218 us (0.965)
  waiting for transfers between devices: 112 us -> 91.8 us
  Pallas kernels: 68.3 us -> 77.5 us
  other arithmetic: 3.47 us -> 6.35 us
    ppermute x10 -> x11, waiting for transfers between devices: 70.8 us -> 34.8 us  [the longest x7 34.8 us: step_of(): xs.append((span, lax.ppermute(for_x, 'tensor', pairs)))]
    ppermute x3, waiting for transfers between devices: 13.8 us -> 27.3 us  [fetch(): sources.insert(2, lax.ppermute(piece, 'replica', pairs))]
    pallas_call x12 -> x14, Pallas kernels: 47.3 us -> 58 us  [the longest x8 49.7 us: term(): pl.pallas_call(functools.partial(term_kernel, ranges), grid_spec=pltpu.Pr...]
    ppermute x2 -> x3, waiting for transfers between devices: 27.3 us -> 29.7 us  [send_mine(): state['theirs'] = lax.ppermute(state['mine'], 'tensor', pairs)]
    unnamed x18 -> x22, local copies, waits for them, and re-layouts: 7.88 us -> 5.91 us
    ppermute x10 -> x11, starting transfers between devices: 26.8 us -> 25.9 us  [the longest x7 22.9 us: step_of(): xs.append((span, lax.ppermute(for_x, 'tensor', pairs)))]
  transfers between devices with their start and end apart: 15 -> 17, of which waited for: 8 -> 8; matrix products, arithmetic and copies ran while one was open for 2% -> 4% of each run, Pallas kernels for 27% -> 33%
where the time goes in v2:
time: 218 us; the launch traced here: 216 us
  waiting for transfers between devices  91.8 us (42%)
  Pallas kernels  77.5 us (36%)
  starting transfers between devices  31.5 us (14%)
  local copies, waits for them, and re-layouts  8.5 us (4%)
  other arithmetic  6.35 us (3%)
    pallas_call x8, Pallas kernels, term(): pl.pallas_call(functools.partial(term_kernel, ranges), grid_spec=pltpu.Pr...  49.7 us
    ppermute x7, waiting for transfers between devices, step_of(): xs.append((span, lax.ppermute(for_x, 'tensor', pairs)))  34.8 us
    ppermute x3, waiting for transfers between devices, send_mine(): state['theirs'] = lax.ppermute(state['mine'], 'tensor', pairs)  29.7 us
    ppermute x3, waiting for transfers between devices, fetch(): sources.insert(2, lax.ppermute(piece, 'replica', pairs))  27.3 us
    ppermute x7, starting transfers between devices, step_of(): xs.append((span, lax.ppermute(for_x, 'tensor', pairs)))  22.9 us
    pallas_call x1, Pallas kernels, own_term(): pl.pallas_call(own_kernel, grid_spec=pltpu.PrefetchScalarGridSpec(num_sca...  12.7 us
    unnamed x22, local copies, waits for them, and re-layouts  5.91 us
    pallas_call x1, Pallas kernels, hold_slots(): pl.pallas_call(functools.partial(slots_kernel, len(sources)), grid_spec=p...  4.8 us
  transfers between devices with their start and end apart: 17, of which 8 were waited for; matrix products, arithmetic and copies ran while one was open for 4% of the time, Pallas kernels for 33%

profile of v2, /device:TPU:0, one launch (start us, length us, event | category | flops | bytes accessed | tf_op | source)
XLA Modules:
  0.0 216.0 jit_solution(15309694743253725158)
XLA Ops:
  0.0 4.5 %shard_map.91.rest_0_ = bf16[768,256]{1,0:T(8,128)(2,1)} custom-call(s32[1]{0:T(128)} %bitcast.9.place_ref, bf16[768,2048]{1,0:T(8,128)(2,1)} %a_ref.19, bf16[2048,8192]{1,0:T(8,128)(2,1)} %w_ref.17), custom_call_target="tpu_custom_call" | custom-call | flops 2415919104 | bytes 3145728 | tf_op jit(solution)/shard_map/pallas_call | solution.py:116
  4.5 3.1 %collective-permute-start.3 = (bf16[768,256]{1,0:T(8,128)(2,1)}, bf16[768,256]{1,0:T(8,128)(2,1)S(1)}, u32[]{:S(2)}, u32[]{:S(2)}) collective-permute-start(bf16[768,256]{1,0:T(8,128)(2,1)} %shard_map.91.rest_0_), channel_id=1, source_target_pairs={{0,1},{3,2},{1,0},{2,3},{4,5},{7,6},{5,4},{6,7},{8,9},{11,10},{9,8... | collective-permute-start | bytes 1179656 | tf_op jit(solution)/shard_map/ppermute | solution.py:384
  7.6 1.0 copy-done.3
  8.6 5.4 %shard_map.92.rest_0_ = bf16[768,768]{1,0:T(8,128)(2,1)} custom-call(s32[1]{0:T(128)} %bitcast.8.place_ref, bf16[768,2048]{1,0:T(8,128)(2,1)S(1)} %copy-done, bf16[2048,8192]{1,0:T(8,128)(2,1)} %w_ref.17, bf16[768,256]{1,0:T(8,128)(2,1)S(1)} %copy-done.3), custom_call_target="tpu_custom_call" | custom-call | flops 7247757312 | bytes 9437184 | tf_op jit(solution)/shard_map/pallas_call | solution.py:60
  14.0 2.9 %collective-permute-start.4 = (bf16[768,768]{1,0:T(8,128)(2,1)}, bf16[768,768]{1,0:T(8,128)(2,1)}, u32[]{:S(2)}, u32[]{:S(2)}) collective-permute-start(bf16[768,768]{1,0:T(8,128)(2,1)} %shard_map.92.rest_0_), channel_id=1, source_target_pairs={{0,1},{3,2},{4,5},{7,6},{8,9},{11,10},{12,13},{15,14},{16,17},{19,... | collective-permute-start | bytes 3538952 | tf_op jit(solution)/shard_map/ppermute | solution.py:384
  16.9 6.4 %shard_map.93.refs_3_ = bf16[768,1024]{1,0:T(8,128)(2,1)} custom-call(s32[1]{0:T(128)} %bitcast.7.place_ref, bf16[768,2048]{1,0:T(8,128)(2,1)S(1)} %copy-done, bf16[2048,8192]{1,0:T(8,128)(2,1)} %w_ref.17, bf16[768,768]{1,0:T(8,128)(2,1)} %shard_map.92.rest_0_), custom_call_target="tpu_custom_call" | custom-call | flops 9663676416 | bytes 12582912 | tf_op jit(solution)/shard_map/pallas_call | solution.py:60
  23.3 2.4 %collective-permute-start.6 = (bf16[768,1024]{1,0:T(8,128)(2,1)}, bf16[768,1024]{1,0:T(8,128)(2,1)}, u32[]{:S(2)}, u32[]{:S(2)}) collective-permute-start(bf16[768,1024]{1,0:T(8,128)(2,1)} %shard_map.93.refs_3_), channel_id=1, source_target_pairs={{0,1},{3,2},{4,5},{7,6},{8,9},{11,10},{12,13},{15,14},{16,17},{19,... | collective-permute-start | bytes 4718600 | tf_op jit(solution)/shard_map/ppermute | solution.py:384
  25.8 0.2 select_reduce_fusion
  26.0 0.6 broadcast_compare_fusion
  26.6 0.9 convert_reduce_fusion
  27.5 0.8 select_reduce_fusion.1
  28.3 0.2 fusion.3
  28.5 0.1 pad_add_fusion.row_ref
  28.6 2.2 %copy-done.1 = bf16[8,2,64,2048]{3,2,1,0:T(8,128)(2,1)S(1)} copy-done((bf16[8,2,64,2048]{3,2,1,0:T(8,128)(2,1)S(1)}, bf16[8,2,64,2048]{3,2,1,0:T(8,128)(2,1)}, u32[]{:S(2)}) %copy-start.1) | copy-done | bytes 4194328
  30.8 2.0 shard_map.94
  32.8 1.0 copy-done.4
  33.8 1.9 collective-permute-start.1
  35.8 0.6 fusion.8
  36.3 0.7 fusion.6
  37.0 0.9 broadcast_in_dim.86.wanted_ref
  37.9 0.7 fusion.1
  38.7 0.7 select_reduce_fusion.2
  39.4 0.7 compare_select_fusion
  40.1 0.6 compare_select_fusion.1
  40.7 0.8 concatenate.6.index_ref
  41.4 0.1 pad_add_fusion.1.place_ref
  41.5 0.1 pad_add_fusion.2.place_ref
  41.6 0.1 pad_add_fusion.3.place_ref
  41.7 0.1 pad_add_fusion.5.place_ref
  41.7 0.2 collective-permute-start
  42.0 0.6 collective-permute-done.4.rest_1_
  42.6 1.6 copy-done.5
  44.2 6.6 %shard_map.95.rest_5_ = bf16[768,1024]{1,0:T(8,128)(2,1)S(1)} custom-call(s32[3]{0:T(128)S(1)} %pad_add_fusion.1.place_ref, bf16[768,2048]{1,0:T(8,128)(2,1)S(1)} %copy-done, bf16[2048,8192]{1,0:T(8,128)(2,1)} %w_ref.17, bf16[768,256]{1,0:T(8,128)(2,1)S(1)} %collective-permute-done.3.rest_0_, bf16[768,768]{1,0:T(8,128)(2,1)} %collective-permute-done.4.rest_1_, ...), custom_call_target="tpu_custom_call" | custom-call | flops 9663676416 | bytes 12582912 | tf_op jit(solution)/shard_map/pallas_call | solution.py:60
  50.8 0.8 collective-permute-start.9
  51.6 0.1 pad_add_fusion.4.place_ref
  51.7 0.1 pad_add_fusion.6.place_ref
  51.7 8.5 %collective-permute-done.1.rest_3_ = bf16[2,2,64,2048]{3,2,1,0:T(8,128)(2,1)} collective-permute-done((bf16[2,2,64,2048]{3,2,1,0:T(8,128)(2,1)}, bf16[2,2,64,2048]{3,2,1,0:T(8,128)(2,1)}, u32[]{:S(2)}, u32[]{:S(2)}) %collective-permute-start.1) | collective-permute-done | bytes 1048608 | tf_op jit(solution)/shard_map/ppermute | solution.py:439
  60.2 1.4 collective-permute-start.8
  61.6 18.8 %collective-permute-done.2.rest_4_ = bf16[2,2,64,2048]{3,2,1,0:T(8,128)(2,1)} collective-permute-done((bf16[2,2,64,2048]{3,2,1,0:T(8,128)(2,1)}, bf16[2,2,64,2048]{3,2,1,0:T(8,128)(2,1)}, u32[]{:S(2)}, u32[]{:S(2)}) %collective-permute-start.2) | collective-permute-done | bytes 1048608 | tf_op jit(solution)/shard_map/ppermute | solution.py:439
  80.4 4.8 %shard_map.96 = (bf16[768,64]{1,0:T(8,128)(2,1)S(1)}, bf16[8,64,2048]{2,1,0:T(8,128)(2,1)S(1)}) custom-call(s32[8]{0:T(128)S(1)} %get-tuple-element.25.kind_ref, s32[40]{0:T(128)S(1)} %concatenate.6.index_ref, s32[8]{0:T(128)S(1)} %get-tuple-element.32.id_ref, bf16[768,2048]{1,0:T(8,128)(2,1)S(1)} %copy-done, s32[768,1]{1,0:T(8,128)S(1)} %copy-done.6, ...), custom_call_target="tpu_custom_call" | custom-call | flops 4831838208 | bytes 18874368 | tf_op jit(solution)/shard_map/pallas_call | solution.py:208
  85.2 1.3 collective-permute-start.5
  86.5 6.4 %shard_map.97.after_ref = bf16[768,1024]{1,0:T(8,128)(2,1)S(1)} custom-call(s32[2]{0:T(128)S(1)} %pad_add_fusion.2.place_ref, bf16[768,2048]{1,0:T(8,128)(2,1)S(1)} %copy-done, bf16[2048,8192]{1,0:T(8,128)(2,1)} %w_ref.17, bf16[768,1024]{1,0:T(8,128)(2,1)} %collective-permute-done.6.rest_0_, bf16[768,64]{1,0:T(8,128)(2,1)S(1)} %get-tuple-element.13.rest_1_.mine_ref), custom_call_target="tpu_custom_call" | custom-call | flops 9663676416 | bytes 12582912 | tf_op jit(solution)/shard_map/pallas_call | solution.py:60
  92.9 0.8 collective-permute-start.12
  93.7 3.4 %collective-permute-start.11 = (bf16[768,1024]{1,0:T(8,128)(2,1)S(1)}, bf16[768,1024]{1,0:T(8,128)(2,1)S(1)}, u32[]{:S(2)}, u32[]{:S(2)}) collective-permute-start(bf16[768,1024]{1,0:T(8,128)(2,1)S(1)} %shard_map.97.after_ref), channel_id=1, source_target_pairs={{0,1},{3,2},{4,5},{7,6},{8,9},{11,10},{12,13},{15,14},{16,17},{19,... | collective-permute-start | bytes 4718600 | tf_op jit(solution)/shard_map/ppermute | solution.py:384
  97.1 17.0 %collective-permute-done.5.theirs_ref = bf16[768,64]{1,0:T(8,128)(2,1)S(1)} collective-permute-done((bf16[768,64]{1,0:T(8,128)(2,1)S(1)}, bf16[768,64]{1,0:T(8,128)(2,1)S(1)}, u32[]{:S(2)}, u32[]{:S(2)}) %collective-permute-start.5) | collective-permute-done | bytes 98336 | tf_op jit(solution)/shard_map/ppermute | solution.py:446
  114.1 0.1 shard_map.98.rest_1_.mine_ref
  114.2 0.7 collective-permute-start.7
  114.8 6.2 %shard_map.99.rest_1_ = bf16[768,1024]{1,0:T(8,128)(2,1)S(1)} custom-call(s32[2]{0:T(128)S(1)} %pad_add_fusion.4.place_ref, bf16[768,2048]{1,0:T(8,128)(2,1)S(1)} %copy-done, bf16[2048,8192]{1,0:T(8,128)(2,1)} %w_ref.17, bf16[768,1024]{1,0:T(8,128)(2,1)S(1)} %collective-permute-done.9.rest_0_, bf16[768,64]{1,0:T(8,128)(2,1)S(1)} %shard_map.98.rest_1_.mine_ref), custom_call_target="tpu_custom_call" | custom-call | flops 9663676416 | bytes 12582912 | tf_op jit(solution)/shard_map/pallas_call | solution.py:60
  121.1 7.0 %collective-permute-start.15 = (bf16[768,1024]{1,0:T(8,128)(2,1)S(1)}, bf16[768,1024]{1,0:T(8,128)(2,1)S(1)}, u32[]{:S(2)}, u32[]{:S(2)}) collective-permute-start(bf16[768,1024]{1,0:T(8,128)(2,1)S(1)} %shard_map.99.rest_1_), channel_id=1, source_target_pairs={{0,1},{1,0},{2,3},{3,2},{4,5},{5,4},{6,7},{7,6},{8,9},{9,8},{10,11... | collective-permute-start | bytes 4718600 | tf_op jit(solution)/shard_map/ppermute | solution.py:384
  128.0 6.2 %shard_map.100.after_ref = bf16[768,1024]{1,0:T(8,128)(2,1)S(1)} custom-call(s32[2]{0:T(128)S(1)} %pad_add_fusion.3.place_ref, bf16[768,2048]{1,0:T(8,128)(2,1)S(1)} %copy-done, bf16[2048,8192]{1,0:T(8,128)(2,1)} %w_ref.17, bf16[768,1024]{1,0:T(8,128)(2,1)S(1)} %collective-permute-done.8.rest_0_, bf16[768,1024]{1,0:T(8,128)(2,1)S(1)} %shard_map.99.rest_1_), custom_call_target="tpu_custom_call" | custom-call | flops 9663676416 | bytes 12582912 | tf_op jit(solution)/shard_map/pallas_call | solution.py:60
  134.3 0.8 collective-permute-start.16
  135.0 0.1 shard_map.101.rest_1_.mine_ref
  135.1 1.5 collective-permute-start.10
  136.6 6.2 %shard_map.102.rest_1_ = bf16[768,1024]{1,0:T(8,128)(2,1)S(1)} custom-call(s32[2]{0:T(128)S(1)} %pad_add_fusion.6.place_ref, bf16[768,2048]{1,0:T(8,128)(2,1)S(1)} %copy-done, bf16[2048,8192]{1,0:T(8,128)(2,1)} %w_ref.17, bf16[768,1024]{1,0:T(8,128)(2,1)S(1)} %collective-permute-done.12.rest_0_, bf16[768,64]{1,0:T(8,128)(2,1)S(1)} %shard_map.101.rest_1_.mine_ref), custom_call_target="tpu_custom_call" | custom-call | flops 9663676416 | bytes 12582912 | tf_op jit(solution)/shard_map/pallas_call | solution.py:60
  142.8 2.7 %collective-permute-start.13 = (bf16[768,1024]{1,0:T(8,128)(2,1)S(1)}, bf16[768,1024]{1,0:T(8,128)(2,1)S(1)}, u32[]{:S(2)}, u32[]{:S(2)}) collective-permute-start(bf16[768,1024]{1,0:T(8,128)(2,1)S(1)} %shard_map.102.rest_1_), channel_id=1, source_target_pairs={{0,1},{1,0},{2,3},{3,2},{4,5},{5,4},{6,7},{7,6},{8,9},{9,8},{10,11... | collective-permute-start | bytes 4718600 | tf_op jit(solution)/shard_map/ppermute | solution.py:384
  145.6 2.2 %collective-permute-done.11.rest_0_ = bf16[768,1024]{1,0:T(8,128)(2,1)S(1)} collective-permute-done((bf16[768,1024]{1,0:T(8,128)(2,1)S(1)}, bf16[768,1024]{1,0:T(8,128)(2,1)S(1)}, u32[]{:S(2)}, u32[]{:S(2)}) %collective-permute-start.11) | collective-permute-done | bytes 1572896 | tf_op jit(solution)/shard_map/ppermute | solution.py:384
  147.8 6.2 %shard_map.103.after_ref = bf16[768,1024]{1,0:T(8,128)(2,1)S(1)} custom-call(s32[2]{0:T(128)S(1)} %pad_add_fusion.5.place_ref, bf16[768,2048]{1,0:T(8,128)(2,1)S(1)} %copy-done, bf16[2048,8192]{1,0:T(8,128)(2,1)} %w_ref.17, bf16[768,1024]{1,0:T(8,128)(2,1)S(1)} %collective-permute-done.11.rest_0_, bf16[768,1024]{1,0:T(8,128)(2,1)S(1)} %shard_map.102.rest_1_), custom_call_target="tpu_custom_call" | custom-call | flops 9663676416 | bytes 12582912 | tf_op jit(solution)/shard_map/pallas_call | solution.py:60
  154.0 0.8 collective-permute-start.14
  154.8 12.8 %collective-permute-done.10.theirs_ref = bf16[768,64]{1,0:T(8,128)(2,1)S(1)} collective-permute-done((bf16[768,64]{1,0:T(8,128)(2,1)S(1)}, bf16[768,64]{1,0:T(8,128)(2,1)S(1)}, u32[]{:S(2)}, u32[]{:S(2)}) %collective-permute-start.10) | collective-permute-done | bytes 98336 | tf_op jit(solution)/shard_map/ppermute | solution.py:446
  167.6 12.7 %shard_map.105.own_ref = f32[768,2048]{1,0:T(8,128)S(1)} custom-call(s32[1]{0:T(128)} %bitcast.block_ref, s32[8]{0:T(128)S(1)} %get-tuple-element.32.id_ref, bf16[768,2048]{1,0:T(8,128)(2,1)S(1)} %copy-done, bf16[2048,8192]{1,0:T(8,128)(2,1)} %w_ref.17, bf16[768,64]{1,0:T(8,128)(2,1)S(1)} %shard_map.104.chosen_ref.after_ref, s32[768,1]{1,0:T(8,128)S(1)} %copy-done.6, ...), custom_call_target="tpu_custom_call" | custom-call | flops 24159191040 | bytes 50331648 | tf_op jit(solution)/shard_map/pallas_call | solution.py:273
  180.4 1.1 collective-permute-done.15.rest_0_
  181.5 1.8 shard_map.106.rest_2_
  183.3 30.9 %collective-permute-done.13.rest_0_ = bf16[768,1024]{1,0:T(8,128)(2,1)S(1)} collective-permute-done((bf16[768,1024]{1,0:T(8,128)(2,1)S(1)}, bf16[768,1024]{1,0:T(8,128)(2,1)S(1)}, u32[]{:S(2)}, u32[]{:S(2)}) %collective-permute-start.13) | collective-permute-done | bytes 1572896 | tf_op jit(solution)/shard_map/ppermute | solution.py:384
  214.2 1.8 shard_map.107
  (31 shorter events, 0.2 us)
Async XLA Ops:
  0.0 7.6 %copy-start = (bf16[768,2048]{1,0:T(8,128)(2,1)S(1)}, bf16[768,2048]{1,0:T(8,128)(2,1)}, u32[]{:S(2)}) copy-start(bf16[768,2048]{1,0:T(8,128)(2,1)} %a_ref.19) | copy-start | bytes 9437188
  4.5 37.3 %collective-permute-start.3 = (bf16[768,256]{1,0:T(8,128)(2,1)}, bf16[768,256]{1,0:T(8,128)(2,1)S(1)}, u32[]{:S(2)}, u32[]{:S(2)}) collective-permute-start(bf16[768,256]{1,0:T(8,128)(2,1)} %shard_map.91.rest_0_), channel_id=1, source_target_pairs={{0,1},{3,2},{1,0},{2,3},{4,5},{7,6},{5,4},{6,7},{8,9},{11,10},{9,8... | collective-permute-start | bytes 1179656 | tf_op jit(solution)/shard_map/ppermute | solution.py:384
  7.6 1.0 copy-start.3
  14.0 28.6 %collective-permute-start.4 = (bf16[768,768]{1,0:T(8,128)(2,1)}, bf16[768,768]{1,0:T(8,128)(2,1)}, u32[]{:S(2)}, u32[]{:S(2)}) collective-permute-start(bf16[768,768]{1,0:T(8,128)(2,1)} %shard_map.92.rest_0_), channel_id=1, source_target_pairs={{0,1},{3,2},{4,5},{7,6},{8,9},{11,10},{12,13},{15,14},{16,17},{19,... | collective-permute-start | bytes 3538952 | tf_op jit(solution)/shard_map/ppermute | solution.py:384
  16.9 8.9 %copy-start.9 = (s32[4,4]{1,0:T(4,128)S(1)}, s32[4,4]{1,0:T(4,128)}, u32[]{:S(2)}) copy-start(s32[4,4]{1,0:T(4,128)} %param.15) | copy-start | bytes 196
  16.9 8.9 %copy-start.10 = (s32[32]{0:T(128)S(1)}, s32[32]{0:T(128)}, u32[]{:S(2)}) copy-start(s32[32]{0:T(128)} %param.16) | copy-start | bytes 388
  23.3 63.2 %collective-permute-start.6 = (bf16[768,1024]{1,0:T(8,128)(2,1)}, bf16[768,1024]{1,0:T(8,128)(2,1)}, u32[]{:S(2)}, u32[]{:S(2)}) collective-permute-start(bf16[768,1024]{1,0:T(8,128)(2,1)} %shard_map.93.refs_3_), channel_id=1, source_target_pairs={{0,1},{3,2},{4,5},{7,6},{8,9},{11,10},{12,13},{15,14},{16,17},{19,... | collective-permute-start | bytes 4718600 | tf_op jit(solution)/shard_map/ppermute | solution.py:384
  28.6 2.2 %copy-start.1 = (bf16[8,2,64,2048]{3,2,1,0:T(8,128)(2,1)S(1)}, bf16[8,2,64,2048]{3,2,1,0:T(8,128)(2,1)}, u32[]{:S(2)}) copy-start(bf16[8,2,64,2048]{3,2,1,0:T(8,128)(2,1)} %rest_1_.1) | copy-start | bytes 12582916
  30.8 6.2 %copy-start.8 = (s32[768]{0:T(1024)S(1)}, s32[768]{0:T(1024)}, u32[]{:S(2)}) copy-start(s32[768]{0:T(1024)} %param.17) | copy-start | bytes 9220
  32.8 1.0 copy-start.4
  33.8 26.4 %collective-permute-start.1 = (bf16[2,2,64,2048]{3,2,1,0:T(8,128)(2,1)}, bf16[2,2,64,2048]{3,2,1,0:T(8,128)(2,1)}, u32[]{:S(2)}, u32[]{:S(2)}) collective-permute-start(bf16[2,2,64,2048]{3,2,1,0:T(8,128)(2,1)} %get-tuple-element.11), channel_id=1, source_target_pairs={{0,8},{4,12},{8,0},{12,4},{1,9},{5,13},{9,1},{13,5},{2,10},{6,14},... | collective-permute-start | bytes 3145736 | tf_op jit(solution)/shard_map/ppermute | solution.py:439
  35.7 44.6 %collective-permute-start.2 = (bf16[2,2,64,2048]{3,2,1,0:T(8,128)(2,1)}, bf16[2,2,64,2048]{3,2,1,0:T(8,128)(2,1)}, u32[]{:S(2)}, u32[]{:S(2)}) collective-permute-start(bf16[2,2,64,2048]{3,2,1,0:T(8,128)(2,1)} %get-tuple-element.12), channel_id=1, source_target_pairs={{0,12},{4,8},{8,4},{12,0},{1,13},{5,9},{9,5},{13,1},{2,14},{6,10},... | collective-permute-start | bytes 3145736 | tf_op jit(solution)/shard_map/ppermute | solution.py:439
  41.7 38.7 %copy-start.2 = (bf16[8,2,64,2048]{3,2,1,0:T(8,128)(2,1)S(1)}, bf16[8,2,64,2048]{3,2,1,0:T(8,128)(2,1)}, u32[]{:S(2)}) copy-start(bf16[8,2,64,2048]{3,2,1,0:T(8,128)(2,1)} %rest_1_.1) | copy-start | bytes 12582916
  41.7 38.7 %collective-permute-start = (bf16[2,2,64,2048]{3,2,1,0:T(8,128)(2,1)}, bf16[2,2,64,2048]{3,2,1,0:T(8,128)(2,1)S(1)}, u32[]{:S(2)}, u32[]{:S(2)}) collective-permute-start(bf16[2,2,64,2048]{3,2,1,0:T(8,128)(2,1)} %copy-done.4), channel_id=1, source_target_pairs={{0,4},{4,0},{8,12},{12,8},{1,5},{5,1},{9,13},{13,9},{2,6},{6,2},{1... | collective-permute-start | bytes 3145736 | tf_op jit(solution)/shard_map/ppermute | solution.py:439
  42.6 1.6 copy-start.5
  44.2 36.2 %copy-start.6 = (s32[768,1]{1,0:T(8,128)S(1)}, s32[768,1]{1,0:T(8,128)}, u32[]{:S(2)}) copy-start(s32[768,1]{1,0:T(8,128)} %broadcast_in_dim.86.wanted_ref) | copy-start | bytes 9220
  44.2 36.2 %copy-start.7 = (bf16[8,2,64,2048]{3,2,1,0:T(8,128)(2,1)S(1)}, bf16[8,2,64,2048]{3,2,1,0:T(8,128)(2,1)}, u32[]{:S(2)}) copy-start(bf16[8,2,64,2048]{3,2,1,0:T(8,128)(2,1)} %rest_0_.1) | copy-start | bytes 12582916
  50.8 64.0 %collective-permute-start.9 = (bf16[768,1024]{1,0:T(8,128)(2,1)S(1)}, bf16[768,1024]{1,0:T(8,128)(2,1)S(1)}, u32[]{:S(2)}, u32[]{:S(2)}) collective-permute-start(bf16[768,1024]{1,0:T(8,128)(2,1)S(1)} %shard_map.95.rest_5_), channel_id=1, source_target_pairs={{1,2},{2,1},{5,6},{6,5},{9,10},{10,9},{13,14},{14,13},{17,18},{18,... | collective-permute-start | bytes 4718600 | tf_op jit(solution)/shard_map/ppermute | solution.py:386
  60.2 67.8 %collective-permute-start.8 = (bf16[768,1024]{1,0:T(8,128)(2,1)S(1)}, bf16[768,1024]{1,0:T(8,128)(2,1)S(1)}, u32[]{:S(2)}, u32[]{:S(2)}) collective-permute-start(bf16[768,1024]{1,0:T(8,128)(2,1)S(1)} %shard_map.95.rest_5_), channel_id=1, source_target_pairs={{0,1},{3,2},{4,5},{7,6},{8,9},{11,10},{12,13},{15,14},{16,17},{19,... | collective-permute-start | bytes 4718600 | tf_op jit(solution)/shard_map/ppermute | solution.py:384
  85.2 28.9 %collective-permute-start.5 = (bf16[768,64]{1,0:T(8,128)(2,1)S(1)}, bf16[768,64]{1,0:T(8,128)(2,1)S(1)}, u32[]{:S(2)}, u32[]{:S(2)}) collective-permute-start(bf16[768,64]{1,0:T(8,128)(2,1)S(1)} %get-tuple-element.13.rest_1_.mine_ref), channel_id=1, source_target_pairs={{0,1},{3,2},{4,5},{7,6},{8,9},{11,10},{12,13},{15,14},{16,17},{19,... | collective-permute-start | bytes 294920 | tf_op jit(solution)/shard_map/ppermute | solution.py:446
  92.9 43.7 %collective-permute-start.12 = (bf16[768,1024]{1,0:T(8,128)(2,1)S(1)}, bf16[768,1024]{1,0:T(8,128)(2,1)S(1)}, u32[]{:S(2)}, u32[]{:S(2)}) collective-permute-start(bf16[768,1024]{1,0:T(8,128)(2,1)S(1)} %shard_map.97.after_ref), channel_id=1, source_target_pairs={{1,2},{2,1},{5,6},{6,5},{9,10},{10,9},{13,14},{14,13},{17,18},{18,... | collective-permute-start | bytes 4718600 | tf_op jit(solution)/shard_map/ppermute | solution.py:386
  93.7 54.1 %collective-permute-start.11 = (bf16[768,1024]{1,0:T(8,128)(2,1)S(1)}, bf16[768,1024]{1,0:T(8,128)(2,1)S(1)}, u32[]{:S(2)}, u32[]{:S(2)}) collective-permute-start(bf16[768,1024]{1,0:T(8,128)(2,1)S(1)} %shard_map.97.after_ref), channel_id=1, source_target_pairs={{0,1},{3,2},{4,5},{7,6},{8,9},{11,10},{12,13},{15,14},{16,17},{19,... | collective-permute-start | bytes 4718600 | tf_op jit(solution)/shard_map/ppermute | solution.py:384
  114.2 20.9 %collective-permute-start.7 = (bf16[768,64]{1,0:T(8,128)(2,1)S(1)}, bf16[768,64]{1,0:T(8,128)(2,1)S(1)}, u32[]{:S(2)}, u32[]{:S(2)}) collective-permute-start(bf16[768,64]{1,0:T(8,128)(2,1)S(1)} %shard_map.98.rest_1_.mine_ref), channel_id=1, source_target_pairs={{1,2},{2,1},{5,6},{6,5},{9,10},{10,9},{13,14},{14,13},{17,18},{18,... | collective-permute-start | bytes 294920 | tf_op jit(solution)/shard_map/ppermute | solution.py:446
  121.1 60.4 %collective-permute-start.15 = (bf16[768,1024]{1,0:T(8,128)(2,1)S(1)}, bf16[768,1024]{1,0:T(8,128)(2,1)S(1)}, u32[]{:S(2)}, u32[]{:S(2)}) collective-permute-start(bf16[768,1024]{1,0:T(8,128)(2,1)S(1)} %shard_map.99.rest_1_), channel_id=1, source_target_pairs={{0,1},{1,0},{2,3},{3,2},{4,5},{5,4},{6,7},{7,6},{8,9},{9,8},{10,11... | collective-permute-start | bytes 4718600 | tf_op jit(solution)/shard_map/ppermute | solution.py:384
  134.3 47.2 %collective-permute-start.16 = (bf16[768,1024]{1,0:T(8,128)(2,1)S(1)}, bf16[768,1024]{1,0:T(8,128)(2,1)S(1)}, u32[]{:S(2)}, u32[]{:S(2)}) collective-permute-start(bf16[768,1024]{1,0:T(8,128)(2,1)S(1)} %shard_map.100.after_ref), channel_id=1, source_target_pairs={{1,2},{2,1},{5,6},{6,5},{9,10},{10,9},{13,14},{14,13},{17,18},{18,... | collective-permute-start | bytes 4718600 | tf_op jit(solution)/shard_map/ppermute | solution.py:386
  135.1 32.4 %collective-permute-start.10 = (bf16[768,64]{1,0:T(8,128)(2,1)S(1)}, bf16[768,64]{1,0:T(8,128)(2,1)S(1)}, u32[]{:S(2)}, u32[]{:S(2)}) collective-permute-start(bf16[768,64]{1,0:T(8,128)(2,1)S(1)} %shard_map.101.rest_1_.mine_ref), channel_id=1, source_target_pairs={{1,0},{2,3},{5,4},{6,7},{9,8},{10,11},{13,12},{14,15},{17,16},{18,... | collective-permute-start | bytes 294920 | tf_op jit(solution)/shard_map/ppermute | solution.py:446
  142.8 71.4 %collective-permute-start.13 = (bf16[768,1024]{1,0:T(8,128)(2,1)S(1)}, bf16[768,1024]{1,0:T(8,128)(2,1)S(1)}, u32[]{:S(2)}, u32[]{:S(2)}) collective-permute-start(bf16[768,1024]{1,0:T(8,128)(2,1)S(1)} %shard_map.102.rest_1_), channel_id=1, source_target_pairs={{0,1},{1,0},{2,3},{3,2},{4,5},{5,4},{6,7},{7,6},{8,9},{9,8},{10,11... | collective-permute-start | bytes 4718600 | tf_op jit(solution)/shard_map/ppermute | solution.py:384
  154.0 29.3 %collective-permute-start.14 = (bf16[768,1024]{1,0:T(8,128)(2,1)S(1)}, bf16[768,1024]{1,0:T(8,128)(2,1)S(1)}, u32[]{:S(2)}, u32[]{:S(2)}) collective-permute-start(bf16[768,1024]{1,0:T(8,128)(2,1)S(1)} %shard_map.103.after_ref), channel_id=1, source_target_pairs={{1,2},{2,1},{5,6},{6,5},{9,10},{10,9},{13,14},{14,13},{17,18},{18,... | collective-permute-start | bytes 4718600 | tf_op jit(solution)/shard_map/ppermute | solution.py:386

commit v3 on v2

--- a/solution.py
+++ b/solution.py
@@ -9,6 +9,7 @@
 
 CAP = 2
 FIRST = 1
+ROW_PARTS = 2
 VMEM = 28 * 1024 * 1024
 FIRST_VMEM = 60 * 1024 * 1024
 SCALE = 3.0
@@ -82,50 +83,32 @@
     )
 
 
-def first_kernel(tile, tiles, place_ref, a_hbm, w_hbm, out_ref, a, w, sems):
-    parts, _, step = a.shape
-    column = pl.multiple_of(place_ref[0] * tile, tile)
-    copies = []
-    for k in range(parts):
-        copies.append(
-            (
-                pltpu.make_async_copy(a_hbm.at[:, pl.ds(k * step, step)], a.at[k], sems.at[0, k]),
-                pltpu.make_async_copy(
-                    w_hbm.at[pl.ds(k * step, step), pl.ds(column, tiles * tile)],
-                    w.at[k],
-                    sems.at[1, k],
-                ),
-            )
-        )
-    for of_a, of_w in copies:
-        of_w.start()
-        of_a.start()
-    total = None
-    for k, (of_a, of_w) in enumerate(copies):
-        of_w.wait()
-        of_a.wait()
-        share = jnp.dot(a[k], w[k], preferred_element_type=jnp.float32)
-        total = share if total is None else total + share
+def first_kernel(place_ref, a_ref, w_ref, out_ref, token_ref):
+    total = jnp.dot(a_ref[...], w_ref[...], preferred_element_type=jnp.float32)
     out_ref[...] = total.astype(out_ref.dtype)
+    token_ref[...] = jnp.zeros_like(token_ref)
 
 
 def first_term(attn, weight, first_tile, tile, tiles):
     rows, depth = attn.shape
-    step = min(depth, 512)
-    parts = depth // step
-    return pl.pallas_call(
-        functools.partial(first_kernel, tile, tiles),
-        in_specs=[
-            pl.BlockSpec(memory_space=pltpu.SMEM),
-            pl.BlockSpec(memory_space=pltpu.HBM),
-            pl.BlockSpec(memory_space=pltpu.HBM),
-        ],
-        out_specs=pl.BlockSpec(memory_space=pltpu.VMEM),
-        out_shape=jax.ShapeDtypeStruct((rows, tiles * tile), jnp.bfloat16),
-        scratch_shapes=[
-            pltpu.VMEM((parts, rows, step), attn.dtype),
-            pltpu.VMEM((parts, step, tiles * tile), weight.dtype),
-            pltpu.SemaphoreType.DMA((2, parts)),
+    step = rows // ROW_PARTS
+    return pl.pallas_call(
+        first_kernel,
+        grid_spec=pltpu.PrefetchScalarGridSpec(
+            num_scalar_prefetch=1,
+            grid=(ROW_PARTS,),
+            in_specs=[
+                pl.BlockSpec((step, depth), lambda n, b: (n, 0)),
+                pl.BlockSpec((depth, tiles * tile), lambda n, b: (0, b[0] // tiles)),
+            ],
+            out_specs=[
+                pl.BlockSpec((step, tiles * tile), lambda n, b: (n, 0)),
+                pl.BlockSpec((8, 128), lambda n, b: (0, 0)),
+            ],
+        ),
+        out_shape=[
+            jax.ShapeDtypeStruct((rows, tiles * tile), jnp.bfloat16),
+            jax.ShapeDtypeStruct((8, 128), jnp.float32),
         ],
         compiler_params=params(FIRST_VMEM),
         cost_estimate=cost(2 * rows * depth * tiles * tile, depth * tiles * tile),
@@ -360,7 +343,8 @@
                 for (low, count), ref in sums:
                     if low < start + tiles and start < low + count:
                         came.append((ref, flag, low - start))
-            return term(attn_out, out_weight, first, tile, tiles, came, after)
+            out = term(attn_out, out_weight, first, tile, tiles, came, after)
+            return out, out
 
         def step_of(step, came_x, came_y, after, between):
             right_block = tensor - 1 - step + z
@@ -373,18 +357,19 @@
                     block = jnp.where(goes_right, right_block, left_block)
                     flag_x = jnp.where(goes_right, odd, even & not_last)
                     flag_y = jnp.where(goes_right, even & not_first, odd & not_last)
-                    for_x = for_y = product(block, span, came_x, flag_x, came_y, flag_y, after)
+                    for_x, last = product(block, span, came_x, flag_x, came_y, flag_y, after)
+                    for_y = for_x
                 else:
                     flag = jnp.where(even, not_first, not_last)
                     block = jnp.where(even, right_block, left_block)
-                    for_x = product(block, span, [], flag, came_y, flag, after)
+                    for_x, last = product(block, span, [], flag, came_y, flag, after)
                     block = jnp.where(even, left_block, right_block)
-                    for_y = product(block, span, came_x, flag, [], flag, for_x)
-                pairs = pairs_x if step or xs else swap(pairs_x)
+                    for_y, last = product(block, span, came_x, flag, [], flag, last)
+                pairs = pairs_x if step else swap(pairs_x)
                 xs.append((span, lax.ppermute(for_x, "tensor", pairs)))
                 if pairs_y:
                     ys.append((span, lax.ppermute(for_y, "tensor", pairs_y)))
-                after = between(step, len(xs) - 1, for_y)
+                after = between(step, len(xs) - 1, last)
             return xs, ys, after
 
         matches = incoming[:, :, None] == jnp.arange(store_place.shape[0], dtype=jnp.int32)

time: 218 us -> 216 us (level)
  waiting for transfers between devices: 91.8 us -> 94.1 us
    ppermute x7, waiting for transfers between devices: 34.8 us -> 42.4 us  [step_of(): xs.append((span, lax.ppermute(for_x, 'tensor', pairs)))]
    ppermute x3, waiting for transfers between devices: 27.3 us -> 22.1 us  [fetch(): sources.insert(2, lax.ppermute(piece, 'replica', pairs))]
    ppermute x7, starting transfers between devices: 22.9 us -> 20.2 us  [step_of(): xs.append((span, lax.ppermute(for_x, 'tensor', pairs)))]
where the time goes in v3:
time: 216 us; the launch traced here: 215 us
  waiting for transfers between devices  94.1 us (44%)
  Pallas kernels  76.8 us (36%)
  starting transfers between devices  29.9 us (14%)
  local copies, waits for them, and re-layouts  7.77 us (4%)
  other arithmetic  6.36 us (3%)
    pallas_call x8, Pallas kernels, term(): pl.pallas_call(functools.partial(term_kernel, ranges), grid_spec=pltpu.Pr...  49.7 us
    ppermute x7, waiting for transfers between devices, step_of(): xs.append((span, lax.ppermute(for_x, 'tensor', pairs)))  42.4 us
    ppermute x3, waiting for transfers between devices, send_mine(): state['theirs'] = lax.ppermute(state['mine'], 'tensor', pairs)  29.6 us
    ppermute x3, waiting for transfers between devices, fetch(): sources.insert(2, lax.ppermute(piece, 'replica', pairs))  22.1 us
    ppermute x7, starting transfers between devices, step_of(): xs.append((span, lax.ppermute(for_x, 'tensor', pairs)))  20.2 us
    pallas_call x1, Pallas kernels, own_term(): pl.pallas_call(own_kernel, grid_spec=pltpu.PrefetchScalarGridSpec(num_sca...  12.7 us
    unnamed x22, local copies, waits for them, and re-layouts  5.17 us
    pallas_call x1, Pallas kernels, hold_slots(): pl.pallas_call(functools.partial(slots_kernel, len(sources)), grid_spec=p...  4.79 us
  transfers between devices with their start and end apart: 17, of which 8 were waited for; matrix products, arithmetic and copies ran while one was open for 4% of the time, Pallas kernels for 33%

profile of v3, /device:TPU:0, one launch (start us, length us, event | category | flops | bytes accessed | tf_op | source)
XLA Modules:
  0.0 215.1 jit_solution(5867218129403822770)
XLA Ops:
  0.0 3.7 %shard_map.91 = (bf16[768,256]{1,0:T(8,128)(2,1)}, f32[8,128]{1,0:T(8,128)}) custom-call(s32[1]{0:T(128)} %bitcast.9.place_ref, bf16[768,2048]{1,0:T(8,128)(2,1)} %a_ref.21, bf16[2048,8192]{1,0:T(8,128)(2,1)} %w_ref.19), custom_call_target="tpu_custom_call" | custom-call | flops 2415919104 | bytes 3145728 | tf_op jit(solution)/shard_map/pallas_call | solution.py:95
  3.7 3.0 %collective-permute-start.3 = (bf16[768,256]{1,0:T(8,128)(2,1)}, bf16[768,256]{1,0:T(8,128)(2,1)S(1)}, u32[]{:S(2)}, u32[]{:S(2)}) collective-permute-start(bf16[768,256]{1,0:T(8,128)(2,1)} %get-tuple-element.16), channel_id=1, source_target_pairs={{0,1},{3,2},{1,0},{2,3},{4,5},{7,6},{5,4},{6,7},{8,9},{11,10},{9,8... | collective-permute-start | bytes 1179656 | tf_op jit(solution)/shard_map/ppermute | solution.py:369
  6.7 0.7 copy-done.6
  7.4 5.4 %shard_map.92.rest_0_ = bf16[768,768]{1,0:T(8,128)(2,1)} custom-call(s32[1]{0:T(128)} %bitcast.8.place_ref, bf16[768,2048]{1,0:T(8,128)(2,1)S(1)} %copy-done, bf16[2048,8192]{1,0:T(8,128)(2,1)} %w_ref.19, f32[8,128]{1,0:T(8,128)S(1)} %copy-done.6), custom_call_target="tpu_custom_call" | custom-call | flops 7247757312 | bytes 9437184 | tf_op jit(solution)/shard_map/pallas_call | solution.py:61
  12.8 6.4 %shard_map.93.refs_3_ = bf16[768,1024]{1,0:T(8,128)(2,1)} custom-call(s32[1]{0:T(128)} %bitcast.7.place_ref, bf16[768,2048]{1,0:T(8,128)(2,1)S(1)} %copy-done, bf16[2048,8192]{1,0:T(8,128)(2,1)} %w_ref.19, bf16[768,768]{1,0:T(8,128)(2,1)} %shard_map.92.rest_0_), custom_call_target="tpu_custom_call" | custom-call | flops 9663676416 | bytes 12582912 | tf_op jit(solution)/shard_map/pallas_call | solution.py:61
  19.2 2.0 collective-permute-start.6
  21.2 0.2 select_reduce_fusion
  21.5 0.6 broadcast_compare_fusion
  22.1 0.9 convert_reduce_fusion
  22.9 0.8 select_reduce_fusion.1
  23.8 0.2 fusion.3
  24.0 0.1 pad_add_fusion.row_ref
  24.1 2.2 %copy-done.1 = bf16[8,2,64,2048]{3,2,1,0:T(8,128)(2,1)S(1)} copy-done((bf16[8,2,64,2048]{3,2,1,0:T(8,128)(2,1)S(1)}, bf16[8,2,64,2048]{3,2,1,0:T(8,128)(2,1)}, u32[]{:S(2)}) %copy-start.1) | copy-done | bytes 4194328
  26.3 2.0 shard_map.94
  28.3 1.0 copy-done.3
  29.3 1.5 collective-permute-start.1
  30.8 0.5 fusion.8
  31.4 0.7 fusion.6
  32.1 0.9 broadcast_in_dim.86.wanted_ref
  33.0 0.7 fusion.1
  33.7 0.7 select_reduce_fusion.2
  34.5 0.7 compare_select_fusion
  35.1 0.6 compare_select_fusion.1
  35.7 0.8 concatenate.6.index_ref
  36.5 0.1 pad_add_fusion.1.place_ref
  36.6 0.1 pad_add_fusion.2.place_ref
  36.6 0.1 pad_add_fusion.3.place_ref
  36.7 0.1 pad_add_fusion.5.place_ref
  36.8 0.7 collective-permute-start
  37.5 4.8 %collective-permute-done.4.rest_1_ = bf16[768,768]{1,0:T(8,128)(2,1)} collective-permute-done((bf16[768,768]{1,0:T(8,128)(2,1)}, bf16[768,768]{1,0:T(8,128)(2,1)}, u32[]{:S(2)}, u32[]{:S(2)}) %collective-permute-start.4) | collective-permute-done | bytes 1179680 | tf_op jit(solution)/shard_map/ppermute | solution.py:369
  42.3 1.2 copy-done.4
  43.5 6.7 %shard_map.95.rest_5_ = bf16[768,1024]{1,0:T(8,128)(2,1)S(1)} custom-call(s32[3]{0:T(128)S(1)} %pad_add_fusion.1.place_ref, bf16[768,2048]{1,0:T(8,128)(2,1)S(1)} %copy-done, bf16[2048,8192]{1,0:T(8,128)(2,1)} %w_ref.19, bf16[768,256]{1,0:T(8,128)(2,1)S(1)} %collective-permute-done.3.rest_0_, bf16[768,768]{1,0:T(8,128)(2,1)} %collective-permute-done.4.rest_1_, ...), custom_call_target="tpu_custom_call" | custom-call | flops 9663676416 | bytes 12582912 | tf_op jit(solution)/shard_map/pallas_call | solution.py:61
  50.2 0.8 collective-permute-start.9
  50.9 0.1 pad_add_fusion.4.place_ref
  51.0 0.1 pad_add_fusion.6.place_ref
  51.1 4.6 %collective-permute-done.1.rest_3_ = bf16[2,2,64,2048]{3,2,1,0:T(8,128)(2,1)} collective-permute-done((bf16[2,2,64,2048]{3,2,1,0:T(8,128)(2,1)}, bf16[2,2,64,2048]{3,2,1,0:T(8,128)(2,1)}, u32[]{:S(2)}, u32[]{:S(2)}) %collective-permute-start.1) | collective-permute-done | bytes 1048608 | tf_op jit(solution)/shard_map/ppermute | solution.py:424
  55.7 2.0 collective-permute-start.8
  57.8 17.4 %collective-permute-done.2.rest_4_ = bf16[2,2,64,2048]{3,2,1,0:T(8,128)(2,1)} collective-permute-done((bf16[2,2,64,2048]{3,2,1,0:T(8,128)(2,1)}, bf16[2,2,64,2048]{3,2,1,0:T(8,128)(2,1)}, u32[]{:S(2)}, u32[]{:S(2)}) %collective-permute-start.2) | collective-permute-done | bytes 1048608 | tf_op jit(solution)/shard_map/ppermute | solution.py:424
  75.2 4.8 %shard_map.96 = (bf16[768,64]{1,0:T(8,128)(2,1)S(1)}, bf16[8,64,2048]{2,1,0:T(8,128)(2,1)S(1)}) custom-call(s32[8]{0:T(128)S(1)} %get-tuple-element.29.kind_ref, s32[40]{0:T(128)S(1)} %concatenate.6.index_ref, s32[8]{0:T(128)S(1)} %get-tuple-element.36.id_ref, bf16[768,2048]{1,0:T(8,128)(2,1)S(1)} %copy-done, s32[768,1]{1,0:T(8,128)S(1)} %copy-done.5, ...), custom_call_target="tpu_custom_call" | custom-call | flops 4831838208 | bytes 18874368 | tf_op jit(solution)/shard_map/pallas_call | solution.py:191
  80.0 2.4 %collective-permute-start.5 = (bf16[768,64]{1,0:T(8,128)(2,1)S(1)}, bf16[768,64]{1,0:T(8,128)(2,1)S(1)}, u32[]{:S(2)}, u32[]{:S(2)}) collective-permute-start(bf16[768,64]{1,0:T(8,128)(2,1)S(1)} %get-tuple-element.17.rest_1_.mine_ref), channel_id=1, source_target_pairs={{0,1},{3,2},{4,5},{7,6},{8,9},{11,10},{12,13},{15,14},{16,17},{19,... | collective-permute-start | bytes 294920 | tf_op jit(solution)/shard_map/ppermute | solution.py:431
  82.4 6.4 %shard_map.97.after_ref = bf16[768,1024]{1,0:T(8,128)(2,1)S(1)} custom-call(s32[2]{0:T(128)S(1)} %pad_add_fusion.2.place_ref, bf16[768,2048]{1,0:T(8,128)(2,1)S(1)} %copy-done, bf16[2048,8192]{1,0:T(8,128)(2,1)} %w_ref.19, bf16[768,1024]{1,0:T(8,128)(2,1)} %collective-permute-done.6.rest_0_, bf16[768,64]{1,0:T(8,128)(2,1)S(1)} %get-tuple-element.17.rest_1_.mine_ref), custom_call_target="tpu_custom_call" | custom-call | flops 9663676416 | bytes 12582912 | tf_op jit(solution)/shard_map/pallas_call | solution.py:61
  88.8 0.8 collective-permute-start.12
  89.5 5.2 %collective-permute-start.11 = (bf16[768,1024]{1,0:T(8,128)(2,1)S(1)}, bf16[768,1024]{1,0:T(8,128)(2,1)S(1)}, u32[]{:S(2)}, u32[]{:S(2)}) collective-permute-start(bf16[768,1024]{1,0:T(8,128)(2,1)S(1)} %shard_map.97.after_ref), channel_id=1, source_target_pairs={{0,1},{3,2},{4,5},{7,6},{8,9},{11,10},{12,13},{15,14},{16,17},{19,... | collective-permute-start | bytes 4718600 | tf_op jit(solution)/shard_map/ppermute | solution.py:369
  94.8 18.6 %collective-permute-done.5.theirs_ref = bf16[768,64]{1,0:T(8,128)(2,1)S(1)} collective-permute-done((bf16[768,64]{1,0:T(8,128)(2,1)S(1)}, bf16[768,64]{1,0:T(8,128)(2,1)S(1)}, u32[]{:S(2)}, u32[]{:S(2)}) %collective-permute-start.5) | collective-permute-done | bytes 98336 | tf_op jit(solution)/shard_map/ppermute | solution.py:431
  113.4 0.1 shard_map.98.rest_1_.mine_ref
  113.4 0.7 collective-permute-start.7
  114.1 6.2 %shard_map.99.rest_1_ = bf16[768,1024]{1,0:T(8,128)(2,1)S(1)} custom-call(s32[2]{0:T(128)S(1)} %pad_add_fusion.4.place_ref, bf16[768,2048]{1,0:T(8,128)(2,1)S(1)} %copy-done, bf16[2048,8192]{1,0:T(8,128)(2,1)} %w_ref.19, bf16[768,1024]{1,0:T(8,128)(2,1)S(1)} %collective-permute-done.9.rest_0_, bf16[768,64]{1,0:T(8,128)(2,1)S(1)} %shard_map.98.rest_1_.mine_ref), custom_call_target="tpu_custom_call" | custom-call | flops 9663676416 | bytes 12582912 | tf_op jit(solution)/shard_map/pallas_call | solution.py:61
  120.4 5.2 %collective-permute-start.15 = (bf16[768,1024]{1,0:T(8,128)(2,1)S(1)}, bf16[768,1024]{1,0:T(8,128)(2,1)S(1)}, u32[]{:S(2)}, u32[]{:S(2)}) collective-permute-start(bf16[768,1024]{1,0:T(8,128)(2,1)S(1)} %shard_map.99.rest_1_), channel_id=1, source_target_pairs={{0,1},{1,0},{2,3},{3,2},{4,5},{5,4},{6,7},{7,6},{8,9},{9,8},{10,11... | collective-permute-start | bytes 4718600 | tf_op jit(solution)/shard_map/ppermute | solution.py:369
  125.6 6.2 %shard_map.100.after_ref = bf16[768,1024]{1,0:T(8,128)(2,1)S(1)} custom-call(s32[2]{0:T(128)S(1)} %pad_add_fusion.3.place_ref, bf16[768,2048]{1,0:T(8,128)(2,1)S(1)} %copy-done, bf16[2048,8192]{1,0:T(8,128)(2,1)} %w_ref.19, bf16[768,1024]{1,0:T(8,128)(2,1)S(1)} %collective-permute-done.8.rest_0_, bf16[768,1024]{1,0:T(8,128)(2,1)S(1)} %shard_map.99.rest_1_), custom_call_target="tpu_custom_call" | custom-call | flops 9663676416 | bytes 12582912 | tf_op jit(solution)/shard_map/pallas_call | solution.py:61
  131.8 0.8 collective-permute-start.16
  132.6 0.1 shard_map.101.rest_1_.mine_ref
  132.7 1.5 collective-permute-start.10
  134.2 6.2 %shard_map.102.rest_1_ = bf16[768,1024]{1,0:T(8,128)(2,1)S(1)} custom-call(s32[2]{0:T(128)S(1)} %pad_add_fusion.6.place_ref, bf16[768,2048]{1,0:T(8,128)(2,1)S(1)} %copy-done, bf16[2048,8192]{1,0:T(8,128)(2,1)} %w_ref.19, bf16[768,1024]{1,0:T(8,128)(2,1)S(1)} %collective-permute-done.12.rest_0_, bf16[768,64]{1,0:T(8,128)(2,1)S(1)} %shard_map.101.rest_1_.mine_ref), custom_call_target="tpu_custom_call" | custom-call | flops 9663676416 | bytes 12582912 | tf_op jit(solution)/shard_map/pallas_call | solution.py:61
  140.4 2.7 %collective-permute-start.13 = (bf16[768,1024]{1,0:T(8,128)(2,1)S(1)}, bf16[768,1024]{1,0:T(8,128)(2,1)S(1)}, u32[]{:S(2)}, u32[]{:S(2)}) collective-permute-start(bf16[768,1024]{1,0:T(8,128)(2,1)S(1)} %shard_map.102.rest_1_), channel_id=1, source_target_pairs={{0,1},{1,0},{2,3},{3,2},{4,5},{5,4},{6,7},{7,6},{8,9},{9,8},{10,11... | collective-permute-start | bytes 4718600 | tf_op jit(solution)/shard_map/ppermute | solution.py:369
  143.1 4.0 %collective-permute-done.11.rest_0_ = bf16[768,1024]{1,0:T(8,128)(2,1)S(1)} collective-permute-done((bf16[768,1024]{1,0:T(8,128)(2,1)S(1)}, bf16[768,1024]{1,0:T(8,128)(2,1)S(1)}, u32[]{:S(2)}, u32[]{:S(2)}) %collective-permute-start.11) | collective-permute-done | bytes 1572896 | tf_op jit(solution)/shard_map/ppermute | solution.py:369
  147.1 6.2 %shard_map.103.after_ref = bf16[768,1024]{1,0:T(8,128)(2,1)S(1)} custom-call(s32[2]{0:T(128)S(1)} %pad_add_fusion.5.place_ref, bf16[768,2048]{1,0:T(8,128)(2,1)S(1)} %copy-done, bf16[2048,8192]{1,0:T(8,128)(2,1)} %w_ref.19, bf16[768,1024]{1,0:T(8,128)(2,1)S(1)} %collective-permute-done.11.rest_0_, bf16[768,1024]{1,0:T(8,128)(2,1)S(1)} %shard_map.102.rest_1_), custom_call_target="tpu_custom_call" | custom-call | flops 9663676416 | bytes 12582912 | tf_op jit(solution)/shard_map/pallas_call | solution.py:61
  153.3 0.8 collective-permute-start.14
  154.1 11.0 %collective-permute-done.10.theirs_ref = bf16[768,64]{1,0:T(8,128)(2,1)S(1)} collective-permute-done((bf16[768,64]{1,0:T(8,128)(2,1)S(1)}, bf16[768,64]{1,0:T(8,128)(2,1)S(1)}, u32[]{:S(2)}, u32[]{:S(2)}) %collective-permute-start.10) | collective-permute-done | bytes 98336 | tf_op jit(solution)/shard_map/ppermute | solution.py:431
  165.1 0.1 shard_map.104.chosen_ref.after_ref
  165.2 12.7 %shard_map.105.own_ref = f32[768,2048]{1,0:T(8,128)S(1)} custom-call(s32[1]{0:T(128)} %bitcast.block_ref, s32[8]{0:T(128)S(1)} %get-tuple-element.36.id_ref, bf16[768,2048]{1,0:T(8,128)(2,1)S(1)} %copy-done, bf16[2048,8192]{1,0:T(8,128)(2,1)} %w_ref.19, bf16[768,64]{1,0:T(8,128)(2,1)S(1)} %shard_map.104.chosen_ref.after_ref, s32[768,1]{1,0:T(8,128)S(1)} %copy-done.5, ...), custom_call_target="tpu_custom_call" | custom-call | flops 24159191040 | bytes 50331648 | tf_op jit(solution)/shard_map/pallas_call | solution.py:256
  177.9 2.9 %collective-permute-done.15.rest_0_ = bf16[768,1024]{1,0:T(8,128)(2,1)S(1)} collective-permute-done((bf16[768,1024]{1,0:T(8,128)(2,1)S(1)}, bf16[768,1024]{1,0:T(8,128)(2,1)S(1)}, u32[]{:S(2)}, u32[]{:S(2)}) %collective-permute-start.15) | collective-permute-done | bytes 1572896 | tf_op jit(solution)/shard_map/ppermute | solution.py:369
  180.8 1.8 shard_map.106.rest_2_
  182.6 30.7 %collective-permute-done.13.rest_0_ = bf16[768,1024]{1,0:T(8,128)(2,1)S(1)} collective-permute-done((bf16[768,1024]{1,0:T(8,128)(2,1)S(1)}, bf16[768,1024]{1,0:T(8,128)(2,1)S(1)}, u32[]{:S(2)}, u32[]{:S(2)}) %collective-permute-start.13) | collective-permute-done | bytes 1572896 | tf_op jit(solution)/shard_map/ppermute | solution.py:369
  213.3 1.8 shard_map.107
  (31 shorter events, 0.1 us)
Async XLA Ops:
  0.0 6.7 %copy-start = (bf16[768,2048]{1,0:T(8,128)(2,1)S(1)}, bf16[768,2048]{1,0:T(8,128)(2,1)}, u32[]{:S(2)}) copy-start(bf16[768,2048]{1,0:T(8,128)(2,1)} %a_ref.21) | copy-start | bytes 9437188
  3.7 33.1 %collective-permute-start.3 = (bf16[768,256]{1,0:T(8,128)(2,1)}, bf16[768,256]{1,0:T(8,128)(2,1)S(1)}, u32[]{:S(2)}, u32[]{:S(2)}) collective-permute-start(bf16[768,256]{1,0:T(8,128)(2,1)} %get-tuple-element.16), channel_id=1, source_target_pairs={{0,1},{3,2},{1,0},{2,3},{4,5},{7,6},{5,4},{6,7},{8,9},{11,10},{9,8... | collective-permute-start | bytes 1179656 | tf_op jit(solution)/shard_map/ppermute | solution.py:369
  6.7 0.7 copy-start.6
  12.8 29.5 %collective-permute-start.4 = (bf16[768,768]{1,0:T(8,128)(2,1)}, bf16[768,768]{1,0:T(8,128)(2,1)}, u32[]{:S(2)}, u32[]{:S(2)}) collective-permute-start(bf16[768,768]{1,0:T(8,128)(2,1)} %shard_map.92.rest_0_), channel_id=1, source_target_pairs={{0,1},{3,2},{1,0},{2,3},{4,5},{7,6},{5,4},{6,7},{8,9},{11,10},{9,8... | collective-permute-start | bytes 3538952 | tf_op jit(solution)/shard_map/ppermute | solution.py:369
  12.8 8.4 %copy-start.9 = (s32[4,4]{1,0:T(4,128)S(1)}, s32[4,4]{1,0:T(4,128)}, u32[]{:S(2)}) copy-start(s32[4,4]{1,0:T(4,128)} %param.15) | copy-start | bytes 196
  12.8 8.4 %copy-start.10 = (s32[32]{0:T(128)S(1)}, s32[32]{0:T(128)}, u32[]{:S(2)}) copy-start(s32[32]{0:T(128)} %param.16) | copy-start | bytes 388
  19.2 63.1 %collective-permute-start.6 = (bf16[768,1024]{1,0:T(8,128)(2,1)}, bf16[768,1024]{1,0:T(8,128)(2,1)}, u32[]{:S(2)}, u32[]{:S(2)}) collective-permute-start(bf16[768,1024]{1,0:T(8,128)(2,1)} %shard_map.93.refs_3_), channel_id=1, source_target_pairs={{0,1},{3,2},{1,0},{2,3},{4,5},{7,6},{5,4},{6,7},{8,9},{11,10},{9,8... | collective-permute-start | bytes 4718600 | tf_op jit(solution)/shard_map/ppermute | solution.py:369
  24.1 2.2 %copy-start.1 = (bf16[8,2,64,2048]{3,2,1,0:T(8,128)(2,1)S(1)}, bf16[8,2,64,2048]{3,2,1,0:T(8,128)(2,1)}, u32[]{:S(2)}) copy-start(bf16[8,2,64,2048]{3,2,1,0:T(8,128)(2,1)} %rest_1_.1) | copy-start | bytes 12582916
  26.3 5.8 %copy-start.8 = (s32[768]{0:T(1024)S(1)}, s32[768]{0:T(1024)}, u32[]{:S(2)}) copy-start(s32[768]{0:T(1024)} %param.17) | copy-start | bytes 9220
  28.3 1.0 copy-start.3
  29.3 26.4 %collective-permute-start.1 = (bf16[2,2,64,2048]{3,2,1,0:T(8,128)(2,1)}, bf16[2,2,64,2048]{3,2,1,0:T(8,128)(2,1)}, u32[]{:S(2)}, u32[]{:S(2)}) collective-permute-start(bf16[2,2,64,2048]{3,2,1,0:T(8,128)(2,1)} %get-tuple-element.14), channel_id=1, source_target_pairs={{0,8},{4,12},{8,0},{12,4},{1,9},{5,13},{9,1},{13,5},{2,10},{6,14},... | collective-permute-start | bytes 3145736 | tf_op jit(solution)/shard_map/ppermute | solution.py:424
  30.8 44.4 %collective-permute-start.2 = (bf16[2,2,64,2048]{3,2,1,0:T(8,128)(2,1)}, bf16[2,2,64,2048]{3,2,1,0:T(8,128)(2,1)}, u32[]{:S(2)}, u32[]{:S(2)}) collective-permute-start(bf16[2,2,64,2048]{3,2,1,0:T(8,128)(2,1)} %get-tuple-element.15), channel_id=1, source_target_pairs={{0,12},{4,8},{8,4},{12,0},{1,13},{5,9},{9,5},{13,1},{2,14},{6,10},... | collective-permute-start | bytes 3145736 | tf_op jit(solution)/shard_map/ppermute | solution.py:424
  36.8 38.4 %copy-start.2 = (bf16[8,2,64,2048]{3,2,1,0:T(8,128)(2,1)S(1)}, bf16[8,2,64,2048]{3,2,1,0:T(8,128)(2,1)}, u32[]{:S(2)}) copy-start(bf16[8,2,64,2048]{3,2,1,0:T(8,128)(2,1)} %rest_1_.1) | copy-start | bytes 12582916
  36.8 38.4 %collective-permute-start = (bf16[2,2,64,2048]{3,2,1,0:T(8,128)(2,1)}, bf16[2,2,64,2048]{3,2,1,0:T(8,128)(2,1)S(1)}, u32[]{:S(2)}, u32[]{:S(2)}) collective-permute-start(bf16[2,2,64,2048]{3,2,1,0:T(8,128)(2,1)} %copy-done.3), channel_id=1, source_target_pairs={{0,4},{4,0},{8,12},{12,8},{1,5},{5,1},{9,13},{13,9},{2,6},{6,2},{1... | collective-permute-start | bytes 3145736 | tf_op jit(solution)/shard_map/ppermute | solution.py:424
  42.3 1.2 copy-start.4
  43.5 31.7 %copy-start.5 = (s32[768,1]{1,0:T(8,128)S(1)}, s32[768,1]{1,0:T(8,128)}, u32[]{:S(2)}) copy-start(s32[768,1]{1,0:T(8,128)} %broadcast_in_dim.86.wanted_ref) | copy-start | bytes 9220
  43.5 31.7 %copy-start.7 = (bf16[8,2,64,2048]{3,2,1,0:T(8,128)(2,1)S(1)}, bf16[8,2,64,2048]{3,2,1,0:T(8,128)(2,1)}, u32[]{:S(2)}) copy-start(bf16[8,2,64,2048]{3,2,1,0:T(8,128)(2,1)} %rest_0_.1) | copy-start | bytes 12582916
  50.2 63.9 %collective-permute-start.9 = (bf16[768,1024]{1,0:T(8,128)(2,1)S(1)}, bf16[768,1024]{1,0:T(8,128)(2,1)S(1)}, u32[]{:S(2)}, u32[]{:S(2)}) collective-permute-start(bf16[768,1024]{1,0:T(8,128)(2,1)S(1)} %shard_map.95.rest_5_), channel_id=1, source_target_pairs={{1,2},{2,1},{5,6},{6,5},{9,10},{10,9},{13,14},{14,13},{17,18},{18,... | collective-permute-start | bytes 4718600 | tf_op jit(solution)/shard_map/ppermute | solution.py:371
  55.7 69.8 %collective-permute-start.8 = (bf16[768,1024]{1,0:T(8,128)(2,1)S(1)}, bf16[768,1024]{1,0:T(8,128)(2,1)S(1)}, u32[]{:S(2)}, u32[]{:S(2)}) collective-permute-start(bf16[768,1024]{1,0:T(8,128)(2,1)S(1)} %shard_map.95.rest_5_), channel_id=1, source_target_pairs={{0,1},{3,2},{4,5},{7,6},{8,9},{11,10},{12,13},{15,14},{16,17},{19,... | collective-permute-start | bytes 4718600 | tf_op jit(solution)/shard_map/ppermute | solution.py:369
  80.0 33.4 %collective-permute-start.5 = (bf16[768,64]{1,0:T(8,128)(2,1)S(1)}, bf16[768,64]{1,0:T(8,128)(2,1)S(1)}, u32[]{:S(2)}, u32[]{:S(2)}) collective-permute-start(bf16[768,64]{1,0:T(8,128)(2,1)S(1)} %get-tuple-element.17.rest_1_.mine_ref), channel_id=1, source_target_pairs={{0,1},{3,2},{4,5},{7,6},{8,9},{11,10},{12,13},{15,14},{16,17},{19,... | collective-permute-start | bytes 294920 | tf_op jit(solution)/shard_map/ppermute | solution.py:431
  88.8 45.4 %collective-permute-start.12 = (bf16[768,1024]{1,0:T(8,128)(2,1)S(1)}, bf16[768,1024]{1,0:T(8,128)(2,1)S(1)}, u32[]{:S(2)}, u32[]{:S(2)}) collective-permute-start(bf16[768,1024]{1,0:T(8,128)(2,1)S(1)} %shard_map.97.after_ref), channel_id=1, source_target_pairs={{1,2},{2,1},{5,6},{6,5},{9,10},{10,9},{13,14},{14,13},{17,18},{18,... | collective-permute-start | bytes 4718600 | tf_op jit(solution)/shard_map/ppermute | solution.py:371
  89.5 57.5 %collective-permute-start.11 = (bf16[768,1024]{1,0:T(8,128)(2,1)S(1)}, bf16[768,1024]{1,0:T(8,128)(2,1)S(1)}, u32[]{:S(2)}, u32[]{:S(2)}) collective-permute-start(bf16[768,1024]{1,0:T(8,128)(2,1)S(1)} %shard_map.97.after_ref), channel_id=1, source_target_pairs={{0,1},{3,2},{4,5},{7,6},{8,9},{11,10},{12,13},{15,14},{16,17},{19,... | collective-permute-start | bytes 4718600 | tf_op jit(solution)/shard_map/ppermute | solution.py:369
  113.4 19.1 %collective-permute-start.7 = (bf16[768,64]{1,0:T(8,128)(2,1)S(1)}, bf16[768,64]{1,0:T(8,128)(2,1)S(1)}, u32[]{:S(2)}, u32[]{:S(2)}) collective-permute-start(bf16[768,64]{1,0:T(8,128)(2,1)S(1)} %shard_map.98.rest_1_.mine_ref), channel_id=1, source_target_pairs={{1,2},{2,1},{5,6},{6,5},{9,10},{10,9},{13,14},{14,13},{17,18},{18,... | collective-permute-start | bytes 294920 | tf_op jit(solution)/shard_map/ppermute | solution.py:431
  120.4 60.4 %collective-permute-start.15 = (bf16[768,1024]{1,0:T(8,128)(2,1)S(1)}, bf16[768,1024]{1,0:T(8,128)(2,1)S(1)}, u32[]{:S(2)}, u32[]{:S(2)}) collective-permute-start(bf16[768,1024]{1,0:T(8,128)(2,1)S(1)} %shard_map.99.rest_1_), channel_id=1, source_target_pairs={{0,1},{1,0},{2,3},{3,2},{4,5},{5,4},{6,7},{7,6},{8,9},{9,8},{10,11... | collective-permute-start | bytes 4718600 | tf_op jit(solution)/shard_map/ppermute | solution.py:369
  131.8 49.0 %collective-permute-start.16 = (bf16[768,1024]{1,0:T(8,128)(2,1)S(1)}, bf16[768,1024]{1,0:T(8,128)(2,1)S(1)}, u32[]{:S(2)}, u32[]{:S(2)}) collective-permute-start(bf16[768,1024]{1,0:T(8,128)(2,1)S(1)} %shard_map.100.after_ref), channel_id=1, source_target_pairs={{1,2},{2,1},{5,6},{6,5},{9,10},{10,9},{13,14},{14,13},{17,18},{18,... | collective-permute-start | bytes 4718600 | tf_op jit(solution)/shard_map/ppermute | solution.py:371
  132.7 32.4 %collective-permute-start.10 = (bf16[768,64]{1,0:T(8,128)(2,1)S(1)}, bf16[768,64]{1,0:T(8,128)(2,1)S(1)}, u32[]{:S(2)}, u32[]{:S(2)}) collective-permute-start(bf16[768,64]{1,0:T(8,128)(2,1)S(1)} %shard_map.101.rest_1_.mine_ref), channel_id=1, source_target_pairs={{1,0},{2,3},{5,4},{6,7},{9,8},{10,11},{13,12},{14,15},{17,16},{18,... | collective-permute-start | bytes 294920 | tf_op jit(solution)/shard_map/ppermute | solution.py:431
  140.4 73.0 %collective-permute-start.13 = (bf16[768,1024]{1,0:T(8,128)(2,1)S(1)}, bf16[768,1024]{1,0:T(8,128)(2,1)S(1)}, u32[]{:S(2)}, u32[]{:S(2)}) collective-permute-start(bf16[768,1024]{1,0:T(8,128)(2,1)S(1)} %shard_map.102.rest_1_), channel_id=1, source_target_pairs={{0,1},{1,0},{2,3},{3,2},{4,5},{5,4},{6,7},{7,6},{8,9},{9,8},{10,11... | collective-permute-start | bytes 4718600 | tf_op jit(solution)/shard_map/ppermute | solution.py:369
  153.3 29.3 %collective-permute-start.14 = (bf16[768,1024]{1,0:T(8,128)(2,1)S(1)}, bf16[768,1024]{1,0:T(8,128)(2,1)S(1)}, u32[]{:S(2)}, u32[]{:S(2)}) collective-permute-start(bf16[768,1024]{1,0:T(8,128)(2,1)S(1)} %shard_map.103.after_ref), channel_id=1, source_target_pairs={{1,2},{2,1},{5,6},{6,5},{9,10},{10,9},{13,14},{14,13},{17,18},{18,... | collective-permute-start | bytes 4718600 | tf_op jit(solution)/shard_map/ppermute | solution.py:371

commit v4 on v3

--- a/solution.py
+++ b/solution.py
@@ -1,4 +1,5 @@
 import functools
+import math
 
 import jax
 import jax.numpy as jnp
@@ -9,6 +10,7 @@
 
 CAP = 2
 FIRST = 1
+LAST = 1
 ROW_PARTS = 2
 VMEM = 28 * 1024 * 1024
 FIRST_VMEM = 60 * 1024 * 1024
@@ -42,12 +44,14 @@
     return max(128, width // 8)
 
 
-def spans(width, first):
+def spans(width, step, steps):
     tiles = width // tile_of(width)
     half = tiles // 2
     shares = [half, tiles - half] if half else [tiles]
-    if first and half > 2:
+    if half > 2 and step == 0:
         shares = [FIRST, half - FIRST, tiles - half]
+    if half > 2 and step == steps - 1:
+        shares = [half, tiles - half - LAST, LAST] if LAST else shares
     return [(sum(shares[:n]), share) for n, share in enumerate(shares)]
 
 
@@ -285,7 +289,7 @@
 
 def finish(own, sums, first_column, so_far):
     rows, width = own.shape
-    tile = tile_of(width) * 2
+    tile = math.gcd(2 * tile_of(width), sums[0].shape[1], first_column)
     here = pl.BlockSpec((rows, tile), lambda j: (0, first_column // tile + j))
     came = pl.BlockSpec((rows, tile), lambda j: (0, j))
     extra = [] if so_far is None else [so_far]
@@ -351,7 +355,7 @@
             left_block = z + step + 1 - tensor
             pairs_x, pairs_y = edges(step, 0), edges(step, 1)
             xs, ys = [], []
-            for span in spans(width, step == 0):
+            for span in spans(width, step, tensor - 1):
                 if 2 * step < tensor - 1:
                     goes_right = 2 * z < tensor
                     block = jnp.where(goes_right, right_block, left_block)
@@ -448,7 +452,7 @@
             return state["mine"]
 
         def between(step, piece, after):
-            if step == 0 and piece == len(spans(width, True)) - 1:
+            if step == 0 and piece == len(spans(width, 0, tensor - 1)) - 1:
                 return fetch(after)
             if step == 1 and piece == 0:
                 return shrink(after)
@@ -472,7 +476,7 @@
             last,
         )
         out = None
-        for span in spans(width, False):
+        for span in spans(width, tensor - 2, tensor - 1):
             sums = [ref for at, ref in came_x + came_y if at == span]
             out = finish(total, sums, span[0] * tile, out)
         return out

time: 216 us -> 215 us (level)
  waiting for transfers between devices: 94.1 us -> 86 us
  Pallas kernels: 76.8 us -> 82 us
    ppermute x7 -> x8, waiting for transfers between devices: 42.4 us -> 34.3 us  [step_of(): xs.append((span, lax.ppermute(for_x, 'tensor', pairs)))]
    pallas_call x8 -> x10, Pallas kernels: 49.7 us -> 52.9 us  [term(): pl.pallas_call(functools.partial(term_kernel, ranges), grid_spec=pltpu.Pr...]
    pallas_call x2 -> x3, Pallas kernels: 3.61 us -> 4.67 us  [finish(): pl.pallas_call(functools.partial(finish_kernel, len(sums)), grid=(sums[0]...]
    ppermute x7 -> x8, starting transfers between devices: 20.2 us -> 20.5 us  [step_of(): xs.append((span, lax.ppermute(for_x, 'tensor', pairs)))]
  transfers between devices with their start and end apart: 17 -> 19, of which waited for: 8 -> 9; matrix products, arithmetic and copies ran while one was open for 4% -> 5% of each run, Pallas kernels for 33% -> 36%
where the time goes in v4:
time: 215 us; the launch traced here: 214 us
  waiting for transfers between devices  86 us (40%)
  Pallas kernels  82 us (38%)
  starting transfers between devices  30.9 us (14%)
  local copies, waits for them, and re-layouts  8.27 us (4%)
  other arithmetic  6.8 us (3%)
    pallas_call x10, Pallas kernels, term(): pl.pallas_call(functools.partial(term_kernel, ranges), grid_spec=pltpu.Pr...  52.9 us
    ppermute x8, waiting for transfers between devices, step_of(): xs.append((span, lax.ppermute(for_x, 'tensor', pairs)))  34.3 us
    ppermute x3, waiting for transfers between devices, send_mine(): state['theirs'] = lax.ppermute(state['mine'], 'tensor', pairs)  30.1 us
    ppermute x3, waiting for transfers between devices, fetch(): sources.insert(2, lax.ppermute(piece, 'replica', pairs))  21.6 us
    ppermute x8, starting transfers between devices, step_of(): xs.append((span, lax.ppermute(for_x, 'tensor', pairs)))  20.5 us
    pallas_call x1, Pallas kernels, own_term(): pl.pallas_call(own_kernel, grid_spec=pltpu.PrefetchScalarGridSpec(num_sca...  12.7 us
    pallas_call x1, Pallas kernels, hold_slots(): pl.pallas_call(functools.partial(slots_kernel, len(sources)), grid_spec=p...  5.77 us
    unnamed x22, local copies, waits for them, and re-layouts  5.18 us
  transfers between devices with their start and end apart: 19, of which 9 were waited for; matrix products, arithmetic and copies ran while one was open for 5% of the time, Pallas kernels for 36%

profile of v4, /device:TPU:0, one launch (start us, length us, event | category | flops | bytes accessed | tf_op | source)
XLA Modules:
  0.0 214.2 jit_solution(4427472472391466913)
XLA Ops:
  0.0 3.7 %shard_map.91 = (bf16[768,256]{1,0:T(8,128)(2,1)}, f32[8,128]{1,0:T(8,128)}) custom-call(s32[1]{0:T(128)} %bitcast.9.place_ref, bf16[768,2048]{1,0:T(8,128)(2,1)} %a_ref.25, bf16[2048,8192]{1,0:T(8,128)(2,1)} %w_ref.23), custom_call_target="tpu_custom_call" | custom-call | flops 2415919104 | bytes 3145728 | tf_op jit(solution)/shard_map/pallas_call | solution.py:99
  3.7 3.0 %collective-permute-start.3 = (bf16[768,256]{1,0:T(8,128)(2,1)}, bf16[768,256]{1,0:T(8,128)(2,1)S(1)}, u32[]{:S(2)}, u32[]{:S(2)}) collective-permute-start(bf16[768,256]{1,0:T(8,128)(2,1)} %get-tuple-element.16), channel_id=1, source_target_pairs={{0,1},{3,2},{1,0},{2,3},{4,5},{7,6},{5,4},{6,7},{8,9},{11,10},{9,8... | collective-permute-start | bytes 1179656 | tf_op jit(solution)/shard_map/ppermute | solution.py:373
  6.7 0.7 copy-done.6
  7.4 5.3 %shard_map.92.rest_0_ = bf16[768,768]{1,0:T(8,128)(2,1)} custom-call(s32[1]{0:T(128)} %bitcast.8.place_ref, bf16[768,2048]{1,0:T(8,128)(2,1)S(1)} %copy-done, bf16[2048,8192]{1,0:T(8,128)(2,1)} %w_ref.23, f32[8,128]{1,0:T(8,128)S(1)} %copy-done.6), custom_call_target="tpu_custom_call" | custom-call | flops 7247757312 | bytes 9437184 | tf_op jit(solution)/shard_map/pallas_call | solution.py:65
  12.8 6.4 %shard_map.93.refs_3_ = bf16[768,1024]{1,0:T(8,128)(2,1)} custom-call(s32[1]{0:T(128)} %bitcast.7.place_ref, bf16[768,2048]{1,0:T(8,128)(2,1)S(1)} %copy-done, bf16[2048,8192]{1,0:T(8,128)(2,1)} %w_ref.23, bf16[768,768]{1,0:T(8,128)(2,1)} %shard_map.92.rest_0_), custom_call_target="tpu_custom_call" | custom-call | flops 9663676416 | bytes 12582912 | tf_op jit(solution)/shard_map/pallas_call | solution.py:65
  19.2 2.0 collective-permute-start.6
  21.2 0.2 select_reduce_fusion
  21.4 0.5 broadcast_compare_fusion
  22.0 0.8 convert_reduce_fusion
  22.8 0.7 select_reduce_fusion.1
  23.5 0.2 fusion.3
  23.7 0.1 pad_add_fusion.row_ref
  23.8 2.2 %copy-done.1 = bf16[8,2,64,2048]{3,2,1,0:T(8,128)(2,1)S(1)} copy-done((bf16[8,2,64,2048]{3,2,1,0:T(8,128)(2,1)S(1)}, bf16[8,2,64,2048]{3,2,1,0:T(8,128)(2,1)}, u32[]{:S(2)}) %copy-start.1) | copy-done | bytes 4194328
  26.0 2.0 shard_map.94
  28.0 1.0 copy-done.3
  29.1 1.5 collective-permute-start.1
  30.6 1.2 fusion.6
  31.7 0.5 add_bitcast_fusion
  32.2 0.6 fusion.8
  32.8 0.9 broadcast_in_dim.86.wanted_ref
  33.8 0.7 select_reduce_fusion.2
  34.5 0.7 fusion.1
  35.2 0.7 compare_select_fusion
  35.9 0.6 compare_select_fusion.1
  36.5 0.8 concatenate.6.index_ref
  37.3 0.1 pad_add_fusion.1.place_ref
  37.4 0.1 pad_add_fusion.2.place_ref
  37.7 0.7 collective-permute-start
  38.4 3.9 %collective-permute-done.4.rest_1_ = bf16[768,768]{1,0:T(8,128)(2,1)} collective-permute-done((bf16[768,768]{1,0:T(8,128)(2,1)}, bf16[768,768]{1,0:T(8,128)(2,1)}, u32[]{:S(2)}, u32[]{:S(2)}) %collective-permute-start.4) | collective-permute-done | bytes 1179680 | tf_op jit(solution)/shard_map/ppermute | solution.py:373
  42.3 1.2 copy-done.4
  43.5 6.7 %shard_map.95.rest_5_ = bf16[768,1024]{1,0:T(8,128)(2,1)S(1)} custom-call(s32[3]{0:T(128)S(1)} %pad_add_fusion.1.place_ref, bf16[768,2048]{1,0:T(8,128)(2,1)S(1)} %copy-done, bf16[2048,8192]{1,0:T(8,128)(2,1)} %w_ref.23, bf16[768,256]{1,0:T(8,128)(2,1)S(1)} %collective-permute-done.3.rest_0_, bf16[768,768]{1,0:T(8,128)(2,1)} %collective-permute-done.4.rest_1_, ...), custom_call_target="tpu_custom_call" | custom-call | flops 9663676416 | bytes 12582912 | tf_op jit(solution)/shard_map/pallas_call | solution.py:65
  50.2 0.8 collective-permute-start.9
  50.9 0.1 pad_add_fusion.6.place_ref
  51.1 4.4 %collective-permute-done.1.rest_3_ = bf16[2,2,64,2048]{3,2,1,0:T(8,128)(2,1)} collective-permute-done((bf16[2,2,64,2048]{3,2,1,0:T(8,128)(2,1)}, bf16[2,2,64,2048]{3,2,1,0:T(8,128)(2,1)}, u32[]{:S(2)}, u32[]{:S(2)}) %collective-permute-start.1) | collective-permute-done | bytes 1048608 | tf_op jit(solution)/shard_map/ppermute | solution.py:428
  55.5 2.3 %collective-permute-start.8 = (bf16[768,1024]{1,0:T(8,128)(2,1)S(1)}, bf16[768,1024]{1,0:T(8,128)(2,1)S(1)}, u32[]{:S(2)}, u32[]{:S(2)}) collective-permute-start(bf16[768,1024]{1,0:T(8,128)(2,1)S(1)} %shard_map.95.rest_5_), channel_id=1, source_target_pairs={{0,1},{3,2},{4,5},{7,6},{8,9},{11,10},{12,13},{15,14},{16,17},{19,... | collective-permute-start | bytes 4718600 | tf_op jit(solution)/shard_map/ppermute | solution.py:373
  57.8 17.2 %collective-permute-done.2.rest_4_ = bf16[2,2,64,2048]{3,2,1,0:T(8,128)(2,1)} collective-permute-done((bf16[2,2,64,2048]{3,2,1,0:T(8,128)(2,1)}, bf16[2,2,64,2048]{3,2,1,0:T(8,128)(2,1)}, u32[]{:S(2)}, u32[]{:S(2)}) %collective-permute-start.2) | collective-permute-done | bytes 1048608 | tf_op jit(solution)/shard_map/ppermute | solution.py:428
  75.0 5.8 %shard_map.96 = (bf16[768,64]{1,0:T(8,128)(2,1)S(1)}, bf16[8,64,2048]{2,1,0:T(8,128)(2,1)S(1)}) custom-call(s32[8]{0:T(128)S(1)} %get-tuple-element.29.kind_ref, s32[40]{0:T(128)S(1)} %concatenate.6.index_ref, s32[8]{0:T(128)S(1)} %get-tuple-element.36.id_ref, bf16[768,2048]{1,0:T(8,128)(2,1)S(1)} %copy-done, s32[768,1]{1,0:T(8,128)S(1)} %copy-done.5, ...), custom_call_target="tpu_custom_call" | custom-call | flops 4831838208 | bytes 18874368 | tf_op jit(solution)/shard_map/pallas_call | solution.py:195
  80.7 2.4 %collective-permute-start.5 = (bf16[768,64]{1,0:T(8,128)(2,1)S(1)}, bf16[768,64]{1,0:T(8,128)(2,1)S(1)}, u32[]{:S(2)}, u32[]{:S(2)}) collective-permute-start(bf16[768,64]{1,0:T(8,128)(2,1)S(1)} %get-tuple-element.17.rest_1_.mine_ref), channel_id=1, source_target_pairs={{0,1},{3,2},{4,5},{7,6},{8,9},{11,10},{12,13},{15,14},{16,17},{19,... | collective-permute-start | bytes 294920 | tf_op jit(solution)/shard_map/ppermute | solution.py:435
  83.1 6.4 %shard_map.97.after_ref = bf16[768,1024]{1,0:T(8,128)(2,1)S(1)} custom-call(s32[2]{0:T(128)S(1)} %pad_add_fusion.2.place_ref, bf16[768,2048]{1,0:T(8,128)(2,1)S(1)} %copy-done, bf16[2048,8192]{1,0:T(8,128)(2,1)} %w_ref.23, bf16[768,1024]{1,0:T(8,128)(2,1)} %collective-permute-done.6.rest_0_, bf16[768,64]{1,0:T(8,128)(2,1)S(1)} %get-tuple-element.17.rest_1_.mine_ref), custom_call_target="tpu_custom_call" | custom-call | flops 9663676416 | bytes 12582912 | tf_op jit(solution)/shard_map/pallas_call | solution.py:65
  89.5 0.8 collective-permute-start.12
  90.3 5.2 %collective-permute-start.11 = (bf16[768,1024]{1,0:T(8,128)(2,1)S(1)}, bf16[768,1024]{1,0:T(8,128)(2,1)S(1)}, u32[]{:S(2)}, u32[]{:S(2)}) collective-permute-start(bf16[768,1024]{1,0:T(8,128)(2,1)S(1)} %shard_map.97.after_ref), channel_id=1, source_target_pairs={{0,1},{3,2},{4,5},{7,6},{8,9},{11,10},{12,13},{15,14},{16,17},{19,... | collective-permute-start | bytes 4718600 | tf_op jit(solution)/shard_map/ppermute | solution.py:373
  95.5 17.8 %collective-permute-done.5.theirs_ref = bf16[768,64]{1,0:T(8,128)(2,1)S(1)} collective-permute-done((bf16[768,64]{1,0:T(8,128)(2,1)S(1)}, bf16[768,64]{1,0:T(8,128)(2,1)S(1)}, u32[]{:S(2)}, u32[]{:S(2)}) %collective-permute-start.5) | collective-permute-done | bytes 98336 | tf_op jit(solution)/shard_map/ppermute | solution.py:435
  113.4 0.7 collective-permute-start.7
  114.1 6.2 %shard_map.99.rest_1_ = bf16[768,1024]{1,0:T(8,128)(2,1)S(1)} custom-call(s32[2]{0:T(128)S(1)} %pad_add_fusion.4.place_ref, bf16[768,2048]{1,0:T(8,128)(2,1)S(1)} %copy-done, bf16[2048,8192]{1,0:T(8,128)(2,1)} %w_ref.23, bf16[768,1024]{1,0:T(8,128)(2,1)S(1)} %collective-permute-done.9.rest_0_, bf16[768,64]{1,0:T(8,128)(2,1)S(1)} %shard_map.98.rest_1_.mine_ref), custom_call_target="tpu_custom_call" | custom-call | flops 9663676416 | bytes 12582912 | tf_op jit(solution)/shard_map/pallas_call | solution.py:65
  120.4 5.2 %collective-permute-start.17 = (bf16[768,1024]{1,0:T(8,128)(2,1)S(1)}, bf16[768,1024]{1,0:T(8,128)(2,1)S(1)}, u32[]{:S(2)}, u32[]{:S(2)}) collective-permute-start(bf16[768,1024]{1,0:T(8,128)(2,1)S(1)} %shard_map.99.rest_1_), channel_id=1, source_target_pairs={{0,1},{1,0},{2,3},{3,2},{4,5},{5,4},{6,7},{7,6},{8,9},{9,8},{10,11... | collective-permute-start | bytes 4718600 | tf_op jit(solution)/shard_map/ppermute | solution.py:373
  125.6 6.2 %shard_map.100.after_ref = bf16[768,1024]{1,0:T(8,128)(2,1)S(1)} custom-call(s32[2]{0:T(128)S(1)} %pad_add_fusion.3.place_ref, bf16[768,2048]{1,0:T(8,128)(2,1)S(1)} %copy-done, bf16[2048,8192]{1,0:T(8,128)(2,1)} %w_ref.23, bf16[768,1024]{1,0:T(8,128)(2,1)S(1)} %collective-permute-done.8.rest_0_, bf16[768,1024]{1,0:T(8,128)(2,1)S(1)} %shard_map.99.rest_1_), custom_call_target="tpu_custom_call" | custom-call | flops 9663676416 | bytes 12582912 | tf_op jit(solution)/shard_map/pallas_call | solution.py:65
  131.8 0.8 collective-permute-start.18
  132.7 1.5 collective-permute-start.10
  134.2 5.1 %shard_map.102.rest_1_ = bf16[768,768]{1,0:T(8,128)(2,1)S(1)} custom-call(s32[2]{0:T(128)S(1)} %pad_add_fusion.6.place_ref, bf16[768,2048]{1,0:T(8,128)(2,1)S(1)} %copy-done, bf16[2048,8192]{1,0:T(8,128)(2,1)} %w_ref.23, bf16[768,1024]{1,0:T(8,128)(2,1)S(1)} %collective-permute-done.12.rest_0_, bf16[768,64]{1,0:T(8,128)(2,1)S(1)} %shard_map.101.rest_1_.mine_ref), custom_call_target="tpu_custom_call" | custom-call | flops 7247757312 | bytes 9437184 | tf_op jit(solution)/shard_map/pallas_call | solution.py:65
  139.2 2.7 %collective-permute-start.15 = (bf16[768,768]{1,0:T(8,128)(2,1)S(1)}, bf16[768,768]{1,0:T(8,128)(2,1)S(1)}, u32[]{:S(2)}, u32[]{:S(2)}) collective-permute-start(bf16[768,768]{1,0:T(8,128)(2,1)S(1)} %shard_map.102.rest_1_), channel_id=1, source_target_pairs={{0,1},{1,0},{2,3},{3,2},{4,5},{5,4},{6,7},{7,6},{8,9},{9,8},{10,11... | collective-permute-start | bytes 3538952 | tf_op jit(solution)/shard_map/ppermute | solution.py:373
  141.9 5.1 %collective-permute-done.11.rest_0_ = bf16[768,1024]{1,0:T(8,128)(2,1)S(1)} collective-permute-done((bf16[768,1024]{1,0:T(8,128)(2,1)S(1)}, bf16[768,1024]{1,0:T(8,128)(2,1)S(1)}, u32[]{:S(2)}, u32[]{:S(2)}) %collective-permute-start.11) | collective-permute-done | bytes 1572896 | tf_op jit(solution)/shard_map/ppermute | solution.py:373
  147.1 5.1 %shard_map.103.after_ref = bf16[768,768]{1,0:T(8,128)(2,1)S(1)} custom-call(s32[2]{0:T(128)S(1)} %pad_add_fusion.5.place_ref, bf16[768,2048]{1,0:T(8,128)(2,1)S(1)} %copy-done, bf16[2048,8192]{1,0:T(8,128)(2,1)} %w_ref.23, bf16[768,1024]{1,0:T(8,128)(2,1)S(1)} %collective-permute-done.11.rest_0_, bf16[768,768]{1,0:T(8,128)(2,1)S(1)} %shard_map.102.rest_1_), custom_call_target="tpu_custom_call" | custom-call | flops 7247757312 | bytes 9437184 | tf_op jit(solution)/shard_map/pallas_call | solution.py:65
  152.1 0.7 collective-permute-start.16
  152.9 12.2 %collective-permute-done.10.theirs_ref = bf16[768,64]{1,0:T(8,128)(2,1)S(1)} collective-permute-done((bf16[768,64]{1,0:T(8,128)(2,1)S(1)}, bf16[768,64]{1,0:T(8,128)(2,1)S(1)}, u32[]{:S(2)}, u32[]{:S(2)}) %collective-permute-start.10) | collective-permute-done | bytes 98336 | tf_op jit(solution)/shard_map/ppermute | solution.py:435
  165.2 2.8 %shard_map.105.rest_1_ = bf16[768,256]{1,0:T(8,128)(2,1)S(1)} custom-call(s32[2]{0:T(128)S(1)} %pad_add_fusion.8.place_ref, bf16[768,2048]{1,0:T(8,128)(2,1)S(1)} %copy-done, bf16[2048,8192]{1,0:T(8,128)(2,1)} %w_ref.23, bf16[768,1024]{1,0:T(8,128)(2,1)S(1)} %collective-permute-done.12.rest_0_, bf16[768,64]{1,0:T(8,128)(2,1)S(1)} %shard_map.104.rest_1_.chosen_ref), custom_call_target="tpu_custom_call" | custom-call | flops 2415919104 | bytes 3145728 | tf_op jit(solution)/shard_map/pallas_call | solution.py:65
  168.0 2.8 %shard_map.106.after_ref = bf16[768,256]{1,0:T(8,128)(2,1)S(1)} custom-call(s32[2]{0:T(128)S(1)} %pad_add_fusion.7.place_ref, bf16[768,2048]{1,0:T(8,128)(2,1)S(1)} %copy-done, bf16[2048,8192]{1,0:T(8,128)(2,1)} %w_ref.23, bf16[768,1024]{1,0:T(8,128)(2,1)S(1)} %collective-permute-done.11.rest_0_, bf16[768,256]{1,0:T(8,128)(2,1)S(1)} %shard_map.105.rest_1_), custom_call_target="tpu_custom_call" | custom-call | flops 2415919104 | bytes 3145728 | tf_op jit(solution)/shard_map/pallas_call | solution.py:65
  170.8 10.0 %collective-permute-done.17.rest_0_ = bf16[768,1024]{1,0:T(8,128)(2,1)S(1)} collective-permute-done((bf16[768,1024]{1,0:T(8,128)(2,1)S(1)}, bf16[768,1024]{1,0:T(8,128)(2,1)S(1)}, u32[]{:S(2)}, u32[]{:S(2)}) %collective-permute-start.17) | collective-permute-done | bytes 1572896 | tf_op jit(solution)/shard_map/ppermute | solution.py:373
  180.8 0.7 collective-permute-start.14
  181.5 12.7 %shard_map.107.own_ref = f32[768,2048]{1,0:T(8,128)S(1)} custom-call(s32[1]{0:T(128)} %bitcast.block_ref, s32[8]{0:T(128)S(1)} %get-tuple-element.36.id_ref, bf16[768,2048]{1,0:T(8,128)(2,1)S(1)} %copy-done, bf16[2048,8192]{1,0:T(8,128)(2,1)} %w_ref.23, bf16[768,64]{1,0:T(8,128)(2,1)S(1)} %shard_map.104.rest_1_.chosen_ref, s32[768,1]{1,0:T(8,128)S(1)} %copy-done.5, ...), custom_call_target="tpu_custom_call" | custom-call | flops 24159191040 | bytes 50331648 | tf_op jit(solution)/shard_map/pallas_call | solution.py:260
  194.2 1.8 shard_map.108.rest_2_
  196.0 10.0 %collective-permute-done.15.rest_0_ = bf16[768,768]{1,0:T(8,128)(2,1)S(1)} collective-permute-done((bf16[768,768]{1,0:T(8,128)(2,1)S(1)}, bf16[768,768]{1,0:T(8,128)(2,1)S(1)}, u32[]{:S(2)}, u32[]{:S(2)}) %collective-permute-start.15) | collective-permute-done | bytes 1179680 | tf_op jit(solution)/shard_map/ppermute | solution.py:373
  206.1 2.0 shard_map.109.rest_2_
  208.0 5.3 %collective-permute-done.13.rest_0_ = bf16[768,256]{1,0:T(8,128)(2,1)S(1)} collective-permute-done((bf16[768,256]{1,0:T(8,128)(2,1)S(1)}, bf16[768,256]{1,0:T(8,128)(2,1)S(1)}, u32[]{:S(2)}, u32[]{:S(2)}) %collective-permute-start.13) | collective-permute-done | bytes 393248 | tf_op jit(solution)/shard_map/ppermute | solution.py:373
  213.3 0.9 shard_map.110
  (40 shorter events, 0.7 us)
Async XLA Ops:
  0.0 6.7 %copy-start = (bf16[768,2048]{1,0:T(8,128)(2,1)S(1)}, bf16[768,2048]{1,0:T(8,128)(2,1)}, u32[]{:S(2)}) copy-start(bf16[768,2048]{1,0:T(8,128)(2,1)} %a_ref.25) | copy-start | bytes 9437188
  3.7 34.0 %collective-permute-start.3 = (bf16[768,256]{1,0:T(8,128)(2,1)}, bf16[768,256]{1,0:T(8,128)(2,1)S(1)}, u32[]{:S(2)}, u32[]{:S(2)}) collective-permute-start(bf16[768,256]{1,0:T(8,128)(2,1)} %get-tuple-element.16), channel_id=1, source_target_pairs={{0,1},{3,2},{1,0},{2,3},{4,5},{7,6},{5,4},{6,7},{8,9},{11,10},{9,8... | collective-permute-start | bytes 1179656 | tf_op jit(solution)/shard_map/ppermute | solution.py:373
  6.7 0.7 copy-start.6
  12.8 29.5 %collective-permute-start.4 = (bf16[768,768]{1,0:T(8,128)(2,1)}, bf16[768,768]{1,0:T(8,128)(2,1)}, u32[]{:S(2)}, u32[]{:S(2)}) collective-permute-start(bf16[768,768]{1,0:T(8,128)(2,1)} %shard_map.92.rest_0_), channel_id=1, source_target_pairs={{0,1},{3,2},{1,0},{2,3},{4,5},{7,6},{5,4},{6,7},{8,9},{11,10},{9,8... | collective-permute-start | bytes 3538952 | tf_op jit(solution)/shard_map/ppermute | solution.py:373
  12.8 8.4 %copy-start.9 = (s32[4,4]{1,0:T(4,128)S(1)}, s32[4,4]{1,0:T(4,128)}, u32[]{:S(2)}) copy-start(s32[4,4]{1,0:T(4,128)} %param.15) | copy-start | bytes 196
  12.8 8.4 %copy-start.10 = (s32[32]{0:T(128)S(1)}, s32[32]{0:T(128)}, u32[]{:S(2)}) copy-start(s32[32]{0:T(128)} %param.16) | copy-start | bytes 388
  19.2 63.9 %collective-permute-start.6 = (bf16[768,1024]{1,0:T(8,128)(2,1)}, bf16[768,1024]{1,0:T(8,128)(2,1)}, u32[]{:S(2)}, u32[]{:S(2)}) collective-permute-start(bf16[768,1024]{1,0:T(8,128)(2,1)} %shard_map.93.refs_3_), channel_id=1, source_target_pairs={{0,1},{3,2},{1,0},{2,3},{4,5},{7,6},{5,4},{6,7},{8,9},{11,10},{9,8... | collective-permute-start | bytes 4718600 | tf_op jit(solution)/shard_map/ppermute | solution.py:373
  23.8 2.2 %copy-start.1 = (bf16[8,2,64,2048]{3,2,1,0:T(8,128)(2,1)S(1)}, bf16[8,2,64,2048]{3,2,1,0:T(8,128)(2,1)}, u32[]{:S(2)}) copy-start(bf16[8,2,64,2048]{3,2,1,0:T(8,128)(2,1)} %rest_1_.1) | copy-start | bytes 12582916
  26.0 6.8 %copy-start.8 = (s32[768]{0:T(1024)S(1)}, s32[768]{0:T(1024)}, u32[]{:S(2)}) copy-start(s32[768]{0:T(1024)} %param.17) | copy-start | bytes 9220
  28.0 1.0 copy-start.3
  29.1 26.4 %collective-permute-start.1 = (bf16[2,2,64,2048]{3,2,1,0:T(8,128)(2,1)}, bf16[2,2,64,2048]{3,2,1,0:T(8,128)(2,1)}, u32[]{:S(2)}, u32[]{:S(2)}) collective-permute-start(bf16[2,2,64,2048]{3,2,1,0:T(8,128)(2,1)} %get-tuple-element.14), channel_id=1, source_target_pairs={{0,8},{4,12},{8,0},{12,4},{1,9},{5,13},{9,1},{13,5},{2,10},{6,14},... | collective-permute-start | bytes 3145736 | tf_op jit(solution)/shard_map/ppermute | solution.py:428
  30.6 44.4 %collective-permute-start.2 = (bf16[2,2,64,2048]{3,2,1,0:T(8,128)(2,1)}, bf16[2,2,64,2048]{3,2,1,0:T(8,128)(2,1)}, u32[]{:S(2)}, u32[]{:S(2)}) collective-permute-start(bf16[2,2,64,2048]{3,2,1,0:T(8,128)(2,1)} %get-tuple-element.15), channel_id=1, source_target_pairs={{0,12},{4,8},{8,4},{12,0},{1,13},{5,9},{9,5},{13,1},{2,14},{6,10},... | collective-permute-start | bytes 3145736 | tf_op jit(solution)/shard_map/ppermute | solution.py:428
  37.7 37.2 %copy-start.2 = (bf16[8,2,64,2048]{3,2,1,0:T(8,128)(2,1)S(1)}, bf16[8,2,64,2048]{3,2,1,0:T(8,128)(2,1)}, u32[]{:S(2)}) copy-start(bf16[8,2,64,2048]{3,2,1,0:T(8,128)(2,1)} %rest_1_.1) | copy-start | bytes 12582916
  37.7 37.2 %collective-permute-start = (bf16[2,2,64,2048]{3,2,1,0:T(8,128)(2,1)}, bf16[2,2,64,2048]{3,2,1,0:T(8,128)(2,1)S(1)}, u32[]{:S(2)}, u32[]{:S(2)}) collective-permute-start(bf16[2,2,64,2048]{3,2,1,0:T(8,128)(2,1)} %copy-done.3), channel_id=1, source_target_pairs={{0,4},{4,0},{8,12},{12,8},{1,5},{5,1},{9,13},{13,9},{2,6},{6,2},{1... | collective-permute-start | bytes 3145736 | tf_op jit(solution)/shard_map/ppermute | solution.py:428
  42.3 1.2 copy-start.4
  43.5 31.5 %copy-start.5 = (s32[768,1]{1,0:T(8,128)S(1)}, s32[768,1]{1,0:T(8,128)}, u32[]{:S(2)}) copy-start(s32[768,1]{1,0:T(8,128)} %broadcast_in_dim.86.wanted_ref) | copy-start | bytes 9220
  43.5 31.5 %copy-start.7 = (bf16[8,2,64,2048]{3,2,1,0:T(8,128)(2,1)S(1)}, bf16[8,2,64,2048]{3,2,1,0:T(8,128)(2,1)}, u32[]{:S(2)}) copy-start(bf16[8,2,64,2048]{3,2,1,0:T(8,128)(2,1)} %rest_0_.1) | copy-start | bytes 12582916
  50.2 63.9 %collective-permute-start.9 = (bf16[768,1024]{1,0:T(8,128)(2,1)S(1)}, bf16[768,1024]{1,0:T(8,128)(2,1)S(1)}, u32[]{:S(2)}, u32[]{:S(2)}) collective-permute-start(bf16[768,1024]{1,0:T(8,128)(2,1)S(1)} %shard_map.95.rest_5_), channel_id=1, source_target_pairs={{1,2},{2,1},{5,6},{6,5},{9,10},{10,9},{13,14},{14,13},{17,18},{18,... | collective-permute-start | bytes 4718600 | tf_op jit(solution)/shard_map/ppermute | solution.py:375
  55.5 70.1 %collective-permute-start.8 = (bf16[768,1024]{1,0:T(8,128)(2,1)S(1)}, bf16[768,1024]{1,0:T(8,128)(2,1)S(1)}, u32[]{:S(2)}, u32[]{:S(2)}) collective-permute-start(bf16[768,1024]{1,0:T(8,128)(2,1)S(1)} %shard_map.95.rest_5_), channel_id=1, source_target_pairs={{0,1},{3,2},{4,5},{7,6},{8,9},{11,10},{12,13},{15,14},{16,17},{19,... | collective-permute-start | bytes 4718600 | tf_op jit(solution)/shard_map/ppermute | solution.py:373
  80.7 32.6 %collective-permute-start.5 = (bf16[768,64]{1,0:T(8,128)(2,1)S(1)}, bf16[768,64]{1,0:T(8,128)(2,1)S(1)}, u32[]{:S(2)}, u32[]{:S(2)}) collective-permute-start(bf16[768,64]{1,0:T(8,128)(2,1)S(1)} %get-tuple-element.17.rest_1_.mine_ref), channel_id=1, source_target_pairs={{0,1},{3,2},{4,5},{7,6},{8,9},{11,10},{12,13},{15,14},{16,17},{19,... | collective-permute-start | bytes 294920 | tf_op jit(solution)/shard_map/ppermute | solution.py:435
  89.5 44.6 %collective-permute-start.12 = (bf16[768,1024]{1,0:T(8,128)(2,1)S(1)}, bf16[768,1024]{1,0:T(8,128)(2,1)S(1)}, u32[]{:S(2)}, u32[]{:S(2)}) collective-permute-start(bf16[768,1024]{1,0:T(8,128)(2,1)S(1)} %shard_map.97.after_ref), channel_id=1, source_target_pairs={{1,2},{2,1},{5,6},{6,5},{9,10},{10,9},{13,14},{14,13},{17,18},{18,... | collective-permute-start | bytes 4718600 | tf_op jit(solution)/shard_map/ppermute | solution.py:375
  90.3 56.8 %collective-permute-start.11 = (bf16[768,1024]{1,0:T(8,128)(2,1)S(1)}, bf16[768,1024]{1,0:T(8,128)(2,1)S(1)}, u32[]{:S(2)}, u32[]{:S(2)}) collective-permute-start(bf16[768,1024]{1,0:T(8,128)(2,1)S(1)} %shard_map.97.after_ref), channel_id=1, source_target_pairs={{0,1},{3,2},{4,5},{7,6},{8,9},{11,10},{12,13},{15,14},{16,17},{19,... | collective-permute-start | bytes 4718600 | tf_op jit(solution)/shard_map/ppermute | solution.py:373
  113.4 19.1 %collective-permute-start.7 = (bf16[768,64]{1,0:T(8,128)(2,1)S(1)}, bf16[768,64]{1,0:T(8,128)(2,1)S(1)}, u32[]{:S(2)}, u32[]{:S(2)}) collective-permute-start(bf16[768,64]{1,0:T(8,128)(2,1)S(1)} %shard_map.98.rest_1_.mine_ref), channel_id=1, source_target_pairs={{1,2},{2,1},{5,6},{6,5},{9,10},{10,9},{13,14},{14,13},{17,18},{18,... | collective-permute-start | bytes 294920 | tf_op jit(solution)/shard_map/ppermute | solution.py:435
  120.4 60.4 %collective-permute-start.17 = (bf16[768,1024]{1,0:T(8,128)(2,1)S(1)}, bf16[768,1024]{1,0:T(8,128)(2,1)S(1)}, u32[]{:S(2)}, u32[]{:S(2)}) collective-permute-start(bf16[768,1024]{1,0:T(8,128)(2,1)S(1)} %shard_map.99.rest_1_), channel_id=1, source_target_pairs={{0,1},{1,0},{2,3},{3,2},{4,5},{5,4},{6,7},{7,6},{8,9},{9,8},{10,11... | collective-permute-start | bytes 4718600 | tf_op jit(solution)/shard_map/ppermute | solution.py:373
  131.8 62.4 %collective-permute-start.18 = (bf16[768,1024]{1,0:T(8,128)(2,1)S(1)}, bf16[768,1024]{1,0:T(8,128)(2,1)S(1)}, u32[]{:S(2)}, u32[]{:S(2)}) collective-permute-start(bf16[768,1024]{1,0:T(8,128)(2,1)S(1)} %shard_map.100.after_ref), channel_id=1, source_target_pairs={{1,2},{2,1},{5,6},{6,5},{9,10},{10,9},{13,14},{14,13},{17,18},{18,... | collective-permute-start | bytes 4718600 | tf_op jit(solution)/shard_map/ppermute | solution.py:375
  132.7 32.4 %collective-permute-start.10 = (bf16[768,64]{1,0:T(8,128)(2,1)S(1)}, bf16[768,64]{1,0:T(8,128)(2,1)S(1)}, u32[]{:S(2)}, u32[]{:S(2)}) collective-permute-start(bf16[768,64]{1,0:T(8,128)(2,1)S(1)} %shard_map.101.rest_1_.mine_ref), channel_id=1, source_target_pairs={{1,0},{2,3},{5,4},{6,7},{9,8},{10,11},{13,12},{14,15},{17,16},{18,... | collective-permute-start | bytes 294920 | tf_op jit(solution)/shard_map/ppermute | solution.py:435
  139.2 66.8 %collective-permute-start.15 = (bf16[768,768]{1,0:T(8,128)(2,1)S(1)}, bf16[768,768]{1,0:T(8,128)(2,1)S(1)}, u32[]{:S(2)}, u32[]{:S(2)}) collective-permute-start(bf16[768,768]{1,0:T(8,128)(2,1)S(1)} %shard_map.102.rest_1_), channel_id=1, source_target_pairs={{0,1},{1,0},{2,3},{3,2},{4,5},{5,4},{6,7},{7,6},{8,9},{9,8},{10,11... | collective-permute-start | bytes 3538952 | tf_op jit(solution)/shard_map/ppermute | solution.py:373
  152.1 43.9 %collective-permute-start.16 = (bf16[768,768]{1,0:T(8,128)(2,1)S(1)}, bf16[768,768]{1,0:T(8,128)(2,1)S(1)}, u32[]{:S(2)}, u32[]{:S(2)}) collective-permute-start(bf16[768,768]{1,0:T(8,128)(2,1)S(1)} %shard_map.103.after_ref), channel_id=1, source_target_pairs={{1,2},{2,1},{5,6},{6,5},{9,10},{10,9},{13,14},{14,13},{17,18},{18,... | collective-permute-start | bytes 3538952 | tf_op jit(solution)/shard_map/ppermute | solution.py:375
  167.9 45.4 %collective-permute-start.13 = (bf16[768,256]{1,0:T(8,128)(2,1)S(1)}, bf16[768,256]{1,0:T(8,128)(2,1)S(1)}, u32[]{:S(2)}, u32[]{:S(2)}) collective-permute-start(bf16[768,256]{1,0:T(8,128)(2,1)S(1)} %shard_map.105.rest_1_), channel_id=1, source_target_pairs={{0,1},{1,0},{2,3},{3,2},{4,5},{5,4},{6,7},{7,6},{8,9},{9,8},{10,11... | collective-permute-start | bytes 1179656 | tf_op jit(solution)/shard_map/ppermute | solution.py:373
  180.8 27.3 %collective-permute-start.14 = (bf16[768,256]{1,0:T(8,128)(2,1)S(1)}, bf16[768,256]{1,0:T(8,128)(2,1)S(1)}, u32[]{:S(2)}, u32[]{:S(2)}) collective-permute-start(bf16[768,256]{1,0:T(8,128)(2,1)S(1)} %shard_map.106.after_ref), channel_id=1, source_target_pairs={{1,2},{2,1},{5,6},{6,5},{9,10},{10,9},{13,14},{14,13},{17,18},{18,... | collective-permute-start | bytes 1179656 | tf_op jit(solution)/shard_map/ppermute | solution.py:375

commit v5 on v4

--- a/solution.py
+++ b/solution.py
@@ -157,6 +157,16 @@
     )(rows, *[store] * count, after)
 
 
+def packed(values, rows):
+    parts = [values[n : n + rows] for n in range(0, values.shape[0], rows)]
+    return jnp.concatenate(parts, axis=1)
+
+
+def unpacked(values, columns):
+    parts = [values[:, n : n + columns] for n in range(0, values.shape[1], columns)]
+    return jnp.concatenate(parts, axis=0)
+
+
 def slots_kernel(count, kind_ref, index_ref, id_ref, a_ref, wanted_ref, *rest):
     from_refs = rest[:count]
     mine_ref, expand_ref, factors = rest[-3:]
@@ -176,16 +186,18 @@
         shrunk = lax.dot_general(
             a_ref[...], factors[...], (((1,), (1,)), ((), ())), preferred_element_type=jnp.float32
         )
-        total = jnp.zeros(mine_ref.shape, jnp.float32)
+        total = jnp.zeros((a_ref.shape[0], rank), jnp.float32)
         for n in range(factors.shape[0] // rank):
             total += jnp.where(wanted_ref[...] == id_ref[n], shrunk[:, n * rank : (n + 1) * rank], 0.0)
-        mine_ref[...] = total.astype(mine_ref.dtype)
+        mine_ref[...] = packed(total.astype(mine_ref.dtype), mine_ref.shape[0])
 
 
 def hold_slots(attn, wanted, ids, kind, index, sources, after):
     rows, depth = attn.shape
     slots = ids.shape[0]
     rank, width = sources[0].shape[2:]
+    beside = max(1, 128 // rank)
+    small = (rows // beside, rank * beside)
 
     def from_spec(n):
         return pl.BlockSpec(
@@ -204,13 +216,13 @@
             + [from_spec(n) for n in range(len(sources))]
             + [ORDER],
             out_specs=[
-                pl.BlockSpec((rows, rank), lambda s, *_: (0, 0)),
+                pl.BlockSpec(small, lambda s, *_: (0, 0)),
                 pl.BlockSpec((1, rank, width), lambda s, *_: (s, 0, 0)),
             ],
             scratch_shapes=[pltpu.VMEM((slots * rank, width), jnp.bfloat16)],
         ),
         out_shape=[
-            jax.ShapeDtypeStruct((rows, rank), jnp.bfloat16),
+            jax.ShapeDtypeStruct(small, jnp.bfloat16),
             jax.ShapeDtypeStruct((slots, rank, width), jnp.bfloat16),
         ],
         compiler_params=params(),
@@ -240,8 +252,8 @@
 def own_kernel(block_ref, id_ref, a_ref, w_ref, chosen_ref, wanted_ref, expand_ref, after_ref, out_ref, masked):
     @pl.when(pl.program_id(0) == 0)
     def _():
-        chosen = chosen_ref[...]
-        rank = chosen.shape[1]
+        rank = chosen_ref.size // wanted_ref.shape[0]
+        chosen = unpacked(chosen_ref[...], rank)
         for n in range(masked.shape[1] // rank):
             masked[:, n * rank : (n + 1) * rank] = jnp.where(
                 wanted_ref[...] == id_ref[n], chosen, jnp.zeros_like(chosen)

time: 215 us -> 213 us (level)
    ppermute x3, waiting for transfers between devices: 30.1 us -> 25.8 us  [send_mine(): state['theirs'] = lax.ppermute(state['mine'], 'tensor', pairs)]
    ppermute x8, waiting for transfers between devices: 34.3 us -> 36.6 us  [step_of(): xs.append((span, lax.ppermute(for_x, 'tensor', pairs)))]
where the time goes in v5:
time: 213 us; the launch traced here: 212 us
  waiting for transfers between devices  84 us (39%)
  Pallas kernels  81.9 us (38%)
  starting transfers between devices  30.9 us (15%)
  local copies, waits for them, and re-layouts  8.27 us (4%)
  other arithmetic  6.8 us (3%)
    pallas_call x10, Pallas kernels, term(): pl.pallas_call(functools.partial(term_kernel, ranges), grid_spec=pltpu.Pr...  52.9 us
    ppermute x8, waiting for transfers between devices, step_of(): xs.append((span, lax.ppermute(for_x, 'tensor', pairs)))  36.6 us
    ppermute x3, waiting for transfers between devices, send_mine(): state['theirs'] = lax.ppermute(state['mine'], 'tensor', pairs)  25.8 us
    ppermute x3, waiting for transfers between devices, fetch(): sources.insert(2, lax.ppermute(piece, 'replica', pairs))  21.6 us
    ppermute x8, starting transfers between devices, step_of(): xs.append((span, lax.ppermute(for_x, 'tensor', pairs)))  20.6 us
    pallas_call x1, Pallas kernels, own_term(): pl.pallas_call(own_kernel, grid_spec=pltpu.PrefetchScalarGridSpec(num_sca...  12.7 us
    pallas_call x1, Pallas kernels, hold_slots(): pl.pallas_call(functools.partial(slots_kernel, len(sources)), grid_spec=p...  5.76 us
    unnamed x22, local copies, waits for them, and re-layouts  5.18 us
  transfers between devices with their start and end apart: 19, of which 9 were waited for; matrix products, arithmetic and copies ran while one was open for 5% of the time, Pallas kernels for 36%

profile of v5, /device:TPU:0, one launch (start us, length us, event | category | flops | bytes accessed | tf_op | source)
XLA Modules:
  0.0 212.1 jit_solution(12417053530768296898)
XLA Ops:
  0.0 3.7 %shard_map.91 = (bf16[768,256]{1,0:T(8,128)(2,1)}, f32[8,128]{1,0:T(8,128)}) custom-call(s32[1]{0:T(128)} %bitcast.9.place_ref, bf16[768,2048]{1,0:T(8,128)(2,1)} %a_ref.25, bf16[2048,8192]{1,0:T(8,128)(2,1)} %w_ref.23), custom_call_target="tpu_custom_call" | custom-call | flops 2415919104 | bytes 3145728 | tf_op jit(solution)/shard_map/pallas_call | solution.py:99
  3.7 3.0 %collective-permute-start.3 = (bf16[768,256]{1,0:T(8,128)(2,1)}, bf16[768,256]{1,0:T(8,128)(2,1)S(1)}, u32[]{:S(2)}, u32[]{:S(2)}) collective-permute-start(bf16[768,256]{1,0:T(8,128)(2,1)} %get-tuple-element.16), channel_id=1, source_target_pairs={{0,1},{3,2},{1,0},{2,3},{4,5},{7,6},{5,4},{6,7},{8,9},{11,10},{9,8... | collective-permute-start | bytes 1179656 | tf_op jit(solution)/shard_map/ppermute | solution.py:385
  6.7 0.7 copy-done.6
  7.4 5.3 %shard_map.92.rest_0_ = bf16[768,768]{1,0:T(8,128)(2,1)} custom-call(s32[1]{0:T(128)} %bitcast.8.place_ref, bf16[768,2048]{1,0:T(8,128)(2,1)S(1)} %copy-done, bf16[2048,8192]{1,0:T(8,128)(2,1)} %w_ref.23, f32[8,128]{1,0:T(8,128)S(1)} %copy-done.6), custom_call_target="tpu_custom_call" | custom-call | flops 7247757312 | bytes 9437184 | tf_op jit(solution)/shard_map/pallas_call | solution.py:65
  12.8 6.4 %shard_map.93.refs_3_ = bf16[768,1024]{1,0:T(8,128)(2,1)} custom-call(s32[1]{0:T(128)} %bitcast.7.place_ref, bf16[768,2048]{1,0:T(8,128)(2,1)S(1)} %copy-done, bf16[2048,8192]{1,0:T(8,128)(2,1)} %w_ref.23, bf16[768,768]{1,0:T(8,128)(2,1)} %shard_map.92.rest_0_), custom_call_target="tpu_custom_call" | custom-call | flops 9663676416 | bytes 12582912 | tf_op jit(solution)/shard_map/pallas_call | solution.py:65
  19.2 2.0 collective-permute-start.6
  21.2 0.2 select_reduce_fusion
  21.4 0.5 broadcast_compare_fusion
  22.0 0.8 convert_reduce_fusion
  22.8 0.7 select_reduce_fusion.1
  23.5 0.2 fusion.3
  23.7 0.1 pad_add_fusion.row_ref
  23.8 2.2 %copy-done.1 = bf16[8,2,64,2048]{3,2,1,0:T(8,128)(2,1)S(1)} copy-done((bf16[8,2,64,2048]{3,2,1,0:T(8,128)(2,1)S(1)}, bf16[8,2,64,2048]{3,2,1,0:T(8,128)(2,1)}, u32[]{:S(2)}) %copy-start.1) | copy-done | bytes 4194328
  26.0 2.0 shard_map.94
  28.0 1.0 copy-done.3
  29.1 1.5 collective-permute-start.1
  30.6 1.2 fusion.6
  31.7 0.5 add_bitcast_fusion
  32.2 0.6 fusion.8
  32.8 0.9 broadcast_in_dim.86.wanted_ref
  33.8 0.7 select_reduce_fusion.2
  34.5 0.7 fusion.1
  35.2 0.7 compare_select_fusion
  35.9 0.6 compare_select_fusion.1
  36.5 0.8 concatenate.6.index_ref
  37.3 0.1 pad_add_fusion.1.place_ref
  37.4 0.1 pad_add_fusion.2.place_ref
  37.7 0.7 collective-permute-start
  38.4 3.9 %collective-permute-done.4.rest_1_ = bf16[768,768]{1,0:T(8,128)(2,1)} collective-permute-done((bf16[768,768]{1,0:T(8,128)(2,1)}, bf16[768,768]{1,0:T(8,128)(2,1)}, u32[]{:S(2)}, u32[]{:S(2)}) %collective-permute-start.4) | collective-permute-done | bytes 1179680 | tf_op jit(solution)/shard_map/ppermute | solution.py:385
  42.3 1.2 copy-done.4
  43.5 6.7 %shard_map.95.rest_5_ = bf16[768,1024]{1,0:T(8,128)(2,1)S(1)} custom-call(s32[3]{0:T(128)S(1)} %pad_add_fusion.1.place_ref, bf16[768,2048]{1,0:T(8,128)(2,1)S(1)} %copy-done, bf16[2048,8192]{1,0:T(8,128)(2,1)} %w_ref.23, bf16[768,256]{1,0:T(8,128)(2,1)S(1)} %collective-permute-done.3.rest_0_, bf16[768,768]{1,0:T(8,128)(2,1)} %collective-permute-done.4.rest_1_, ...), custom_call_target="tpu_custom_call" | custom-call | flops 9663676416 | bytes 12582912 | tf_op jit(solution)/shard_map/pallas_call | solution.py:65
  50.2 0.8 collective-permute-start.9
  50.9 0.1 pad_add_fusion.6.place_ref
  51.1 4.4 %collective-permute-done.1.rest_3_ = bf16[2,2,64,2048]{3,2,1,0:T(8,128)(2,1)} collective-permute-done((bf16[2,2,64,2048]{3,2,1,0:T(8,128)(2,1)}, bf16[2,2,64,2048]{3,2,1,0:T(8,128)(2,1)}, u32[]{:S(2)}, u32[]{:S(2)}) %collective-permute-start.1) | collective-permute-done | bytes 1048608 | tf_op jit(solution)/shard_map/ppermute | solution.py:440
  55.5 2.3 %collective-permute-start.8 = (bf16[768,1024]{1,0:T(8,128)(2,1)S(1)}, bf16[768,1024]{1,0:T(8,128)(2,1)S(1)}, u32[]{:S(2)}, u32[]{:S(2)}) collective-permute-start(bf16[768,1024]{1,0:T(8,128)(2,1)S(1)} %shard_map.95.rest_5_), channel_id=1, source_target_pairs={{0,1},{3,2},{4,5},{7,6},{8,9},{11,10},{12,13},{15,14},{16,17},{19,... | collective-permute-start | bytes 4718600 | tf_op jit(solution)/shard_map/ppermute | solution.py:385
  57.8 17.2 %collective-permute-done.2.rest_4_ = bf16[2,2,64,2048]{3,2,1,0:T(8,128)(2,1)} collective-permute-done((bf16[2,2,64,2048]{3,2,1,0:T(8,128)(2,1)}, bf16[2,2,64,2048]{3,2,1,0:T(8,128)(2,1)}, u32[]{:S(2)}, u32[]{:S(2)}) %collective-permute-start.2) | collective-permute-done | bytes 1048608 | tf_op jit(solution)/shard_map/ppermute | solution.py:440
  75.0 5.8 %shard_map.96 = (bf16[384,128]{1,0:T(8,128)(2,1)S(1)}, bf16[8,64,2048]{2,1,0:T(8,128)(2,1)S(1)}) custom-call(s32[8]{0:T(128)S(1)} %get-tuple-element.29.kind_ref, s32[40]{0:T(128)S(1)} %concatenate.6.index_ref, s32[8]{0:T(128)S(1)} %get-tuple-element.36.id_ref, bf16[768,2048]{1,0:T(8,128)(2,1)S(1)} %copy-done, s32[768,1]{1,0:T(8,128)S(1)} %copy-done.5, ...), custom_call_target="tpu_custom_call" | custom-call | flops 4831838208 | bytes 18874368 | tf_op jit(solution)/shard_map/pallas_call | solution.py:207
  80.7 2.4 %collective-permute-start.5 = (bf16[384,128]{1,0:T(8,128)(2,1)S(1)}, bf16[384,128]{1,0:T(8,128)(2,1)S(1)}, u32[]{:S(2)}, u32[]{:S(2)}) collective-permute-start(bf16[384,128]{1,0:T(8,128)(2,1)S(1)} %get-tuple-element.17.rest_1_.mine_ref), channel_id=1, source_target_pairs={{0,1},{3,2},{4,5},{7,6},{8,9},{11,10},{12,13},{15,14},{16,17},{19,... | collective-permute-start | bytes 294920 | tf_op jit(solution)/shard_map/ppermute | solution.py:447
  83.1 6.4 %shard_map.97.after_ref = bf16[768,1024]{1,0:T(8,128)(2,1)S(1)} custom-call(s32[2]{0:T(128)S(1)} %pad_add_fusion.2.place_ref, bf16[768,2048]{1,0:T(8,128)(2,1)S(1)} %copy-done, bf16[2048,8192]{1,0:T(8,128)(2,1)} %w_ref.23, bf16[768,1024]{1,0:T(8,128)(2,1)} %collective-permute-done.6.rest_0_, bf16[384,128]{1,0:T(8,128)(2,1)S(1)} %get-tuple-element.17.rest_1_.mine_ref), custom_call_target="tpu_custom_call" | custom-call | flops 9663676416 | bytes 12582912 | tf_op jit(solution)/shard_map/pallas_call | solution.py:65
  89.5 0.8 collective-permute-start.12
  90.3 5.2 %collective-permute-start.11 = (bf16[768,1024]{1,0:T(8,128)(2,1)S(1)}, bf16[768,1024]{1,0:T(8,128)(2,1)S(1)}, u32[]{:S(2)}, u32[]{:S(2)}) collective-permute-start(bf16[768,1024]{1,0:T(8,128)(2,1)S(1)} %shard_map.97.after_ref), channel_id=1, source_target_pairs={{0,1},{3,2},{4,5},{7,6},{8,9},{11,10},{12,13},{15,14},{16,17},{19,... | collective-permute-start | bytes 4718600 | tf_op jit(solution)/shard_map/ppermute | solution.py:385
  95.5 15.7 %collective-permute-done.5.theirs_ref = bf16[384,128]{1,0:T(8,128)(2,1)S(1)} collective-permute-done((bf16[384,128]{1,0:T(8,128)(2,1)S(1)}, bf16[384,128]{1,0:T(8,128)(2,1)S(1)}, u32[]{:S(2)}, u32[]{:S(2)}) %collective-permute-start.5) | collective-permute-done | bytes 98336 | tf_op jit(solution)/shard_map/ppermute | solution.py:447
  111.3 0.7 collective-permute-start.7
  112.0 6.2 %shard_map.99.rest_1_ = bf16[768,1024]{1,0:T(8,128)(2,1)S(1)} custom-call(s32[2]{0:T(128)S(1)} %pad_add_fusion.4.place_ref, bf16[768,2048]{1,0:T(8,128)(2,1)S(1)} %copy-done, bf16[2048,8192]{1,0:T(8,128)(2,1)} %w_ref.23, bf16[768,1024]{1,0:T(8,128)(2,1)S(1)} %collective-permute-done.9.rest_0_, bf16[384,128]{1,0:T(8,128)(2,1)S(1)} %shard_map.98.rest_1_.mine_ref), custom_call_target="tpu_custom_call" | custom-call | flops 9663676416 | bytes 12582912 | tf_op jit(solution)/shard_map/pallas_call | solution.py:65
  118.2 5.2 %collective-permute-start.17 = (bf16[768,1024]{1,0:T(8,128)(2,1)S(1)}, bf16[768,1024]{1,0:T(8,128)(2,1)S(1)}, u32[]{:S(2)}, u32[]{:S(2)}) collective-permute-start(bf16[768,1024]{1,0:T(8,128)(2,1)S(1)} %shard_map.99.rest_1_), channel_id=1, source_target_pairs={{0,1},{1,0},{2,3},{3,2},{4,5},{5,4},{6,7},{7,6},{8,9},{9,8},{10,11... | collective-permute-start | bytes 4718600 | tf_op jit(solution)/shard_map/ppermute | solution.py:385
  123.4 6.2 %shard_map.100.after_ref = bf16[768,1024]{1,0:T(8,128)(2,1)S(1)} custom-call(s32[2]{0:T(128)S(1)} %pad_add_fusion.3.place_ref, bf16[768,2048]{1,0:T(8,128)(2,1)S(1)} %copy-done, bf16[2048,8192]{1,0:T(8,128)(2,1)} %w_ref.23, bf16[768,1024]{1,0:T(8,128)(2,1)S(1)} %collective-permute-done.8.rest_0_, bf16[768,1024]{1,0:T(8,128)(2,1)S(1)} %shard_map.99.rest_1_), custom_call_target="tpu_custom_call" | custom-call | flops 9663676416 | bytes 12582912 | tf_op jit(solution)/shard_map/pallas_call | solution.py:65
  129.7 0.8 collective-permute-start.18
  130.5 1.5 collective-permute-start.10
  132.0 5.1 %shard_map.102.rest_1_ = bf16[768,768]{1,0:T(8,128)(2,1)S(1)} custom-call(s32[2]{0:T(128)S(1)} %pad_add_fusion.6.place_ref, bf16[768,2048]{1,0:T(8,128)(2,1)S(1)} %copy-done, bf16[2048,8192]{1,0:T(8,128)(2,1)} %w_ref.23, bf16[768,1024]{1,0:T(8,128)(2,1)S(1)} %collective-permute-done.12.rest_0_, bf16[384,128]{1,0:T(8,128)(2,1)S(1)} %shard_map.101.rest_1_.mine_ref), custom_call_target="tpu_custom_call" | custom-call | flops 7247757312 | bytes 9437184 | tf_op jit(solution)/shard_map/pallas_call | solution.py:65
  137.0 2.7 %collective-permute-start.15 = (bf16[768,768]{1,0:T(8,128)(2,1)S(1)}, bf16[768,768]{1,0:T(8,128)(2,1)S(1)}, u32[]{:S(2)}, u32[]{:S(2)}) collective-permute-start(bf16[768,768]{1,0:T(8,128)(2,1)S(1)} %shard_map.102.rest_1_), channel_id=1, source_target_pairs={{0,1},{1,0},{2,3},{3,2},{4,5},{5,4},{6,7},{7,6},{8,9},{9,8},{10,11... | collective-permute-start | bytes 3538952 | tf_op jit(solution)/shard_map/ppermute | solution.py:385
  139.8 5.2 %collective-permute-done.11.rest_0_ = bf16[768,1024]{1,0:T(8,128)(2,1)S(1)} collective-permute-done((bf16[768,1024]{1,0:T(8,128)(2,1)S(1)}, bf16[768,1024]{1,0:T(8,128)(2,1)S(1)}, u32[]{:S(2)}, u32[]{:S(2)}) %collective-permute-start.11) | collective-permute-done | bytes 1572896 | tf_op jit(solution)/shard_map/ppermute | solution.py:385
  145.0 5.1 %shard_map.103.after_ref = bf16[768,768]{1,0:T(8,128)(2,1)S(1)} custom-call(s32[2]{0:T(128)S(1)} %pad_add_fusion.5.place_ref, bf16[768,2048]{1,0:T(8,128)(2,1)S(1)} %copy-done, bf16[2048,8192]{1,0:T(8,128)(2,1)} %w_ref.23, bf16[768,1024]{1,0:T(8,128)(2,1)S(1)} %collective-permute-done.11.rest_0_, bf16[768,768]{1,0:T(8,128)(2,1)S(1)} %shard_map.102.rest_1_), custom_call_target="tpu_custom_call" | custom-call | flops 7247757312 | bytes 9437184 | tf_op jit(solution)/shard_map/pallas_call | solution.py:65
  150.0 0.7 collective-permute-start.16
  150.8 10.1 %collective-permute-done.10.theirs_ref = bf16[384,128]{1,0:T(8,128)(2,1)S(1)} collective-permute-done((bf16[384,128]{1,0:T(8,128)(2,1)S(1)}, bf16[384,128]{1,0:T(8,128)(2,1)S(1)}, u32[]{:S(2)}, u32[]{:S(2)}) %collective-permute-start.10) | collective-permute-done | bytes 98336 | tf_op jit(solution)/shard_map/ppermute | solution.py:447
  160.9 2.8 %shard_map.105.rest_1_ = bf16[768,256]{1,0:T(8,128)(2,1)S(1)} custom-call(s32[2]{0:T(128)S(1)} %pad_add_fusion.8.place_ref, bf16[768,2048]{1,0:T(8,128)(2,1)S(1)} %copy-done, bf16[2048,8192]{1,0:T(8,128)(2,1)} %w_ref.23, bf16[768,1024]{1,0:T(8,128)(2,1)S(1)} %collective-permute-done.12.rest_0_, bf16[384,128]{1,0:T(8,128)(2,1)S(1)} %shard_map.104.rest_1_.chosen_ref), custom_call_target="tpu_custom_call" | custom-call | flops 2415919104 | bytes 3145728 | tf_op jit(solution)/shard_map/pallas_call | solution.py:65
  163.7 2.8 %shard_map.106.after_ref = bf16[768,256]{1,0:T(8,128)(2,1)S(1)} custom-call(s32[2]{0:T(128)S(1)} %pad_add_fusion.7.place_ref, bf16[768,2048]{1,0:T(8,128)(2,1)S(1)} %copy-done, bf16[2048,8192]{1,0:T(8,128)(2,1)} %w_ref.23, bf16[768,1024]{1,0:T(8,128)(2,1)S(1)} %collective-permute-done.11.rest_0_, bf16[768,256]{1,0:T(8,128)(2,1)S(1)} %shard_map.105.rest_1_), custom_call_target="tpu_custom_call" | custom-call | flops 2415919104 | bytes 3145728 | tf_op jit(solution)/shard_map/pallas_call | solution.py:65
  166.5 12.2 %collective-permute-done.17.rest_0_ = bf16[768,1024]{1,0:T(8,128)(2,1)S(1)} collective-permute-done((bf16[768,1024]{1,0:T(8,128)(2,1)S(1)}, bf16[768,1024]{1,0:T(8,128)(2,1)S(1)}, u32[]{:S(2)}, u32[]{:S(2)}) %collective-permute-start.17) | collective-permute-done | bytes 1572896 | tf_op jit(solution)/shard_map/ppermute | solution.py:385
  178.7 0.7 collective-permute-start.14
  179.4 12.7 %shard_map.107.own_ref = f32[768,2048]{1,0:T(8,128)S(1)} custom-call(s32[1]{0:T(128)} %bitcast.block_ref, s32[8]{0:T(128)S(1)} %get-tuple-element.36.id_ref, bf16[768,2048]{1,0:T(8,128)(2,1)S(1)} %copy-done, bf16[2048,8192]{1,0:T(8,128)(2,1)} %w_ref.23, bf16[384,128]{1,0:T(8,128)(2,1)S(1)} %shard_map.104.rest_1_.chosen_ref, s32[768,1]{1,0:T(8,128)S(1)} %copy-done.5, ...), custom_call_target="tpu_custom_call" | custom-call | flops 24159191040 | bytes 50331648 | tf_op jit(solution)/shard_map/pallas_call | solution.py:272
  192.1 1.8 shard_map.108.rest_2_
  193.9 10.0 %collective-permute-done.15.rest_0_ = bf16[768,768]{1,0:T(8,128)(2,1)S(1)} collective-permute-done((bf16[768,768]{1,0:T(8,128)(2,1)S(1)}, bf16[768,768]{1,0:T(8,128)(2,1)S(1)}, u32[]{:S(2)}, u32[]{:S(2)}) %collective-permute-start.15) | collective-permute-done | bytes 1179680 | tf_op jit(solution)/shard_map/ppermute | solution.py:385
  204.0 2.0 shard_map.109.rest_2_
  205.9 5.3 %collective-permute-done.13.rest_0_ = bf16[768,256]{1,0:T(8,128)(2,1)S(1)} collective-permute-done((bf16[768,256]{1,0:T(8,128)(2,1)S(1)}, bf16[768,256]{1,0:T(8,128)(2,1)S(1)}, u32[]{:S(2)}, u32[]{:S(2)}) %collective-permute-start.13) | collective-permute-done | bytes 393248 | tf_op jit(solution)/shard_map/ppermute | solution.py:385
  211.2 0.9 shard_map.110
  (40 shorter events, 0.6 us)
Async XLA Ops:
  0.0 6.7 %copy-start = (bf16[768,2048]{1,0:T(8,128)(2,1)S(1)}, bf16[768,2048]{1,0:T(8,128)(2,1)}, u32[]{:S(2)}) copy-start(bf16[768,2048]{1,0:T(8,128)(2,1)} %a_ref.25) | copy-start | bytes 9437188
  3.7 34.0 %collective-permute-start.3 = (bf16[768,256]{1,0:T(8,128)(2,1)}, bf16[768,256]{1,0:T(8,128)(2,1)S(1)}, u32[]{:S(2)}, u32[]{:S(2)}) collective-permute-start(bf16[768,256]{1,0:T(8,128)(2,1)} %get-tuple-element.16), channel_id=1, source_target_pairs={{0,1},{3,2},{1,0},{2,3},{4,5},{7,6},{5,4},{6,7},{8,9},{11,10},{9,8... | collective-permute-start | bytes 1179656 | tf_op jit(solution)/shard_map/ppermute | solution.py:385
  6.7 0.7 copy-start.6
  12.8 29.5 %collective-permute-start.4 = (bf16[768,768]{1,0:T(8,128)(2,1)}, bf16[768,768]{1,0:T(8,128)(2,1)}, u32[]{:S(2)}, u32[]{:S(2)}) collective-permute-start(bf16[768,768]{1,0:T(8,128)(2,1)} %shard_map.92.rest_0_), channel_id=1, source_target_pairs={{0,1},{3,2},{1,0},{2,3},{4,5},{7,6},{5,4},{6,7},{8,9},{11,10},{9,8... | collective-permute-start | bytes 3538952 | tf_op jit(solution)/shard_map/ppermute | solution.py:385
  12.8 8.4 %copy-start.9 = (s32[4,4]{1,0:T(4,128)S(1)}, s32[4,4]{1,0:T(4,128)}, u32[]{:S(2)}) copy-start(s32[4,4]{1,0:T(4,128)} %param.15) | copy-start | bytes 196
  12.8 8.4 %copy-start.10 = (s32[32]{0:T(128)S(1)}, s32[32]{0:T(128)}, u32[]{:S(2)}) copy-start(s32[32]{0:T(128)} %param.16) | copy-start | bytes 388
  19.2 63.9 %collective-permute-start.6 = (bf16[768,1024]{1,0:T(8,128)(2,1)}, bf16[768,1024]{1,0:T(8,128)(2,1)}, u32[]{:S(2)}, u32[]{:S(2)}) collective-permute-start(bf16[768,1024]{1,0:T(8,128)(2,1)} %shard_map.93.refs_3_), channel_id=1, source_target_pairs={{0,1},{3,2},{1,0},{2,3},{4,5},{7,6},{5,4},{6,7},{8,9},{11,10},{9,8... | collective-permute-start | bytes 4718600 | tf_op jit(solution)/shard_map/ppermute | solution.py:385
  23.8 2.2 %copy-start.1 = (bf16[8,2,64,2048]{3,2,1,0:T(8,128)(2,1)S(1)}, bf16[8,2,64,2048]{3,2,1,0:T(8,128)(2,1)}, u32[]{:S(2)}) copy-start(bf16[8,2,64,2048]{3,2,1,0:T(8,128)(2,1)} %rest_1_.1) | copy-start | bytes 12582916
  26.0 6.8 %copy-start.8 = (s32[768]{0:T(1024)S(1)}, s32[768]{0:T(1024)}, u32[]{:S(2)}) copy-start(s32[768]{0:T(1024)} %param.17) | copy-start | bytes 9220
  28.0 1.0 copy-start.3
  29.1 26.4 %collective-permute-start.1 = (bf16[2,2,64,2048]{3,2,1,0:T(8,128)(2,1)}, bf16[2,2,64,2048]{3,2,1,0:T(8,128)(2,1)}, u32[]{:S(2)}, u32[]{:S(2)}) collective-permute-start(bf16[2,2,64,2048]{3,2,1,0:T(8,128)(2,1)} %get-tuple-element.14), channel_id=1, source_target_pairs={{0,8},{4,12},{8,0},{12,4},{1,9},{5,13},{9,1},{13,5},{2,10},{6,14},... | collective-permute-start | bytes 3145736 | tf_op jit(solution)/shard_map/ppermute | solution.py:440
  30.6 44.4 %collective-permute-start.2 = (bf16[2,2,64,2048]{3,2,1,0:T(8,128)(2,1)}, bf16[2,2,64,2048]{3,2,1,0:T(8,128)(2,1)}, u32[]{:S(2)}, u32[]{:S(2)}) collective-permute-start(bf16[2,2,64,2048]{3,2,1,0:T(8,128)(2,1)} %get-tuple-element.15), channel_id=1, source_target_pairs={{0,12},{4,8},{8,4},{12,0},{1,13},{5,9},{9,5},{13,1},{2,14},{6,10},... | collective-permute-start | bytes 3145736 | tf_op jit(solution)/shard_map/ppermute | solution.py:440
  37.7 37.2 %copy-start.2 = (bf16[8,2,64,2048]{3,2,1,0:T(8,128)(2,1)S(1)}, bf16[8,2,64,2048]{3,2,1,0:T(8,128)(2,1)}, u32[]{:S(2)}) copy-start(bf16[8,2,64,2048]{3,2,1,0:T(8,128)(2,1)} %rest_1_.1) | copy-start | bytes 12582916
  37.7 37.2 %collective-permute-start = (bf16[2,2,64,2048]{3,2,1,0:T(8,128)(2,1)}, bf16[2,2,64,2048]{3,2,1,0:T(8,128)(2,1)S(1)}, u32[]{:S(2)}, u32[]{:S(2)}) collective-permute-start(bf16[2,2,64,2048]{3,2,1,0:T(8,128)(2,1)} %copy-done.3), channel_id=1, source_target_pairs={{0,4},{4,0},{8,12},{12,8},{1,5},{5,1},{9,13},{13,9},{2,6},{6,2},{1... | collective-permute-start | bytes 3145736 | tf_op jit(solution)/shard_map/ppermute | solution.py:440
  42.3 1.2 copy-start.4
  43.5 31.5 %copy-start.5 = (s32[768,1]{1,0:T(8,128)S(1)}, s32[768,1]{1,0:T(8,128)}, u32[]{:S(2)}) copy-start(s32[768,1]{1,0:T(8,128)} %broadcast_in_dim.86.wanted_ref) | copy-start | bytes 9220
  43.5 31.5 %copy-start.7 = (bf16[8,2,64,2048]{3,2,1,0:T(8,128)(2,1)S(1)}, bf16[8,2,64,2048]{3,2,1,0:T(8,128)(2,1)}, u32[]{:S(2)}) copy-start(bf16[8,2,64,2048]{3,2,1,0:T(8,128)(2,1)} %rest_0_.1) | copy-start | bytes 12582916
  50.2 61.8 %collective-permute-start.9 = (bf16[768,1024]{1,0:T(8,128)(2,1)S(1)}, bf16[768,1024]{1,0:T(8,128)(2,1)S(1)}, u32[]{:S(2)}, u32[]{:S(2)}) collective-permute-start(bf16[768,1024]{1,0:T(8,128)(2,1)S(1)} %shard_map.95.rest_5_), channel_id=1, source_target_pairs={{1,2},{2,1},{5,6},{6,5},{9,10},{10,9},{13,14},{14,13},{17,18},{18,... | collective-permute-start | bytes 4718600 | tf_op jit(solution)/shard_map/ppermute | solution.py:387
  55.5 67.9 %collective-permute-start.8 = (bf16[768,1024]{1,0:T(8,128)(2,1)S(1)}, bf16[768,1024]{1,0:T(8,128)(2,1)S(1)}, u32[]{:S(2)}, u32[]{:S(2)}) collective-permute-start(bf16[768,1024]{1,0:T(8,128)(2,1)S(1)} %shard_map.95.rest_5_), channel_id=1, source_target_pairs={{0,1},{3,2},{4,5},{7,6},{8,9},{11,10},{12,13},{15,14},{16,17},{19,... | collective-permute-start | bytes 4718600 | tf_op jit(solution)/shard_map/ppermute | solution.py:385
  80.7 30.5 %collective-permute-start.5 = (bf16[384,128]{1,0:T(8,128)(2,1)S(1)}, bf16[384,128]{1,0:T(8,128)(2,1)S(1)}, u32[]{:S(2)}, u32[]{:S(2)}) collective-permute-start(bf16[384,128]{1,0:T(8,128)(2,1)S(1)} %get-tuple-element.17.rest_1_.mine_ref), channel_id=1, source_target_pairs={{0,1},{3,2},{4,5},{7,6},{8,9},{11,10},{12,13},{15,14},{16,17},{19,... | collective-permute-start | bytes 294920 | tf_op jit(solution)/shard_map/ppermute | solution.py:447
  89.5 42.5 %collective-permute-start.12 = (bf16[768,1024]{1,0:T(8,128)(2,1)S(1)}, bf16[768,1024]{1,0:T(8,128)(2,1)S(1)}, u32[]{:S(2)}, u32[]{:S(2)}) collective-permute-start(bf16[768,1024]{1,0:T(8,128)(2,1)S(1)} %shard_map.97.after_ref), channel_id=1, source_target_pairs={{1,2},{2,1},{5,6},{6,5},{9,10},{10,9},{13,14},{14,13},{17,18},{18,... | collective-permute-start | bytes 4718600 | tf_op jit(solution)/shard_map/ppermute | solution.py:387
  90.3 54.7 %collective-permute-start.11 = (bf16[768,1024]{1,0:T(8,128)(2,1)S(1)}, bf16[768,1024]{1,0:T(8,128)(2,1)S(1)}, u32[]{:S(2)}, u32[]{:S(2)}) collective-permute-start(bf16[768,1024]{1,0:T(8,128)(2,1)S(1)} %shard_map.97.after_ref), channel_id=1, source_target_pairs={{0,1},{3,2},{4,5},{7,6},{8,9},{11,10},{12,13},{15,14},{16,17},{19,... | collective-permute-start | bytes 4718600 | tf_op jit(solution)/shard_map/ppermute | solution.py:385
  111.3 19.1 %collective-permute-start.7 = (bf16[384,128]{1,0:T(8,128)(2,1)S(1)}, bf16[384,128]{1,0:T(8,128)(2,1)S(1)}, u32[]{:S(2)}, u32[]{:S(2)}) collective-permute-start(bf16[384,128]{1,0:T(8,128)(2,1)S(1)} %shard_map.98.rest_1_.mine_ref), channel_id=1, source_target_pairs={{1,2},{2,1},{5,6},{6,5},{9,10},{10,9},{13,14},{14,13},{17,18},{18,... | collective-permute-start | bytes 294920 | tf_op jit(solution)/shard_map/ppermute | solution.py:447
  118.2 60.5 %collective-permute-start.17 = (bf16[768,1024]{1,0:T(8,128)(2,1)S(1)}, bf16[768,1024]{1,0:T(8,128)(2,1)S(1)}, u32[]{:S(2)}, u32[]{:S(2)}) collective-permute-start(bf16[768,1024]{1,0:T(8,128)(2,1)S(1)} %shard_map.99.rest_1_), channel_id=1, source_target_pairs={{0,1},{1,0},{2,3},{3,2},{4,5},{5,4},{6,7},{7,6},{8,9},{9,8},{10,11... | collective-permute-start | bytes 4718600 | tf_op jit(solution)/shard_map/ppermute | solution.py:385
  129.7 62.4 %collective-permute-start.18 = (bf16[768,1024]{1,0:T(8,128)(2,1)S(1)}, bf16[768,1024]{1,0:T(8,128)(2,1)S(1)}, u32[]{:S(2)}, u32[]{:S(2)}) collective-permute-start(bf16[768,1024]{1,0:T(8,128)(2,1)S(1)} %shard_map.100.after_ref), channel_id=1, source_target_pairs={{1,2},{2,1},{5,6},{6,5},{9,10},{10,9},{13,14},{14,13},{17,18},{18,... | collective-permute-start | bytes 4718600 | tf_op jit(solution)/shard_map/ppermute | solution.py:387
  130.5 30.4 %collective-permute-start.10 = (bf16[384,128]{1,0:T(8,128)(2,1)S(1)}, bf16[384,128]{1,0:T(8,128)(2,1)S(1)}, u32[]{:S(2)}, u32[]{:S(2)}) collective-permute-start(bf16[384,128]{1,0:T(8,128)(2,1)S(1)} %shard_map.101.rest_1_.mine_ref), channel_id=1, source_target_pairs={{1,0},{2,3},{5,4},{6,7},{9,8},{10,11},{13,12},{14,15},{17,16},{18,... | collective-permute-start | bytes 294920 | tf_op jit(solution)/shard_map/ppermute | solution.py:447
  137.0 66.9 %collective-permute-start.15 = (bf16[768,768]{1,0:T(8,128)(2,1)S(1)}, bf16[768,768]{1,0:T(8,128)(2,1)S(1)}, u32[]{:S(2)}, u32[]{:S(2)}) collective-permute-start(bf16[768,768]{1,0:T(8,128)(2,1)S(1)} %shard_map.102.rest_1_), channel_id=1, source_target_pairs={{0,1},{1,0},{2,3},{3,2},{4,5},{5,4},{6,7},{7,6},{8,9},{9,8},{10,11... | collective-permute-start | bytes 3538952 | tf_op jit(solution)/shard_map/ppermute | solution.py:385
  150.0 43.9 %collective-permute-start.16 = (bf16[768,768]{1,0:T(8,128)(2,1)S(1)}, bf16[768,768]{1,0:T(8,128)(2,1)S(1)}, u32[]{:S(2)}, u32[]{:S(2)}) collective-permute-start(bf16[768,768]{1,0:T(8,128)(2,1)S(1)} %shard_map.103.after_ref), channel_id=1, source_target_pairs={{1,2},{2,1},{5,6},{6,5},{9,10},{10,9},{13,14},{14,13},{17,18},{18,... | collective-permute-start | bytes 3538952 | tf_op jit(solution)/shard_map/ppermute | solution.py:387
  163.7 47.6 %collective-permute-start.13 = (bf16[768,256]{1,0:T(8,128)(2,1)S(1)}, bf16[768,256]{1,0:T(8,128)(2,1)S(1)}, u32[]{:S(2)}, u32[]{:S(2)}) collective-permute-start(bf16[768,256]{1,0:T(8,128)(2,1)S(1)} %shard_map.105.rest_1_), channel_id=1, source_target_pairs={{0,1},{1,0},{2,3},{3,2},{4,5},{5,4},{6,7},{7,6},{8,9},{9,8},{10,11... | collective-permute-start | bytes 1179656 | tf_op jit(solution)/shard_map/ppermute | solution.py:385
  178.7 27.3 %collective-permute-start.14 = (bf16[768,256]{1,0:T(8,128)(2,1)S(1)}, bf16[768,256]{1,0:T(8,128)(2,1)S(1)}, u32[]{:S(2)}, u32[]{:S(2)}) collective-permute-start(bf16[768,256]{1,0:T(8,128)(2,1)S(1)} %shard_map.106.after_ref), channel_id=1, source_target_pairs={{1,2},{2,1},{5,6},{6,5},{9,10},{10,9},{13,14},{14,13},{17,18},{18,... | collective-permute-start | bytes 1179656 | tf_op jit(solution)/shard_map/ppermute | solution.py:387

commit v6 on v5

--- a/solution.py
+++ b/solution.py
@@ -87,23 +87,33 @@
     )
 
 
-def first_kernel(place_ref, a_ref, w_ref, out_ref, token_ref):
-    total = jnp.dot(a_ref[...], w_ref[...], preferred_element_type=jnp.float32)
-    out_ref[...] = total.astype(out_ref.dtype)
+def first_kernel(tensor, at_ref, a_ref, w_ref, out_ref, token_ref):
+    sends = (at_ref[0] == 0) | (at_ref[0] == tensor - 1)
+
+    @pl.when(jnp.logical_not(sends))
+    def _():
+        out_ref[...] = jnp.zeros_like(out_ref)
+
+    @pl.when(sends)
+    def _():
+        total = jnp.dot(a_ref[...], w_ref[...], preferred_element_type=jnp.float32)
+        out_ref[...] = total.astype(out_ref.dtype)
+
     token_ref[...] = jnp.zeros_like(token_ref)
 
 
-def first_term(attn, weight, first_tile, tile, tiles):
+def first_term(attn, weight, z, tensor, tile, tiles):
     rows, depth = attn.shape
+    last_block = (tensor - 1) * (weight.shape[1] // tensor // (tiles * tile))
     step = rows // ROW_PARTS
     return pl.pallas_call(
-        first_kernel,
+        functools.partial(first_kernel, tensor),
         grid_spec=pltpu.PrefetchScalarGridSpec(
             num_scalar_prefetch=1,
             grid=(ROW_PARTS,),
             in_specs=[
-                pl.BlockSpec((step, depth), lambda n, b: (n, 0)),
-                pl.BlockSpec((depth, tiles * tile), lambda n, b: (0, b[0] // tiles)),
+                pl.BlockSpec((step, depth), lambda n, at: (jnp.where((at[0] == 0) | (at[0] == tensor - 1), n, 0), 0)),
+                pl.BlockSpec((depth, tiles * tile), lambda n, at: (0, jnp.where(2 * at[0] < tensor, last_block, 0))),
             ],
             out_specs=[
                 pl.BlockSpec((step, tiles * tile), lambda n, b: (n, 0)),
@@ -116,7 +126,7 @@
         ],
         compiler_params=params(FIRST_VMEM),
         cost_estimate=cost(2 * rows * depth * tiles * tile, depth * tiles * tile),
-    )(first_tile.reshape(1).astype(jnp.int32), attn, weight)
+    )(z.reshape(1).astype(jnp.int32), attn, weight)
 
 
 def exchange(size, hop):
@@ -353,7 +363,7 @@
             start, tiles = span
             first = jnp.clip(block, 0, tensor - 1) * (width // tile) + start
             if after is None:
-                return first_term(attn_out, out_weight, first, tile, tiles)
+                return first_term(attn_out, out_weight, z, tensor, tile, tiles)
             came = []
             for sums, flag in ((came_a, flag_a), (came_b, flag_b)):
                 for (low, count), ref in sums:

time: 213 us -> 213 us (level)
  no operation moved by 1% of the time
where the time goes in v6:
time: 213 us; the launch traced here: 211 us
  waiting for transfers between devices  82.4 us (39%)
  Pallas kernels  80.9 us (38%)
  starting transfers between devices  32.4 us (15%)
  local copies, waits for them, and re-layouts  8.27 us (4%)
  other arithmetic  6.8 us (3%)
    pallas_call x10, Pallas kernels, term(): pl.pallas_call(functools.partial(term_kernel, ranges), grid_spec=pltpu.Pr...  52.9 us
    ppermute x8, waiting for transfers between devices, step_of(): xs.append((span, lax.ppermute(for_x, 'tensor', pairs)))  35.2 us
    ppermute x3, waiting for transfers between devices, send_mine(): state['theirs'] = lax.ppermute(state['mine'], 'tensor', pairs)  26.4 us
    ppermute x8, starting transfers between devices, step_of(): xs.append((span, lax.ppermute(for_x, 'tensor', pairs)))  21 us
    ppermute x3, waiting for transfers between devices, fetch(): sources.insert(2, lax.ppermute(piece, 'replica', pairs))  20.8 us
    pallas_call x1, Pallas kernels, own_term(): pl.pallas_call(own_kernel, grid_spec=pltpu.PrefetchScalarGridSpec(num_sca...  12.7 us
    ppermute x3, starting transfers between devices, send_mine(): state['theirs'] = lax.ppermute(state['mine'], 'tensor', pairs)  5.59 us
    unnamed x22, local copies, waits for them, and re-layouts  5.18 us
  transfers between devices with their start and end apart: 19, of which 9 were waited for; matrix products, arithmetic and copies ran while one was open for 5% of the time, Pallas kernels for 36%

profile of v6, /device:TPU:0, one launch (start us, length us, event | category | flops | bytes accessed | tf_op | source)
XLA Modules:
  0.0 211.1 jit_solution(14150848984316279586)
XLA Ops:
  0.0 3.7 %shard_map.91 = (bf16[768,256]{1,0:T(8,128)(2,1)}, f32[8,128]{1,0:T(8,128)}) custom-call(s32[1]{0:T(128)} %bitcast.at_ref.block_ref, bf16[768,2048]{1,0:T(8,128)(2,1)} %a_ref.25, bf16[2048,8192]{1,0:T(8,128)(2,1)} %w_ref.23), custom_call_target="tpu_custom_call" | custom-call | flops 2415919104 | bytes 3145728 | tf_op jit(solution)/shard_map/pallas_call | solution.py:109
  3.7 2.0 collective-permute-start.3
  5.7 0.7 copy-done.6
  6.4 5.3 %shard_map.92.rest_0_ = bf16[768,768]{1,0:T(8,128)(2,1)} custom-call(s32[1]{0:T(128)} %bitcast.8.place_ref, bf16[768,2048]{1,0:T(8,128)(2,1)S(1)} %copy-done, bf16[2048,8192]{1,0:T(8,128)(2,1)} %w_ref.23, f32[8,128]{1,0:T(8,128)S(1)} %copy-done.6), custom_call_target="tpu_custom_call" | custom-call | flops 7247757312 | bytes 9437184 | tf_op jit(solution)/shard_map/pallas_call | solution.py:65
  11.8 6.4 %shard_map.93.refs_3_ = bf16[768,1024]{1,0:T(8,128)(2,1)} custom-call(s32[1]{0:T(128)} %bitcast.7.place_ref, bf16[768,2048]{1,0:T(8,128)(2,1)S(1)} %copy-done, bf16[2048,8192]{1,0:T(8,128)(2,1)} %w_ref.23, bf16[768,768]{1,0:T(8,128)(2,1)} %shard_map.92.rest_0_), custom_call_target="tpu_custom_call" | custom-call | flops 9663676416 | bytes 12582912 | tf_op jit(solution)/shard_map/pallas_call | solution.py:65
  18.2 2.0 collective-permute-start.6
  20.2 0.2 select_reduce_fusion
  20.4 0.5 broadcast_compare_fusion
  20.9 0.8 convert_reduce_fusion
  21.8 0.7 select_reduce_fusion.1
  22.5 0.2 fusion.3
  22.7 0.1 pad_add_fusion.row_ref
  22.8 2.2 %copy-done.1 = bf16[8,2,64,2048]{3,2,1,0:T(8,128)(2,1)S(1)} copy-done((bf16[8,2,64,2048]{3,2,1,0:T(8,128)(2,1)S(1)}, bf16[8,2,64,2048]{3,2,1,0:T(8,128)(2,1)}, u32[]{:S(2)}) %copy-start.1) | copy-done | bytes 4194328
  25.0 2.0 shard_map.94
  27.0 1.0 copy-done.3
  28.0 1.5 collective-permute-start.1
  29.5 1.2 fusion.6
  30.7 0.5 add_bitcast_fusion
  31.2 0.6 fusion.8
  31.8 0.9 broadcast_in_dim.86.wanted_ref
  32.7 0.7 select_reduce_fusion.2
  33.5 0.7 fusion.1
  34.2 0.7 compare_select_fusion
  34.9 0.6 compare_select_fusion.1
  35.5 0.8 concatenate.6.index_ref
  36.2 0.1 pad_add_fusion.1.place_ref
  36.4 0.1 pad_add_fusion.3.place_ref
  36.7 0.7 collective-permute-start
  37.3 3.9 %collective-permute-done.4.rest_1_ = bf16[768,768]{1,0:T(8,128)(2,1)} collective-permute-done((bf16[768,768]{1,0:T(8,128)(2,1)}, bf16[768,768]{1,0:T(8,128)(2,1)}, u32[]{:S(2)}, u32[]{:S(2)}) %collective-permute-start.4) | collective-permute-done | bytes 1179680 | tf_op jit(solution)/shard_map/ppermute | solution.py:395
  41.2 1.2 copy-done.4
  42.5 6.7 %shard_map.95.rest_5_ = bf16[768,1024]{1,0:T(8,128)(2,1)S(1)} custom-call(s32[3]{0:T(128)S(1)} %pad_add_fusion.1.place_ref, bf16[768,2048]{1,0:T(8,128)(2,1)S(1)} %copy-done, bf16[2048,8192]{1,0:T(8,128)(2,1)} %w_ref.23, bf16[768,256]{1,0:T(8,128)(2,1)S(1)} %collective-permute-done.3.rest_0_, bf16[768,768]{1,0:T(8,128)(2,1)} %collective-permute-done.4.rest_1_, ...), custom_call_target="tpu_custom_call" | custom-call | flops 9663676416 | bytes 12582912 | tf_op jit(solution)/shard_map/pallas_call | solution.py:65
  49.1 0.8 collective-permute-start.9
  49.9 0.1 pad_add_fusion.6.place_ref
  50.1 4.4 %collective-permute-done.1.rest_3_ = bf16[2,2,64,2048]{3,2,1,0:T(8,128)(2,1)} collective-permute-done((bf16[2,2,64,2048]{3,2,1,0:T(8,128)(2,1)}, bf16[2,2,64,2048]{3,2,1,0:T(8,128)(2,1)}, u32[]{:S(2)}, u32[]{:S(2)}) %collective-permute-start.1) | collective-permute-done | bytes 1048608 | tf_op jit(solution)/shard_map/ppermute | solution.py:450
  54.5 3.0 %collective-permute-start.8 = (bf16[768,1024]{1,0:T(8,128)(2,1)S(1)}, bf16[768,1024]{1,0:T(8,128)(2,1)S(1)}, u32[]{:S(2)}, u32[]{:S(2)}) collective-permute-start(bf16[768,1024]{1,0:T(8,128)(2,1)S(1)} %shard_map.95.rest_5_), channel_id=1, source_target_pairs={{0,1},{3,2},{4,5},{7,6},{8,9},{11,10},{12,13},{15,14},{16,17},{19,... | collective-permute-start | bytes 4718600 | tf_op jit(solution)/shard_map/ppermute | solution.py:395
  57.5 16.4 %collective-permute-done.2.rest_4_ = bf16[2,2,64,2048]{3,2,1,0:T(8,128)(2,1)} collective-permute-done((bf16[2,2,64,2048]{3,2,1,0:T(8,128)(2,1)}, bf16[2,2,64,2048]{3,2,1,0:T(8,128)(2,1)}, u32[]{:S(2)}, u32[]{:S(2)}) %collective-permute-start.2) | collective-permute-done | bytes 1048608 | tf_op jit(solution)/shard_map/ppermute | solution.py:450
  73.9 4.8 %shard_map.96 = (bf16[384,128]{1,0:T(8,128)(2,1)S(1)}, bf16[8,64,2048]{2,1,0:T(8,128)(2,1)S(1)}) custom-call(s32[8]{0:T(128)S(1)} %get-tuple-element.29.kind_ref, s32[40]{0:T(128)S(1)} %concatenate.6.index_ref, s32[8]{0:T(128)S(1)} %get-tuple-element.36.id_ref, bf16[768,2048]{1,0:T(8,128)(2,1)S(1)} %copy-done, s32[768,1]{1,0:T(8,128)S(1)} %copy-done.5, ...), custom_call_target="tpu_custom_call" | custom-call | flops 4831838208 | bytes 18874368 | tf_op jit(solution)/shard_map/pallas_call | solution.py:217
  78.7 3.4 %collective-permute-start.5 = (bf16[384,128]{1,0:T(8,128)(2,1)S(1)}, bf16[384,128]{1,0:T(8,128)(2,1)S(1)}, u32[]{:S(2)}, u32[]{:S(2)}) collective-permute-start(bf16[384,128]{1,0:T(8,128)(2,1)S(1)} %get-tuple-element.17.rest_1_.mine_ref), channel_id=1, source_target_pairs={{0,1},{3,2},{4,5},{7,6},{8,9},{11,10},{12,13},{15,14},{16,17},{19,... | collective-permute-start | bytes 294920 | tf_op jit(solution)/shard_map/ppermute | solution.py:457
  82.2 6.4 %shard_map.97.after_ref = bf16[768,1024]{1,0:T(8,128)(2,1)S(1)} custom-call(s32[2]{0:T(128)S(1)} %pad_add_fusion.2.place_ref, bf16[768,2048]{1,0:T(8,128)(2,1)S(1)} %copy-done, bf16[2048,8192]{1,0:T(8,128)(2,1)} %w_ref.23, bf16[768,1024]{1,0:T(8,128)(2,1)} %collective-permute-done.6.rest_0_, bf16[384,128]{1,0:T(8,128)(2,1)S(1)} %get-tuple-element.17.rest_1_.mine_ref), custom_call_target="tpu_custom_call" | custom-call | flops 9663676416 | bytes 12582912 | tf_op jit(solution)/shard_map/pallas_call | solution.py:65
  88.6 0.8 collective-permute-start.12
  89.4 5.2 %collective-permute-start.11 = (bf16[768,1024]{1,0:T(8,128)(2,1)S(1)}, bf16[768,1024]{1,0:T(8,128)(2,1)S(1)}, u32[]{:S(2)}, u32[]{:S(2)}) collective-permute-start(bf16[768,1024]{1,0:T(8,128)(2,1)S(1)} %shard_map.97.after_ref), channel_id=1, source_target_pairs={{0,1},{3,2},{4,5},{7,6},{8,9},{11,10},{12,13},{15,14},{16,17},{19,... | collective-permute-start | bytes 4718600 | tf_op jit(solution)/shard_map/ppermute | solution.py:395
  94.6 15.6 %collective-permute-done.5.theirs_ref = bf16[384,128]{1,0:T(8,128)(2,1)S(1)} collective-permute-done((bf16[384,128]{1,0:T(8,128)(2,1)S(1)}, bf16[384,128]{1,0:T(8,128)(2,1)S(1)}, u32[]{:S(2)}, u32[]{:S(2)}) %collective-permute-start.5) | collective-permute-done | bytes 98336 | tf_op jit(solution)/shard_map/ppermute | solution.py:457
  110.2 0.7 collective-permute-start.7
  110.9 6.2 %shard_map.99.rest_1_ = bf16[768,1024]{1,0:T(8,128)(2,1)S(1)} custom-call(s32[2]{0:T(128)S(1)} %pad_add_fusion.4.place_ref, bf16[768,2048]{1,0:T(8,128)(2,1)S(1)} %copy-done, bf16[2048,8192]{1,0:T(8,128)(2,1)} %w_ref.23, bf16[768,1024]{1,0:T(8,128)(2,1)S(1)} %collective-permute-done.9.rest_0_, bf16[384,128]{1,0:T(8,128)(2,1)S(1)} %shard_map.98.rest_1_.mine_ref), custom_call_target="tpu_custom_call" | custom-call | flops 9663676416 | bytes 12582912 | tf_op jit(solution)/shard_map/pallas_call | solution.py:65
  117.2 6.0 %collective-permute-start.17 = (bf16[768,1024]{1,0:T(8,128)(2,1)S(1)}, bf16[768,1024]{1,0:T(8,128)(2,1)S(1)}, u32[]{:S(2)}, u32[]{:S(2)}) collective-permute-start(bf16[768,1024]{1,0:T(8,128)(2,1)S(1)} %shard_map.99.rest_1_), channel_id=1, source_target_pairs={{0,1},{1,0},{2,3},{3,2},{4,5},{5,4},{6,7},{7,6},{8,9},{9,8},{10,11... | collective-permute-start | bytes 4718600 | tf_op jit(solution)/shard_map/ppermute | solution.py:395
  123.1 6.2 %shard_map.100.after_ref = bf16[768,1024]{1,0:T(8,128)(2,1)S(1)} custom-call(s32[2]{0:T(128)S(1)} %pad_add_fusion.3.place_ref, bf16[768,2048]{1,0:T(8,128)(2,1)S(1)} %copy-done, bf16[2048,8192]{1,0:T(8,128)(2,1)} %w_ref.23, bf16[768,1024]{1,0:T(8,128)(2,1)S(1)} %collective-permute-done.8.rest_0_, bf16[768,1024]{1,0:T(8,128)(2,1)S(1)} %shard_map.99.rest_1_), custom_call_target="tpu_custom_call" | custom-call | flops 9663676416 | bytes 12582912 | tf_op jit(solution)/shard_map/pallas_call | solution.py:65
  129.3 0.8 collective-permute-start.18
  130.2 1.5 collective-permute-start.10
  131.7 5.1 %shard_map.102.rest_1_ = bf16[768,768]{1,0:T(8,128)(2,1)S(1)} custom-call(s32[2]{0:T(128)S(1)} %pad_add_fusion.6.place_ref, bf16[768,2048]{1,0:T(8,128)(2,1)S(1)} %copy-done, bf16[2048,8192]{1,0:T(8,128)(2,1)} %w_ref.23, bf16[768,1024]{1,0:T(8,128)(2,1)S(1)} %collective-permute-done.12.rest_0_, bf16[384,128]{1,0:T(8,128)(2,1)S(1)} %shard_map.101.rest_1_.mine_ref), custom_call_target="tpu_custom_call" | custom-call | flops 7247757312 | bytes 9437184 | tf_op jit(solution)/shard_map/pallas_call | solution.py:65
  136.7 2.7 %collective-permute-start.15 = (bf16[768,768]{1,0:T(8,128)(2,1)S(1)}, bf16[768,768]{1,0:T(8,128)(2,1)S(1)}, u32[]{:S(2)}, u32[]{:S(2)}) collective-permute-start(bf16[768,768]{1,0:T(8,128)(2,1)S(1)} %shard_map.102.rest_1_), channel_id=1, source_target_pairs={{0,1},{1,0},{2,3},{3,2},{4,5},{5,4},{6,7},{7,6},{8,9},{9,8},{10,11... | collective-permute-start | bytes 3538952 | tf_op jit(solution)/shard_map/ppermute | solution.py:395
  139.4 4.5 %collective-permute-done.11.rest_0_ = bf16[768,1024]{1,0:T(8,128)(2,1)S(1)} collective-permute-done((bf16[768,1024]{1,0:T(8,128)(2,1)S(1)}, bf16[768,1024]{1,0:T(8,128)(2,1)S(1)}, u32[]{:S(2)}, u32[]{:S(2)}) %collective-permute-start.11) | collective-permute-done | bytes 1572896 | tf_op jit(solution)/shard_map/ppermute | solution.py:395
  143.9 5.1 %shard_map.103.after_ref = bf16[768,768]{1,0:T(8,128)(2,1)S(1)} custom-call(s32[2]{0:T(128)S(1)} %pad_add_fusion.5.place_ref, bf16[768,2048]{1,0:T(8,128)(2,1)S(1)} %copy-done, bf16[2048,8192]{1,0:T(8,128)(2,1)} %w_ref.23, bf16[768,1024]{1,0:T(8,128)(2,1)S(1)} %collective-permute-done.11.rest_0_, bf16[768,768]{1,0:T(8,128)(2,1)S(1)} %shard_map.102.rest_1_), custom_call_target="tpu_custom_call" | custom-call | flops 7247757312 | bytes 9437184 | tf_op jit(solution)/shard_map/pallas_call | solution.py:65
  149.0 0.7 collective-permute-start.16
  149.7 10.8 %collective-permute-done.10.theirs_ref = bf16[384,128]{1,0:T(8,128)(2,1)S(1)} collective-permute-done((bf16[384,128]{1,0:T(8,128)(2,1)S(1)}, bf16[384,128]{1,0:T(8,128)(2,1)S(1)}, u32[]{:S(2)}, u32[]{:S(2)}) %collective-permute-start.10) | collective-permute-done | bytes 98336 | tf_op jit(solution)/shard_map/ppermute | solution.py:457
  160.6 2.8 %shard_map.105.rest_1_ = bf16[768,256]{1,0:T(8,128)(2,1)S(1)} custom-call(s32[2]{0:T(128)S(1)} %pad_add_fusion.8.place_ref, bf16[768,2048]{1,0:T(8,128)(2,1)S(1)} %copy-done, bf16[2048,8192]{1,0:T(8,128)(2,1)} %w_ref.23, bf16[768,1024]{1,0:T(8,128)(2,1)S(1)} %collective-permute-done.12.rest_0_, bf16[384,128]{1,0:T(8,128)(2,1)S(1)} %shard_map.104.rest_1_.chosen_ref), custom_call_target="tpu_custom_call" | custom-call | flops 2415919104 | bytes 3145728 | tf_op jit(solution)/shard_map/pallas_call | solution.py:65
  163.4 2.8 %shard_map.106.after_ref = bf16[768,256]{1,0:T(8,128)(2,1)S(1)} custom-call(s32[2]{0:T(128)S(1)} %pad_add_fusion.7.place_ref, bf16[768,2048]{1,0:T(8,128)(2,1)S(1)} %copy-done, bf16[2048,8192]{1,0:T(8,128)(2,1)} %w_ref.23, bf16[768,1024]{1,0:T(8,128)(2,1)S(1)} %collective-permute-done.11.rest_0_, bf16[768,256]{1,0:T(8,128)(2,1)S(1)} %shard_map.105.rest_1_), custom_call_target="tpu_custom_call" | custom-call | flops 2415919104 | bytes 3145728 | tf_op jit(solution)/shard_map/pallas_call | solution.py:65
  166.2 11.4 %collective-permute-done.17.rest_0_ = bf16[768,1024]{1,0:T(8,128)(2,1)S(1)} collective-permute-done((bf16[768,1024]{1,0:T(8,128)(2,1)S(1)}, bf16[768,1024]{1,0:T(8,128)(2,1)S(1)}, u32[]{:S(2)}, u32[]{:S(2)}) %collective-permute-start.17) | collective-permute-done | bytes 1572896 | tf_op jit(solution)/shard_map/ppermute | solution.py:395
  177.6 0.7 collective-permute-start.14
  178.3 12.7 %shard_map.107.own_ref = f32[768,2048]{1,0:T(8,128)S(1)} custom-call(s32[1]{0:T(128)} %bitcast.at_ref.block_ref, s32[8]{0:T(128)S(1)} %get-tuple-element.36.id_ref, bf16[768,2048]{1,0:T(8,128)(2,1)S(1)} %copy-done, bf16[2048,8192]{1,0:T(8,128)(2,1)} %w_ref.23, bf16[384,128]{1,0:T(8,128)(2,1)S(1)} %shard_map.104.rest_1_.chosen_ref, s32[768,1]{1,0:T(8,128)S(1)} %copy-done.5, ...), custom_call_target="tpu_custom_call" | custom-call | flops 24159191040 | bytes 50331648 | tf_op jit(solution)/shard_map/pallas_call | solution.py:282
  191.0 1.8 shard_map.108.rest_2_
  192.9 10.0 %collective-permute-done.15.rest_0_ = bf16[768,768]{1,0:T(8,128)(2,1)S(1)} collective-permute-done((bf16[768,768]{1,0:T(8,128)(2,1)S(1)}, bf16[768,768]{1,0:T(8,128)(2,1)S(1)}, u32[]{:S(2)}, u32[]{:S(2)}) %collective-permute-start.15) | collective-permute-done | bytes 1179680 | tf_op jit(solution)/shard_map/ppermute | solution.py:395
  202.9 2.0 shard_map.109.rest_2_
  204.9 5.3 %collective-permute-done.13.rest_0_ = bf16[768,256]{1,0:T(8,128)(2,1)S(1)} collective-permute-done((bf16[768,256]{1,0:T(8,128)(2,1)S(1)}, bf16[768,256]{1,0:T(8,128)(2,1)S(1)}, u32[]{:S(2)}, u32[]{:S(2)}) %collective-permute-start.13) | collective-permute-done | bytes 393248 | tf_op jit(solution)/shard_map/ppermute | solution.py:395
  210.2 0.9 shard_map.110
  (40 shorter events, 0.7 us)
Async XLA Ops:
  0.0 5.7 %copy-start = (bf16[768,2048]{1,0:T(8,128)(2,1)S(1)}, bf16[768,2048]{1,0:T(8,128)(2,1)}, u32[]{:S(2)}) copy-start(bf16[768,2048]{1,0:T(8,128)(2,1)} %a_ref.25) | copy-start | bytes 9437188
  3.7 33.0 %collective-permute-start.3 = (bf16[768,256]{1,0:T(8,128)(2,1)}, bf16[768,256]{1,0:T(8,128)(2,1)S(1)}, u32[]{:S(2)}, u32[]{:S(2)}) collective-permute-start(bf16[768,256]{1,0:T(8,128)(2,1)} %get-tuple-element.16), channel_id=1, source_target_pairs={{0,1},{3,2},{1,0},{2,3},{4,5},{7,6},{5,4},{6,7},{8,9},{11,10},{9,8... | collective-permute-start | bytes 1179656 | tf_op jit(solution)/shard_map/ppermute | solution.py:395
  5.7 0.7 copy-start.6
  11.7 29.5 %collective-permute-start.4 = (bf16[768,768]{1,0:T(8,128)(2,1)}, bf16[768,768]{1,0:T(8,128)(2,1)}, u32[]{:S(2)}, u32[]{:S(2)}) collective-permute-start(bf16[768,768]{1,0:T(8,128)(2,1)} %shard_map.92.rest_0_), channel_id=1, source_target_pairs={{0,1},{3,2},{1,0},{2,3},{4,5},{7,6},{5,4},{6,7},{8,9},{11,10},{9,8... | collective-permute-start | bytes 3538952 | tf_op jit(solution)/shard_map/ppermute | solution.py:395
  11.8 8.4 %copy-start.9 = (s32[4,4]{1,0:T(4,128)S(1)}, s32[4,4]{1,0:T(4,128)}, u32[]{:S(2)}) copy-start(s32[4,4]{1,0:T(4,128)} %param.15) | copy-start | bytes 196
  11.8 8.4 %copy-start.10 = (s32[32]{0:T(128)S(1)}, s32[32]{0:T(128)}, u32[]{:S(2)}) copy-start(s32[32]{0:T(128)} %param.16) | copy-start | bytes 388
  18.2 64.0 %collective-permute-start.6 = (bf16[768,1024]{1,0:T(8,128)(2,1)}, bf16[768,1024]{1,0:T(8,128)(2,1)}, u32[]{:S(2)}, u32[]{:S(2)}) collective-permute-start(bf16[768,1024]{1,0:T(8,128)(2,1)} %shard_map.93.refs_3_), channel_id=1, source_target_pairs={{0,1},{3,2},{1,0},{2,3},{4,5},{7,6},{5,4},{6,7},{8,9},{11,10},{9,8... | collective-permute-start | bytes 4718600 | tf_op jit(solution)/shard_map/ppermute | solution.py:395
  22.8 2.2 %copy-start.1 = (bf16[8,2,64,2048]{3,2,1,0:T(8,128)(2,1)S(1)}, bf16[8,2,64,2048]{3,2,1,0:T(8,128)(2,1)}, u32[]{:S(2)}) copy-start(bf16[8,2,64,2048]{3,2,1,0:T(8,128)(2,1)} %rest_1_.1) | copy-start | bytes 12582916
  25.0 6.8 %copy-start.8 = (s32[768]{0:T(1024)S(1)}, s32[768]{0:T(1024)}, u32[]{:S(2)}) copy-start(s32[768]{0:T(1024)} %param.17) | copy-start | bytes 9220
  27.0 1.0 copy-start.3
  28.0 26.4 %collective-permute-start.1 = (bf16[2,2,64,2048]{3,2,1,0:T(8,128)(2,1)}, bf16[2,2,64,2048]{3,2,1,0:T(8,128)(2,1)}, u32[]{:S(2)}, u32[]{:S(2)}) collective-permute-start(bf16[2,2,64,2048]{3,2,1,0:T(8,128)(2,1)} %get-tuple-element.14), channel_id=1, source_target_pairs={{0,8},{4,12},{8,0},{12,4},{1,9},{5,13},{9,1},{13,5},{2,10},{6,14},... | collective-permute-start | bytes 3145736 | tf_op jit(solution)/shard_map/ppermute | solution.py:450
  29.5 44.4 %collective-permute-start.2 = (bf16[2,2,64,2048]{3,2,1,0:T(8,128)(2,1)}, bf16[2,2,64,2048]{3,2,1,0:T(8,128)(2,1)}, u32[]{:S(2)}, u32[]{:S(2)}) collective-permute-start(bf16[2,2,64,2048]{3,2,1,0:T(8,128)(2,1)} %get-tuple-element.15), channel_id=1, source_target_pairs={{0,12},{4,8},{8,4},{12,0},{1,13},{5,9},{9,5},{13,1},{2,14},{6,10},... | collective-permute-start | bytes 3145736 | tf_op jit(solution)/shard_map/ppermute | solution.py:450
  36.7 37.2 %copy-start.2 = (bf16[8,2,64,2048]{3,2,1,0:T(8,128)(2,1)S(1)}, bf16[8,2,64,2048]{3,2,1,0:T(8,128)(2,1)}, u32[]{:S(2)}) copy-start(bf16[8,2,64,2048]{3,2,1,0:T(8,128)(2,1)} %rest_1_.1) | copy-start | bytes 12582916
  36.7 37.2 %collective-permute-start = (bf16[2,2,64,2048]{3,2,1,0:T(8,128)(2,1)}, bf16[2,2,64,2048]{3,2,1,0:T(8,128)(2,1)S(1)}, u32[]{:S(2)}, u32[]{:S(2)}) collective-permute-start(bf16[2,2,64,2048]{3,2,1,0:T(8,128)(2,1)} %copy-done.3), channel_id=1, source_target_pairs={{0,4},{4,0},{8,12},{12,8},{1,5},{5,1},{9,13},{13,9},{2,6},{6,2},{1... | collective-permute-start | bytes 3145736 | tf_op jit(solution)/shard_map/ppermute | solution.py:450
  41.2 1.2 copy-start.4
  42.5 31.4 %copy-start.5 = (s32[768,1]{1,0:T(8,128)S(1)}, s32[768,1]{1,0:T(8,128)}, u32[]{:S(2)}) copy-start(s32[768,1]{1,0:T(8,128)} %broadcast_in_dim.86.wanted_ref) | copy-start | bytes 9220
  42.5 31.4 %copy-start.7 = (bf16[8,2,64,2048]{3,2,1,0:T(8,128)(2,1)S(1)}, bf16[8,2,64,2048]{3,2,1,0:T(8,128)(2,1)}, u32[]{:S(2)}) copy-start(bf16[8,2,64,2048]{3,2,1,0:T(8,128)(2,1)} %rest_0_.1) | copy-start | bytes 12582916
  49.1 61.8 %collective-permute-start.9 = (bf16[768,1024]{1,0:T(8,128)(2,1)S(1)}, bf16[768,1024]{1,0:T(8,128)(2,1)S(1)}, u32[]{:S(2)}, u32[]{:S(2)}) collective-permute-start(bf16[768,1024]{1,0:T(8,128)(2,1)S(1)} %shard_map.95.rest_5_), channel_id=1, source_target_pairs={{1,2},{2,1},{5,6},{6,5},{9,10},{10,9},{13,14},{14,13},{17,18},{18,... | collective-permute-start | bytes 4718600 | tf_op jit(solution)/shard_map/ppermute | solution.py:397
  54.5 68.7 %collective-permute-start.8 = (bf16[768,1024]{1,0:T(8,128)(2,1)S(1)}, bf16[768,1024]{1,0:T(8,128)(2,1)S(1)}, u32[]{:S(2)}, u32[]{:S(2)}) collective-permute-start(bf16[768,1024]{1,0:T(8,128)(2,1)S(1)} %shard_map.95.rest_5_), channel_id=1, source_target_pairs={{0,1},{3,2},{4,5},{7,6},{8,9},{11,10},{12,13},{15,14},{16,17},{19,... | collective-permute-start | bytes 4718600 | tf_op jit(solution)/shard_map/ppermute | solution.py:395
  78.7 31.5 %collective-permute-start.5 = (bf16[384,128]{1,0:T(8,128)(2,1)S(1)}, bf16[384,128]{1,0:T(8,128)(2,1)S(1)}, u32[]{:S(2)}, u32[]{:S(2)}) collective-permute-start(bf16[384,128]{1,0:T(8,128)(2,1)S(1)} %get-tuple-element.17.rest_1_.mine_ref), channel_id=1, source_target_pairs={{0,1},{3,2},{4,5},{7,6},{8,9},{11,10},{12,13},{15,14},{16,17},{19,... | collective-permute-start | bytes 294920 | tf_op jit(solution)/shard_map/ppermute | solution.py:457
  88.6 43.0 %collective-permute-start.12 = (bf16[768,1024]{1,0:T(8,128)(2,1)S(1)}, bf16[768,1024]{1,0:T(8,128)(2,1)S(1)}, u32[]{:S(2)}, u32[]{:S(2)}) collective-permute-start(bf16[768,1024]{1,0:T(8,128)(2,1)S(1)} %shard_map.97.after_ref), channel_id=1, source_target_pairs={{1,2},{2,1},{5,6},{6,5},{9,10},{10,9},{13,14},{14,13},{17,18},{18,... | collective-permute-start | bytes 4718600 | tf_op jit(solution)/shard_map/ppermute | solution.py:397
  89.4 54.5 %collective-permute-start.11 = (bf16[768,1024]{1,0:T(8,128)(2,1)S(1)}, bf16[768,1024]{1,0:T(8,128)(2,1)S(1)}, u32[]{:S(2)}, u32[]{:S(2)}) collective-permute-start(bf16[768,1024]{1,0:T(8,128)(2,1)S(1)} %shard_map.97.after_ref), channel_id=1, source_target_pairs={{0,1},{3,2},{4,5},{7,6},{8,9},{11,10},{12,13},{15,14},{16,17},{19,... | collective-permute-start | bytes 4718600 | tf_op jit(solution)/shard_map/ppermute | solution.py:395
  110.2 19.9 %collective-permute-start.7 = (bf16[384,128]{1,0:T(8,128)(2,1)S(1)}, bf16[384,128]{1,0:T(8,128)(2,1)S(1)}, u32[]{:S(2)}, u32[]{:S(2)}) collective-permute-start(bf16[384,128]{1,0:T(8,128)(2,1)S(1)} %shard_map.98.rest_1_.mine_ref), channel_id=1, source_target_pairs={{1,2},{2,1},{5,6},{6,5},{9,10},{10,9},{13,14},{14,13},{17,18},{18,... | collective-permute-start | bytes 294920 | tf_op jit(solution)/shard_map/ppermute | solution.py:457
  117.2 60.5 %collective-permute-start.17 = (bf16[768,1024]{1,0:T(8,128)(2,1)S(1)}, bf16[768,1024]{1,0:T(8,128)(2,1)S(1)}, u32[]{:S(2)}, u32[]{:S(2)}) collective-permute-start(bf16[768,1024]{1,0:T(8,128)(2,1)S(1)} %shard_map.99.rest_1_), channel_id=1, source_target_pairs={{0,1},{1,0},{2,3},{3,2},{4,5},{5,4},{6,7},{7,6},{8,9},{9,8},{10,11... | collective-permute-start | bytes 4718600 | tf_op jit(solution)/shard_map/ppermute | solution.py:395
  129.3 61.7 %collective-permute-start.18 = (bf16[768,1024]{1,0:T(8,128)(2,1)S(1)}, bf16[768,1024]{1,0:T(8,128)(2,1)S(1)}, u32[]{:S(2)}, u32[]{:S(2)}) collective-permute-start(bf16[768,1024]{1,0:T(8,128)(2,1)S(1)} %shard_map.100.after_ref), channel_id=1, source_target_pairs={{1,2},{2,1},{5,6},{6,5},{9,10},{10,9},{13,14},{14,13},{17,18},{18,... | collective-permute-start | bytes 4718600 | tf_op jit(solution)/shard_map/ppermute | solution.py:397
  130.2 30.4 %collective-permute-start.10 = (bf16[384,128]{1,0:T(8,128)(2,1)S(1)}, bf16[384,128]{1,0:T(8,128)(2,1)S(1)}, u32[]{:S(2)}, u32[]{:S(2)}) collective-permute-start(bf16[384,128]{1,0:T(8,128)(2,1)S(1)} %shard_map.101.rest_1_.mine_ref), channel_id=1, source_target_pairs={{1,0},{2,3},{5,4},{6,7},{9,8},{10,11},{13,12},{14,15},{17,16},{18,... | collective-permute-start | bytes 294920 | tf_op jit(solution)/shard_map/ppermute | solution.py:457
  136.7 66.2 %collective-permute-start.15 = (bf16[768,768]{1,0:T(8,128)(2,1)S(1)}, bf16[768,768]{1,0:T(8,128)(2,1)S(1)}, u32[]{:S(2)}, u32[]{:S(2)}) collective-permute-start(bf16[768,768]{1,0:T(8,128)(2,1)S(1)} %shard_map.102.rest_1_), channel_id=1, source_target_pairs={{0,1},{1,0},{2,3},{3,2},{4,5},{5,4},{6,7},{7,6},{8,9},{9,8},{10,11... | collective-permute-start | bytes 3538952 | tf_op jit(solution)/shard_map/ppermute | solution.py:395
  149.0 43.9 %collective-permute-start.16 = (bf16[768,768]{1,0:T(8,128)(2,1)S(1)}, bf16[768,768]{1,0:T(8,128)(2,1)S(1)}, u32[]{:S(2)}, u32[]{:S(2)}) collective-permute-start(bf16[768,768]{1,0:T(8,128)(2,1)S(1)} %shard_map.103.after_ref), channel_id=1, source_target_pairs={{1,2},{2,1},{5,6},{6,5},{9,10},{10,9},{13,14},{14,13},{17,18},{18,... | collective-permute-start | bytes 3538952 | tf_op jit(solution)/shard_map/ppermute | solution.py:397
  163.3 46.8 %collective-permute-start.13 = (bf16[768,256]{1,0:T(8,128)(2,1)S(1)}, bf16[768,256]{1,0:T(8,128)(2,1)S(1)}, u32[]{:S(2)}, u32[]{:S(2)}) collective-permute-start(bf16[768,256]{1,0:T(8,128)(2,1)S(1)} %shard_map.105.rest_1_), channel_id=1, source_target_pairs={{0,1},{1,0},{2,3},{3,2},{4,5},{5,4},{6,7},{7,6},{8,9},{9,8},{10,11... | collective-permute-start | bytes 1179656 | tf_op jit(solution)/shard_map/ppermute | solution.py:395
  177.6 27.3 %collective-permute-start.14 = (bf16[768,256]{1,0:T(8,128)(2,1)S(1)}, bf16[768,256]{1,0:T(8,128)(2,1)S(1)}, u32[]{:S(2)}, u32[]{:S(2)}) collective-permute-start(bf16[768,256]{1,0:T(8,128)(2,1)S(1)} %shard_map.106.after_ref), channel_id=1, source_target_pairs={{1,2},{2,1},{5,6},{6,5},{9,10},{10,9},{13,14},{14,13},{17,18},{18,... | collective-permute-start | bytes 1179656 | tf_op jit(solution)/shard_map/ppermute | solution.py:397
